TPU v7x, 32 devices: a whole 2x2x4 slice. The times are simulated.
32 devices in a mesh: tok: 8 (over z, core), hid: 4 (over y, x).
Axes of the slice: x: 2, y: 2, z: 4, core: 2. Of those that a mesh axis runs over, the one named last changes fastest.
Arguments:
- tokens: bfloat16 [32768, 1024], P('tok', 'hid'), may hold values from -6 to 6
- middle_cond: bfloat16 [8192, 1024], P('tok', 'hid'), may hold values from -6 to 6
- coarse_cond: bfloat16 [2048, 1024], P('tok', 'hid'), may hold values from -6 to 6
- first_gain: float32 [1024], P('hid'), may hold values from 0.1 to 1.9
- first_shift: float32 [1024], P('hid'), may hold values from -3 to 3
- attend_weight: bfloat16 [1024, 3, 1024], P('tok', None, 'hid'), may hold values from -0.1875 to 0.1875
- query_bias: float32 [1024], P('hid'), may hold values from -3 to 3
- value_bias: float32 [1024], P('hid'), may hold values from -3 to 3
- output_weight: bfloat16 [1024, 1024], P('hid', 'tok'), may hold values from -0.75 to 0.75
- mixer_bias: float32 [1024], P('hid'), may hold values from -3 to 3
- second_gain: float32 [1024], P('hid'), may hold values from 0.1 to 1.9
- second_shift: float32 [1024], P('hid'), may hold values from -3 to 3
- up_weight: bfloat16 [1024, 4096], P('tok', 'hid'), may hold values from -1 to 1
- hidden_bias: float32 [4096], P('hid'), may hold values from -3 to 3
- down_weight: bfloat16 [4096, 1024], P('hid', 'tok'), may hold values from -0.09375 to 0.09375
- down_bias: float32 [1024], P('hid'), may hold values from -3 to 3
- cotangent: bfloat16 [32768, 1024], P('tok', 'hid'), may hold values from -6 to 6
Outputs:
- layer_out: bfloat16 [32768, 1024], P('tok', 'hid')
- grad_tokens: float32 [32768, 1024], P('tok', 'hid')
- grad_middle: float32 [8192, 1024], P('tok', 'hid')
- grad_coarse: float32 [2048, 1024], P('tok', 'hid')
- grad_first_gain: float32 [1024], P(('hid', 'tok'))
- grad_first_shift: float32 [1024], P(('hid', 'tok'))
- grad_attend: float32 [1024, 3, 1024], P('tok', None, 'hid')
- grad_query_bias: float32 [1024], P(('hid', 'tok'))
- grad_value_bias: float32 [1024], P(('hid', 'tok'))
- grad_output: float32 [1024, 1024], P('hid', 'tok')
- grad_mixer_bias: float32 [1024], P(('hid', 'tok'))
- grad_second_gain: float32 [1024], P(('hid', 'tok'))
- grad_second_shift: float32 [1024], P(('hid', 'tok'))
- grad_up: float32 [1024, 4096], P('tok', 'hid')
- grad_hidden_bias: float32 [4096], P(('hid', 'tok'))
- grad_down: float32 [4096, 1024], P('hid', 'tok')
- grad_down_bias: float32 [1024], P(('hid', 'tok'))
All inputs are finite; a program needn't handle non-finite values.
Results may differ from a plain program's by a relative error of at most 0.017.
Values may be sent and summed in bfloat16 or wider, within the bound.
A program may use at most 256 MiB of HBM per device.

v0:
```python
import jax
import jax.numpy as jnp
from jax import lax
from jax.sharding import PartitionSpec as P

D = 1024
HEAD = 64
BLOCK = 128


epsilon = 1e-05


def full_features(values):
    return lax.all_gather(values, "hid", axis=1, tiled=True)


def feature_share(partial_value):
    return lax.psum_scatter(partial_value, "hid", scatter_dimension=1, tiled=True)


def norm_forward(summed, gain_row, shift_row):
    row_total, row_square = lax.psum(
        (jnp.sum(summed, axis=1), jnp.sum(summed * summed, axis=1)), "hid"
    )
    average = row_total / D
    inverse = lax.rsqrt(row_square / D - average * average + epsilon)
    scaled = (summed - average[:, None]) * inverse[:, None]
    normed = (scaled * gain_row + shift_row).astype(jnp.bfloat16)
    return (full_features(normed), scaled, inverse)


def norm_backward(upstream, scaled, inverse, gain_row):
    weighted = upstream * gain_row
    row_total, row_dot = (
        lax.psum(jnp.sum(weighted, axis=1).astype(jnp.bfloat16), "hid").astype(jnp.float32),
        lax.psum(jnp.sum(weighted * scaled, axis=1).astype(jnp.bfloat16), "hid").astype(
            jnp.float32
        ),
    )
    grad_input = inverse[:, None] * (
        weighted - row_total[:, None] / D - scaled * (row_dot[:, None] / D)
    )
    return (grad_input, jnp.sum(upstream * scaled, axis=0), jnp.sum(upstream, axis=0))


def split_heads(values):
    positions, features = values.shape
    return values.reshape(positions // BLOCK, BLOCK, features // HEAD, HEAD)


def block_logits(queries, key_rows):
    scores = jnp.einsum("bqhd,bkhd->bhqk", queries, key_rows, preferred_element_type=jnp.float32)
    logits = scores * HEAD ** (-0.5)
    places = jnp.arange(BLOCK)
    allowed = places[:, None] >= places[None, :]
    return jnp.where(allowed, logits, -1e30)


def project_heads(normed, attend_full, biases):
    return (
        jnp.einsum("td,dck->tck", normed, attend_full, preferred_element_type=jnp.float32) + biases
    ).astype(jnp.bfloat16)


def attend_forward(projected):
    queries = split_heads(projected[:, 0])
    key_rows = split_heads(projected[:, 1])
    value_rows = split_heads(projected[:, 2])
    logits = block_logits(queries, key_rows)
    totals = jax.nn.logsumexp(logits, axis=-1, keepdims=True)
    attention = jnp.exp(logits - totals).astype(jnp.bfloat16)
    attended = jnp.einsum(
        "bhqk,bkhd->bqhd", attention, value_rows, preferred_element_type=jnp.float32
    )
    return (attended.reshape(projected.shape[0], projected.shape[2]).astype(jnp.bfloat16), totals)


def attend_backward(projected, totals, grad_attended):
    positions, features = grad_attended.shape
    queries = split_heads(projected[:, 0])
    key_rows = split_heads(projected[:, 1])
    value_rows = split_heads(projected[:, 2])
    grad_heads = split_heads(grad_attended)
    logits = block_logits(queries, key_rows)
    attention_f = jnp.exp(logits - totals)
    attention_b = attention_f.astype(jnp.bfloat16)
    grad_attention = jnp.einsum(
        "bqhd,bkhd->bhqk", grad_heads, value_rows, preferred_element_type=jnp.float32
    )
    grad_values = jnp.einsum(
        "bhqk,bqhd->bkhd", attention_b, grad_heads, preferred_element_type=jnp.float32
    )
    centre = jnp.sum(attention_f * grad_attention, axis=-1, keepdims=True)
    grad_scores = (attention_f * (grad_attention - centre) * HEAD ** (-0.5)).astype(jnp.bfloat16)
    grad_queries = jnp.einsum(
        "bhqk,bkhd->bqhd", grad_scores, key_rows, preferred_element_type=jnp.float32
    )
    grad_keys = jnp.einsum(
        "bhqk,bqhd->bkhd", grad_scores, queries, preferred_element_type=jnp.float32
    )
    pieces = [
        member.reshape(positions, features) for member in (grad_queries, grad_keys, grad_values)
    ]
    return jnp.stack(pieces, axis=1).astype(jnp.bfloat16)


def shards(
    tokens,
    middle_cond,
    coarse_cond,
    first_gain,
    first_shift,
    attend_weight,
    query_bias,
    value_bias,
    output_weight,
    mixer_bias,
    second_gain,
    second_shift,
    up_weight,
    hidden_bias,
    down_weight,
    down_bias,
    cotangent,
):
    positions, features = tokens.shape
    summed = (
        tokens.astype(jnp.float32).reshape(positions // 16, 4, 4, features)
        + middle_cond.astype(jnp.float32).reshape(positions // 16, 4, 1, features)
        + coarse_cond.astype(jnp.float32)[:, None, None, :]
    ).reshape(positions, features)
    attend_full, up_full = (
        lax.all_gather(attend_weight, "tok", axis=0, tiled=True),
        lax.all_gather(up_weight, "tok", axis=0, tiled=True),
    )
    output_cols, down_full = (
        lax.all_gather(output_weight, "tok", axis=1, tiled=True),
        lax.all_gather(down_weight, "tok", axis=1, tiled=True),
    )
    normed, scaled, inverse = norm_forward(summed, first_gain, first_shift)
    no_bias = jnp.zeros_like(query_bias)
    biases = jnp.stack([query_bias, no_bias, value_bias])
    attended, totals = attend_forward(project_heads(normed, attend_full, biases))
    branch_out = lax.psum_scatter(
        jnp.dot(attended, output_cols, preferred_element_type=jnp.float32),
        "hid",
        scatter_dimension=1,
        tiled=True,
    )
    residual = summed + (branch_out + mixer_bias)
    normed_two, scaled_two, inverse_two = norm_forward(residual, second_gain, second_shift)
    before = jnp.dot(normed_two, up_full, preferred_element_type=jnp.float32) + hidden_bias
    activated, gelu_pull = jax.vjp(jax.nn.gelu, before)
    hidden = activated.astype(jnp.bfloat16)
    feed_out = feature_share(jnp.dot(hidden, down_full, preferred_element_type=jnp.float32))
    layer_out = (residual + (feed_out + down_bias)).astype(jnp.bfloat16)
    upstream = cotangent.astype(jnp.float32)
    grad_down_bias = jnp.sum(upstream, axis=0)
    upstream_full = full_features(cotangent)
    grad_down = jnp.einsum("tf,td->fd", hidden, upstream_full, preferred_element_type=jnp.float32)
    grad_hidden = jnp.einsum(
        "td,fd->tf", upstream_full, down_full, preferred_element_type=jnp.float32
    )
    grad_before = gelu_pull(grad_hidden)[0].astype(jnp.bfloat16)
    grad_hidden_bias = jnp.sum(grad_before.astype(jnp.float32), axis=0)
    grad_up = jnp.einsum("td,tf->df", normed_two, grad_before, preferred_element_type=jnp.float32)
    grad_normed_two = feature_share(
        jnp.einsum("tf,df->td", grad_before, up_full, preferred_element_type=jnp.float32)
    )
    grad_back_two, grad_second_gain, grad_second_shift = norm_backward(
        grad_normed_two, scaled_two, inverse_two, second_gain
    )
    grad_residual = upstream + grad_back_two
    grad_mixed = grad_residual.astype(jnp.bfloat16)
    grad_mixer_bias = jnp.sum(grad_mixed.astype(jnp.float32), axis=0)
    mixed_full = full_features(grad_mixed)
    grad_output = jnp.einsum("tk,td->kd", attended, mixed_full, preferred_element_type=jnp.float32)
    grad_attended = jnp.einsum(
        "td,kd->tk", mixed_full, output_cols, preferred_element_type=jnp.float32
    ).astype(jnp.bfloat16)
    grad_projected = attend_backward(
        project_heads(normed, attend_full, biases), totals, grad_attended
    )
    grad_query_bias = jnp.sum(grad_projected[:, 0].astype(jnp.float32), axis=0)
    grad_value_bias = jnp.sum(grad_projected[:, 2].astype(jnp.float32), axis=0)
    grad_attend = jnp.einsum(
        "td,tck->dck", normed, grad_projected, preferred_element_type=jnp.float32
    )
    grad_normed = feature_share(
        jnp.einsum("tck,dck->td", grad_projected, attend_full, preferred_element_type=jnp.float32)
    )
    grad_back, grad_first_gain, grad_first_shift = norm_backward(
        grad_normed, scaled, inverse, first_gain
    )
    grad_tokens = grad_residual + grad_back
    grad_middle = jnp.sum(grad_tokens.reshape(positions // 4, 4, features), axis=1)
    grad_coarse = jnp.sum(grad_tokens.reshape(positions // 16, 16, features), axis=1)
    small_grads = jnp.stack(
        [
            grad_first_gain,
            grad_first_shift,
            grad_second_gain,
            grad_second_shift,
            grad_query_bias,
            grad_value_bias,
            grad_mixer_bias,
            grad_down_bias,
        ]
    )
    grad_attend, grad_up, grad_hidden_bias = (
        lax.psum_scatter(
            grad_attend.astype(jnp.bfloat16), "tok", scatter_dimension=0, tiled=True
        ).astype(jnp.float32),
        lax.psum_scatter(
            grad_up.astype(jnp.bfloat16), "tok", scatter_dimension=0, tiled=True
        ).astype(jnp.float32),
        lax.psum_scatter(
            grad_hidden_bias.astype(jnp.bfloat16), "tok", scatter_dimension=0, tiled=True
        ).astype(jnp.float32),
    )
    grad_output, grad_down, small_grads = (
        lax.psum_scatter(
            grad_output.astype(jnp.bfloat16), "tok", scatter_dimension=1, tiled=True
        ).astype(jnp.float32),
        lax.psum_scatter(
            grad_down.astype(jnp.bfloat16), "tok", scatter_dimension=1, tiled=True
        ).astype(jnp.float32),
        lax.psum_scatter(
            small_grads.astype(jnp.bfloat16), "tok", scatter_dimension=1, tiled=True
        ).astype(jnp.float32),
    )
    return (
        layer_out,
        grad_tokens,
        grad_middle,
        grad_coarse,
        small_grads[0],
        small_grads[1],
        grad_attend,
        small_grads[4],
        small_grads[5],
        grad_output,
        small_grads[6],
        small_grads[2],
        small_grads[3],
        grad_up,
        grad_hidden_bias,
        grad_down,
        small_grads[7],
    )


def solution(mesh):
    return jax.shard_map(
        shards,
        mesh=mesh,
        in_specs=(
            P("tok", "hid"),
            P("tok", "hid"),
            P("tok", "hid"),
            P("hid"),
            P("hid"),
            P("tok", None, "hid"),
            P("hid"),
            P("hid"),
            P("hid", "tok"),
            P("hid"),
            P("hid"),
            P("hid"),
            P("tok", "hid"),
            P("hid"),
            P("hid", "tok"),
            P("hid"),
            P("tok", "hid"),
        ),
        out_specs=(
            P("tok", "hid"),
            P("tok", "hid"),
            P("tok", "hid"),
            P("tok", "hid"),
            P(("hid", "tok")),
            P(("hid", "tok")),
            P("tok", None, "hid"),
            P(("hid", "tok")),
            P(("hid", "tok")),
            P("hid", "tok"),
            P(("hid", "tok")),
            P(("hid", "tok")),
            P(("hid", "tok")),
            P("tok", "hid"),
            P(("hid", "tok")),
            P("hid", "tok"),
            P(("hid", "tok")),
        ),
        check_vma=False,
    )
```

profile of v0, /device:TPU:8, one launch (start us, length us, event | category | flops | bytes accessed | tf_op | source)
XLA Modules:
  0.0 1427.2 jit_solution(16967891488735285250)
XLA Ops:
  32.2 16.3 %all-reduce.2 = (f32[4096]{0:T(1024)S(1)}, f32[4096]{0:T(1024)S(1)}) all-reduce(f32[4096]{0:T(1024)S(1)} %get-tuple-element.28, f32[4096]{0:T(1024)S(1)} %get-tuple-element.27), channel_id=1, replica_groups=mesh['tok'=8,'hid'=4] {'hid'}, use_global_device_ids=true, to_apply=%region_3.0 | all-reduce | flops 8192 | bytes 65536 | tf_op jit(solution)/shard_map/psum | solution.py:23
  53.3 14.4 %all_gather.26 = bf16[256,1024]{1,0:T(8,128)(2,1)S(1)} all-gather(bf16[256,128]{1,0:T(8,128)(2,1)S(1)} %copy-done.18), channel_id=1, replica_groups=mesh['tok'=8,'hid'=4] {'tok'}, dimensions={1}, use_global_device_ids=true | all-gather | bytes 589824 | tf_op jit(solution)/shard_map/all_gather | solution.py:138
  67.6 72.3 %all-gather.8.cloned.1.call-done = bf16[4096,1024]{1,0:T(8,128)(2,1)} async-done(((bf16[4096,256]{1,0:T(8,128)(2,1)}), bf16[4096,1024]{1,0:T(8,128)(2,1)}) %all-gather.8.cloned.1.call-update) | async-done | bytes 8388624 | tf_op jit(solution)/shard_map/all_gather | solution.py:15
  210.1 153.3 %reduce-scatter.16.cloned.1.call-done = f32[4096,256]{1,0:T(8,128)} async-done(((f32[4096,1024]{1,0:T(8,128)}), f32[4096,256]{1,0:T(8,128)}) %reduce-scatter.16.cloned.1.call-update) | async-done | bytes 4194320 | tf_op jit(solution)/shard_map/reduce_scatter | solution.py:145
  369.4 15.6 %all-reduce.1 = (f32[4096]{0:T(1024)S(1)}, f32[4096]{0:T(1024)S(1)}) all-reduce(f32[4096]{0:T(1024)S(1)} %get-tuple-element.26, f32[4096]{0:T(1024)S(1)} %get-tuple-element.25), channel_id=1, replica_groups=mesh['tok'=8,'hid'=4] {'hid'}, use_global_device_ids=true, to_apply=%region_10.11 | all-reduce | flops 8192 | bytes 65536 | tf_op jit(solution)/shard_map/psum | solution.py:23
  394.0 89.3 %all-gather.12.cloned.1.call-done = bf16[4096,1024]{1,0:T(8,128)(2,1)} async-done(((bf16[4096,256]{1,0:T(8,128)(2,1)}), bf16[4096,1024]{1,0:T(8,128)(2,1)}) %all-gather.12.cloned.1.call-update) | async-done | bytes 8388624 | tf_op jit(solution)/shard_map/all_gather | solution.py:15
  483.3 16.1 %fusion.84 = f32[4096,1024]{1,0:T(8,128)} fusion(bf16[4096,1024]{1,0:T(8,128)(2,1)} %all-gather.12.cloned.1.call-done, bf16[1024,1024]{1,0:T(8,128)(2,1)} %all-gather.14.cloned.1.call-done), kind=kOutput, calls=%fused_computation.110 | convolution fusion | flops 8589934592 | bytes 27262976 | tf_op jit(solution)/shard_map/dot_general | solution.py:153
  499.4 18.1 %all-gather.16.cloned.1.call-done = bf16[1024,1024]{1,0:T(8,128)(2,1)} async-done(((bf16[1024,128]{1,0:T(8,128)(2,1)}), bf16[1024,1024]{1,0:T(8,128)(2,1)}) %all-gather.16.cloned.1.call-update) | async-done | bytes 2097168 | tf_op jit(solution)/shard_map/all_gather | solution.py:139
  517.4 18.5 %fusion.73 = f32[4096,1024]{1,0:T(8,128)} fusion(bf16[1024,1024]{1,0:T(8,128)(2,1)} %all-gather.16.cloned.1.call-done, f32[4096,1024]{1,0:T(8,128)} %fusion.84, f32[1024]{0:T(1024)S(1)} %copy-done.32), kind=kOutput, calls=%fused_computation.102 | convolution fusion | flops 8631877632 | bytes 35655680 | tf_op jit(solution)/shard_map/dot_general | solution.py:156
  536.0 68.0 %all-gather.18.cloned.1.call-done = bf16[4096,1024]{1,0:T(8,128)(2,1)} async-done(((bf16[4096,256]{1,0:T(8,128)(2,1)}), bf16[4096,1024]{1,0:T(8,128)(2,1)}) %all-gather.18.cloned.1.call-update) | async-done | bytes 8388624 | tf_op jit(solution)/shard_map/all_gather | solution.py:15
  604.0 24.0 %fusion.76 = (bf16[1024]{0:T(1024)(128)(2,1)S(1)}, bf16[4096,1024]{1,0:T(8,128)(2,1)S(1)}) fusion(f32[4096,1024]{1,0:T(8,128)} %fusion.84, f32[1024]{0:T(1024)S(1)} %copy-done.32, bf16[4096,1024]{1,0:T(8,128)(2,1)} %all-gather.18.cloned.1.call-done, bf16[1024,1024]{1,0:T(8,128)(2,1)} %all-gather.16.cloned.1.call-done), kind=kOutput, calls=%fused_computation.105 | convolution fusion | flops 8682208256 | bytes 35657728 | tf_op jit(solution)/shard_map/td,fd->tf/dot_general | solution.py:162
  643.1 117.8 %reduce-scatter.18.cloned.1.call-done = f32[4096,256]{1,0:T(8,128)} async-done(((f32[4096,1024]{1,0:T(8,128)}), f32[4096,256]{1,0:T(8,128)}) %reduce-scatter.18.cloned.1.call-update) | async-done | bytes 4194320 | tf_op jit(solution)/shard_map/reduce_scatter | solution.py:19
  760.9 156.9 %reduce-scatter.20.cloned.1.call-done = f32[4096,256]{1,0:T(8,128)} async-done(((f32[4096,1024]{1,0:T(8,128)}), f32[4096,256]{1,0:T(8,128)}) %reduce-scatter.20.cloned.1.call-update) | async-done | bytes 4194320 | tf_op jit(solution)/shard_map/reduce_scatter | solution.py:19
  924.6 15.1 %all-reduce.4 = (bf16[4096]{0:T(1024)(128)(2,1)S(1)}, bf16[4096]{0:T(1024)(128)(2,1)S(1)}) all-reduce(bf16[4096]{0:T(1024)(128)(2,1)S(1)} %get-tuple-element.18, bf16[4096]{0:T(1024)(128)(2,1)S(1)} %get-tuple-element.22), channel_id=1, replica_groups=mesh['tok'=8,'hid'=4] {'hid'}, use_global_device_ids=true, to_apply=%region_16.17 | all-reduce | flops 8192 | bytes 32768 | tf_op jit(solution)/shard_map/psum | solution.py:37
  948.4 15.6 %convolution_convert_fusion.1 = bf16[1024,1024]{1,0:T(8,128)(2,1)S(1)} fusion(bf16[4096,1024]{1,0:T(8,128)(2,1)} %all-gather.18.cloned.1.call-done, f32[4096,1024]{1,0:T(8,128)} %fusion.84, f32[1024]{0:T(1024)S(1)} %copy-done.32), kind=kOutput, calls=%fused_computation.62 | convolution fusion | flops 8632926208 | bytes 27267072 | tf_op jit(solution)/shard_map/tf,td->fd/dot_general | solution.py:161
  966.7 14.9 %convolution_convert_fusion.2 = bf16[1024,1024]{1,0:T(8,128)(2,1)} fusion(bf16[4096,1024]{1,0:T(8,128)(2,1)} %all-gather.12.cloned.1.call-done, bf16[4096,1024]{1,0:T(8,128)(2,1)} %copy-done.34), kind=kOutput, calls=%fused_computation.63 | convolution fusion | flops 8590983168 | bytes 18874368 | tf_op jit(solution)/shard_map/td,tf->df/dot_general | solution.py:167
  981.6 54.3 %all-gather.20.cloned.1.call-done = bf16[4096,1024]{1,0:T(8,128)(2,1)} async-done(((bf16[4096,256]{1,0:T(8,128)(2,1)}), bf16[4096,1024]{1,0:T(8,128)(2,1)}) %all-gather.20.cloned.1.call-update) | async-done | bytes 8388624 | tf_op jit(solution)/shard_map/all_gather | solution.py:15
  1066.1 16.7 %convert_bitcast_fusion.1 = bf16[32,128,4,64]{1,3,2,0:T(8,128)(2,1)} fusion(bf16[32,128,4,64]{1,3,2,0:T(8,128)(2,1)S(1)} %copy-done.6, f32[32,4,128,128]{2,3,1,0:T(8,128)} %fusion.86, f32[32,4,128,128]{2,3,1,0:T(8,128)} %copy-done, f32[32,4,128]{2,1,0:T(4,128)S(1)} %copy-done.20, pred[128,128]{0,1:T(8,128)(4,1)S(1)} %copy-done.16), kind=kOutput, calls=%fused_computation.59 | convolution fusion | flops 292569216 | bytes 21053440 | tf_op jit(solution)/shard_map/bhqk,bqhd->bkhd/dot_general | solution.py:99
  1095.8 15.8 %fusion.80 = (bf16[4,64]{1,0:T(4,128)(2,1)S(1)}, bf16[32,128,4,64]{1,3,2,0:T(8,128)(2,1)}) fusion(bf16[32,128,4,64]{1,3,2,0:T(8,128)(2,1)} %copy-done.5, f32[32,4,128,128]{2,3,1,0:T(8,128)} %fusion.86, f32[32,4,128,128]{2,3,1,0:T(8,128)} %copy-done, f32[32,4,128]{2,1,0:T(4,128)S(1)} %copy-done.20, pred[128,128]{0,1:T(8,128)(4,1)S(1)} %copy-done.16), kind=kOutput, calls=%fused_computation.108 | convolution fusion | flops 293617536 | bytes 21053952 | tf_op jit(solution)/shard_map/bhqk,bkhd->bqhd/dot_general | solution.py:96
  1154.9 12.1 fusion.51
  1167.0 13.1 convolution_bitcast_fusion
  1182.0 13.2 all-reduce
  1214.4 157.5 %reduce-scatter.22.cloned.1.call-done = f32[4096,256]{1,0:T(8,128)} async-done(((f32[4096,1024]{1,0:T(8,128)}), f32[4096,256]{1,0:T(8,128)}) %reduce-scatter.22.cloned.1.call-update) | async-done | bytes 4194320 | tf_op jit(solution)/shard_map/reduce_scatter | solution.py:19
  1376.7 15.1 %all-reduce.3 = (bf16[4096]{0:T(1024)(128)(2,1)S(1)}, bf16[4096]{0:T(1024)(128)(2,1)S(1)}) all-reduce(bf16[4096]{0:T(1024)(128)(2,1)S(1)} %get-tuple-element.20, bf16[4096]{0:T(1024)(128)(2,1)S(1)} %get-tuple-element.21), channel_id=1, replica_groups=mesh['tok'=8,'hid'=4] {'hid'}, use_global_device_ids=true, to_apply=%region_22.23 | all-reduce | flops 8192 | bytes 32768 | tf_op jit(solution)/shard_map/psum | solution.py:37
  (186 shorter events, 288.2 us)
Async XLA Ops:
  7.2 60.4 %all-gather.10.cloned.1.call-start = ((), (), s32[]{:S(2)}) async-start(), calls=%async_computation.10 | async-start | bytes 1769472 | tf_op jit(solution)/shard_map/all_gather | solution.py:134
  7.9 132.0 %all-gather.8.cloned.1.call-start = ((), (), s32[]{:S(2)}) async-start(), calls=%async_computation.9 | async-start | bytes 10485760 | tf_op jit(solution)/shard_map/all_gather | solution.py:15
  53.0 310.4 %reduce-scatter.16.cloned.1.call-start = ((), (), s32[]{:S(2)}) async-start(), calls=%async_computation.11 | async-start | bytes 20971520 | tf_op jit(solution)/shard_map/reduce_scatter | solution.py:145
  209.5 154.0 %copy-start.25 = (f32[256]{0:T(256)S(1)}, f32[256]{0:T(256)}, u32[]{:S(2)}) copy-start(f32[256]{0:T(256)} %param.26) | copy-start | bytes 3076
  209.5 184.5 %all-gather.14.cloned.1.call-start = ((), (), s32[]{:S(2)}) async-start(), calls=%async_computation.13 | async-start | bytes 2359296 | tf_op jit(solution)/shard_map/all_gather | solution.py:135
  210.1 175.0 %copy-start.21 = (f32[256]{0:T(256)S(1)}, f32[256]{0:T(256)}, u32[]{:S(2)}) copy-start(f32[256]{0:T(256)} %param.27) | copy-start | bytes 3076
  210.1 175.0 %copy-start.26 = (f32[256]{0:T(256)S(1)}, f32[256]{0:T(256)}, u32[]{:S(2)}) copy-start(f32[256]{0:T(256)} %param.28) | copy-start | bytes 3076
  210.1 273.2 %all-gather.12.cloned.1.call-start = ((), (), s32[]{:S(2)}) async-start(), calls=%async_computation.12 | async-start | bytes 10485760 | tf_op jit(solution)/shard_map/all_gather | solution.py:15
  389.0 128.4 %all-gather.16.cloned.1.call-start = ((), (), s32[]{:S(2)}) async-start(), calls=%async_computation.14 | async-start | bytes 2359296 | tf_op jit(solution)/shard_map/all_gather | solution.py:139
  389.6 214.4 %all-gather.18.cloned.1.call-start = ((), (), s32[]{:S(2)}) async-start(), calls=%async_computation.16 | async-start | bytes 10485760 | tf_op jit(solution)/shard_map/all_gather | solution.py:15
  390.3 370.6 %reduce-scatter.18.cloned.1.call-start = ((), (), s32[]{:S(2)}) async-start(), calls=%async_computation.15 | async-start | bytes 20971520 | tf_op jit(solution)/shard_map/reduce_scatter | solution.py:19
  536.0 381.8 %reduce-scatter.20.cloned.1.call-start = ((), (), s32[]{:S(2)}) async-start(), calls=%async_computation.17 | async-start | bytes 20971520 | tf_op jit(solution)/shard_map/reduce_scatter | solution.py:19
  643.0 274.8 %copy-start.27 = (f32[256]{0:T(256)S(1)}, f32[256]{0:T(256)}, u32[]{:S(2)}) copy-start(f32[256]{0:T(256)} %param.32) | copy-start | bytes 3076
  643.1 296.7 %copy-start.1 = (bf16[4096,256]{1,0:T(8,128)(2,1)S(1)}, bf16[4096,256]{1,0:T(8,128)(2,1)}, u32[]{:S(2)}) copy-start(bf16[4096,256]{1,0:T(8,128)(2,1)} %param.33) | copy-start | bytes 6291460
  643.1 392.8 %all-gather.20.cloned.1.call-start = ((), (), s32[]{:S(2)}) async-start(), calls=%async_computation.18 | async-start | bytes 10485760 | tf_op jit(solution)/shard_map/all_gather | solution.py:15
  948.4 247.3 %reduce-scatter.32.cloned.1.call-start = ((), (), s32[]{:S(2)}) async-start(), calls=%async_computation.24 | async-start | bytes 2359296
  966.6 231.1 %reduce-scatter.26.cloned.1.call-start = ((), (), s32[]{:S(2)}) async-start(), calls=%async_computation.21 | async-start | bytes 2359296 | tf_op jit(solution)/shard_map/reduce_scatter | solution.py:215
  981.6 218.1 %reduce-scatter.30.cloned.1.call-start = ((), (), s32[]{:S(2)}) async-start(), calls=%async_computation.23 | async-start | bytes 589824
  1151.0 61.7 %reduce-scatter.24.cloned.1.call-start = ((), (), s32[]{:S(2)}) async-start(), calls=%async_computation.20 | async-start | bytes 1769472 | tf_op jit(solution)/shard_map/reduce_scatter | solution.py:212
  1167.0 205.0 %reduce-scatter.22.cloned.1.call-start = ((), (), s32[]{:S(2)}) async-start(), calls=%async_computation.19 | async-start | bytes 20971520 | tf_op jit(solution)/shard_map/reduce_scatter | solution.py:19
  1180.1 191.9 %copy-start.12 = (f32[4096]{0:T(1024)S(1)}, f32[4096]{0:T(1024)}, u32[]{:S(2)}) copy-start(f32[4096]{0:T(1024)} %copy-done.11) | copy-start | bytes 49156
  1180.1 191.9 %copy-start.14 = (f32[4096]{0:T(1024)S(1)}, f32[4096]{0:T(1024)}, u32[]{:S(2)}) copy-start(f32[4096]{0:T(1024)} %copy-done.13) | copy-start | bytes 49156
  1180.1 191.9 %copy-start.23 = (f32[256]{0:T(256)S(1)}, f32[256]{0:T(256)}, u32[]{:S(2)}) copy-start(f32[256]{0:T(256)} %param.20) | copy-start | bytes 3076
  1180.1 238.9 %reduce-scatter.28.cloned.1.call-start = ((), (), s32[]{:S(2)}) async-start(), calls=%async_computation.22 | async-start | bytes 73728
  (27 other events, 776.4 us)
Sparse Core Ops, SparseCore 0:
  9.6 26.1 all-gather.9
  53.1 86.7 all-gather.7
  209.6 153.7 reduce-scatter.15
  364.9 29.0 all-gather.13
  396.3 86.9 all-gather.11
  484.7 32.6 all-gather.15
  519.2 84.7 all-gather.17
  607.1 153.7 reduce-scatter.17
  764.0 153.7 reduce-scatter.19
  948.5 87.3 all-gather.19
  1038.2 32.0 reduce-scatter.31
  1072.5 34.4 reduce-scatter.25
  1151.1 27.2 reduce-scatter.29
  1180.7 31.9 reduce-scatter.23
  1215.9 155.9 reduce-scatter.21
  1392.6 26.3 reduce-scatter.27
where the time goes:
time: 1440 us; the launch traced here: 1430 us
  waiting for transfers between devices  912 us (63%)
  matrix products  209 us (15%)
  local copies, waits for them, and re-layouts  137 us (10%)
  blocking collectives  89.6 us (6%)
  other arithmetic  62.6 us (4%)
  between operations  15.4 us (1%)
    reduce_scatter x3, waiting for transfers between devices, feature_share(): lax.psum_scatter(partial_value, 'hid', scatter_dimension=1, tiled=True)  432 us
    all_gather x4, waiting for transfers between devices, full_features(): return lax.all_gather(values, 'hid', axis=1, tiled=True)  284 us
    reduce_scatter x1, waiting for transfers between devices, shards(): lax.psum_scatter(jnp.dot(attended, output_cols, preferred_element_type=jn...  153 us
    another operation x7, local copies, waits for them, and re-layouts, attend_backward(): return jnp.stack(pieces, axis=1).astype(jnp.bfloat16)  42.5 us
    another operation x6, local copies, waits for them, and re-layouts, split_heads(): return values.reshape(positions // BLOCK, BLOCK, features // HEAD, HEAD)  37 us
    psum x2, blocking collectives, norm_forward(): lax.psum((jnp.sum(summed, axis=1), jnp.sum(summed * summed, axis=1)), 'hid')  31.9 us
    psum x2, blocking collectives, norm_backward(): lax.psum(jnp.sum(weighted * scaled, axis=1).astype(jnp.bfloat16), 'hid')  30.1 us
  transfers between devices with their start and end apart: 16, of which 12 were waited for; matrix products, arithmetic and copies ran while one was open for 22% of the time, Pallas kernels for 0%

commit v1 on v0

v1 whole, which is shorter than its diff:
```python
import jax
import jax.numpy as jnp
from jax import lax
from jax.sharding import PartitionSpec as P

D = 1024
HEAD = 64
BLOCK = 128


epsilon = 1e-05


def split_heads(values):
    positions, features = values.shape
    return values.reshape(positions // BLOCK, BLOCK, features // HEAD, HEAD)


def block_logits(queries, key_rows):
    scores = jnp.einsum("bqhd,bkhd->bhqk", queries, key_rows, preferred_element_type=jnp.float32)
    logits = scores * HEAD ** (-0.5)
    places = jnp.arange(BLOCK)
    allowed = places[:, None] >= places[None, :]
    return jnp.where(allowed, logits, -1e30)


def project_heads(normed, attend_full, biases):
    return (
        jnp.einsum("td,dck->tck", normed, attend_full, preferred_element_type=jnp.float32) + biases
    ).astype(jnp.bfloat16)


def attend_forward(projected):
    queries = split_heads(projected[:, 0])
    key_rows = split_heads(projected[:, 1])
    value_rows = split_heads(projected[:, 2])
    logits = block_logits(queries, key_rows)
    totals = jax.nn.logsumexp(logits, axis=-1, keepdims=True)
    attention = jnp.exp(logits - totals).astype(jnp.bfloat16)
    attended = jnp.einsum(
        "bhqk,bkhd->bqhd", attention, value_rows, preferred_element_type=jnp.float32
    )
    return (attended.reshape(projected.shape[0], projected.shape[2]).astype(jnp.bfloat16), totals)


def attend_backward(projected, totals, grad_attended):
    positions, features = grad_attended.shape
    queries = split_heads(projected[:, 0])
    key_rows = split_heads(projected[:, 1])
    value_rows = split_heads(projected[:, 2])
    grad_heads = split_heads(grad_attended)
    logits = block_logits(queries, key_rows)
    attention_f = jnp.exp(logits - totals)
    attention_b = attention_f.astype(jnp.bfloat16)
    grad_attention = jnp.einsum(
        "bqhd,bkhd->bhqk", grad_heads, value_rows, preferred_element_type=jnp.float32
    )
    grad_values = jnp.einsum(
        "bhqk,bqhd->bkhd", attention_b, grad_heads, preferred_element_type=jnp.float32
    )
    centre = jnp.sum(attention_f * grad_attention, axis=-1, keepdims=True)
    grad_scores = (attention_f * (grad_attention - centre) * HEAD ** (-0.5)).astype(jnp.bfloat16)
    grad_queries = jnp.einsum(
        "bhqk,bkhd->bqhd", grad_scores, key_rows, preferred_element_type=jnp.float32
    )
    grad_keys = jnp.einsum(
        "bhqk,bqhd->bkhd", grad_scores, queries, preferred_element_type=jnp.float32
    )
    pieces = [
        member.reshape(positions, features) for member in (grad_queries, grad_keys, grad_values)
    ]
    return jnp.stack(pieces, axis=1).astype(jnp.bfloat16)


def spread(values):
    return lax.all_to_all(values, "hid", split_axis=0, concat_axis=1, tiled=True)


def unspread(values):
    return lax.all_to_all(values, "hid", split_axis=1, concat_axis=0, tiled=True)


def gather_all(part):
    return lax.all_gather(part, ("hid", "tok"), axis=0)


def scatter_all(partial_value):
    return lax.psum_scatter(
        partial_value.astype(jnp.bfloat16), ("hid", "tok"), scatter_dimension=0
    ).astype(jnp.float32)


def whole(vector):
    return lax.all_gather(vector, "hid", axis=0, tiled=True)


def norm_stats(values):
    average = jnp.mean(values, axis=1, keepdims=True)
    inverse = lax.rsqrt(
        jnp.mean(values * values, axis=1, keepdims=True) - average * average + epsilon
    )
    return (values - average) * inverse, inverse


def norm_backward(upstream, scaled, inverse, gain_row):
    weighted = upstream * gain_row
    mean_weighted = jnp.mean(weighted, axis=1, keepdims=True)
    mean_dot = jnp.mean(weighted * scaled, axis=1, keepdims=True)
    grad_input = inverse * (weighted - mean_weighted - scaled * mean_dot)
    return (grad_input, jnp.sum(upstream * scaled, axis=0), jnp.sum(upstream, axis=0))


def shards(
    tokens,
    middle_cond,
    coarse_cond,
    first_gain,
    first_shift,
    attend_weight,
    query_bias,
    value_bias,
    output_weight,
    mixer_bias,
    second_gain,
    second_shift,
    up_weight,
    hidden_bias,
    down_weight,
    down_bias,
    cotangent,
):
    positions, features = tokens.shape
    n_hid = lax.axis_size("hid")
    n_tok = lax.axis_size("tok")
    summed_part = (
        tokens.astype(jnp.float32).reshape(positions // 16, 4, 4, features)
        + middle_cond.astype(jnp.float32).reshape(positions // 16, 4, 1, features)
        + coarse_cond.astype(jnp.float32)[:, None, None, :]
    ).reshape(positions, features)
    summed = spread(summed_part.astype(jnp.bfloat16)).astype(jnp.float32)
    first_gain, first_shift, query_bias, value_bias = map(
        whole, (first_gain, first_shift, query_bias, value_bias)
    )
    mixer_bias, second_gain, second_shift, down_bias, hidden_bias = map(
        whole, (mixer_bias, second_gain, second_shift, down_bias, hidden_bias)
    )
    attend_full = (
        gather_all(attend_weight)
        .reshape(n_hid, D, 3, features)
        .transpose(1, 2, 0, 3)
        .reshape(D, 3, D)
    )
    output_full = (
        gather_all(output_weight)
        .reshape(n_hid, n_tok, features, D // n_tok)
        .transpose(0, 2, 1, 3)
        .reshape(D, D)
    )
    up_full = gather_all(up_weight).reshape(n_hid, D, up_weight.shape[1])
    down_full = (
        gather_all(down_weight)
        .reshape(n_hid, n_tok, down_weight.shape[0], D // n_tok)
        .transpose(0, 2, 1, 3)
        .reshape(n_hid, down_weight.shape[0], D)
    )
    scaled, inverse = norm_stats(summed)
    normed = (scaled * first_gain + first_shift).astype(jnp.bfloat16)
    biases = jnp.stack([query_bias, jnp.zeros_like(query_bias), value_bias])
    projected = project_heads(normed, attend_full, biases)
    attended, totals = attend_forward(projected)
    branch_out = jnp.dot(attended, output_full, preferred_element_type=jnp.float32)
    residual = summed + (branch_out + mixer_bias)
    scaled_two, inverse_two = norm_stats(residual)
    normed_two = (scaled_two * second_gain + second_shift).astype(jnp.bfloat16)
    upstream_low = spread(cotangent)
    upstream = upstream_low.astype(jnp.float32)
    hidden_chunk = up_weight.shape[1]
    feed_out = 0.0
    grad_normed_two = 0.0
    grad_ups, grad_downs, grad_hidden_biases = [], [], []
    for chunk in range(n_hid):
        bias = hidden_bias[chunk * hidden_chunk : (chunk + 1) * hidden_chunk]
        before = jnp.dot(normed_two, up_full[chunk], preferred_element_type=jnp.float32) + bias
        activated, gelu_pull = jax.vjp(jax.nn.gelu, before)
        hidden = activated.astype(jnp.bfloat16)
        feed_out = feed_out + jnp.dot(hidden, down_full[chunk], preferred_element_type=jnp.float32)
        grad_downs.append(
            jnp.einsum("tf,td->fd", hidden, upstream_low, preferred_element_type=jnp.float32)
        )
        grad_hidden = jnp.einsum(
            "td,fd->tf", upstream_low, down_full[chunk], preferred_element_type=jnp.float32
        )
        grad_before = gelu_pull(grad_hidden)[0].astype(jnp.bfloat16)
        grad_hidden_biases.append(jnp.sum(grad_before.astype(jnp.float32), axis=0))
        grad_ups.append(
            jnp.einsum("td,tf->df", normed_two, grad_before, preferred_element_type=jnp.float32)
        )
        grad_normed_two = grad_normed_two + jnp.einsum(
            "tf,df->td", grad_before, up_full[chunk], preferred_element_type=jnp.float32
        )
    layer_out = unspread((residual + (feed_out + down_bias)).astype(jnp.bfloat16))
    grad_up = scatter_all(
        jnp.stack(grad_ups).astype(jnp.bfloat16).reshape(n_hid * n_tok, D // n_tok, hidden_chunk)
    )
    grad_down = scatter_all(
        jnp.stack(grad_downs)
        .astype(jnp.bfloat16)
        .reshape(n_hid, hidden_chunk, n_tok, D // n_tok)
        .transpose(0, 2, 1, 3)
        .reshape(n_hid * n_tok, hidden_chunk, D // n_tok)
    )
    grad_down_bias = jnp.sum(upstream, axis=0)
    grad_back_two, grad_second_gain, grad_second_shift = norm_backward(
        grad_normed_two, scaled_two, inverse_two, second_gain
    )
    grad_residual = upstream + grad_back_two
    grad_mixed = grad_residual.astype(jnp.bfloat16)
    grad_mixer_bias = jnp.sum(grad_mixed.astype(jnp.float32), axis=0)
    grad_output = scatter_all(
        jnp.einsum("tk,td->kd", attended, grad_mixed, preferred_element_type=jnp.float32)
        .astype(jnp.bfloat16)
        .reshape(n_hid, features, n_tok, D // n_tok)
        .transpose(0, 2, 1, 3)
        .reshape(n_hid * n_tok, features, D // n_tok)
    )
    grad_attended = jnp.einsum(
        "td,kd->tk", grad_mixed, output_full, preferred_element_type=jnp.float32
    ).astype(jnp.bfloat16)
    grad_projected = attend_backward(projected, totals, grad_attended)
    grad_query_bias = jnp.sum(grad_projected[:, 0].astype(jnp.float32), axis=0)
    grad_value_bias = jnp.sum(grad_projected[:, 2].astype(jnp.float32), axis=0)
    grad_attend = scatter_all(
        jnp.einsum("td,tck->dck", normed, grad_projected, preferred_element_type=jnp.float32)
        .astype(jnp.bfloat16)
        .reshape(n_tok, D // n_tok, 3, n_hid, features)
        .transpose(3, 0, 1, 2, 4)
        .reshape(n_hid * n_tok, D // n_tok, 3, features)
    )
    grad_normed = jnp.einsum(
        "tck,dck->td", grad_projected, attend_full, preferred_element_type=jnp.float32
    )
    grad_back, grad_first_gain, grad_first_shift = norm_backward(
        grad_normed, scaled, inverse, first_gain
    )
    grad_tokens = unspread((grad_residual + grad_back).astype(jnp.bfloat16)).astype(jnp.float32)
    grad_middle = jnp.sum(grad_tokens.reshape(positions // 4, 4, features), axis=1)
    grad_coarse = jnp.sum(grad_tokens.reshape(positions // 16, 16, features), axis=1)
    small_grads = jnp.stack(
        [
            grad_first_gain,
            grad_first_shift,
            grad_second_gain,
            grad_second_shift,
            grad_query_bias,
            grad_value_bias,
            grad_mixer_bias,
            grad_down_bias,
        ]
    )
    share = D // (n_hid * n_tok)
    wide = hidden_chunk // n_tok
    packed = jnp.concatenate(
        [
            small_grads.reshape(8, n_hid * n_tok, share)
            .transpose(1, 0, 2)
            .reshape(n_hid * n_tok, 8 * share),
            jnp.concatenate(grad_hidden_biases).reshape(n_hid * n_tok, wide),
        ],
        axis=1,
    )
    packed = lax.psum_scatter(packed, ("hid", "tok"), scatter_dimension=0)
    small = packed[: 8 * share].reshape(8, share)
    return (
        layer_out,
        grad_tokens,
        grad_middle,
        grad_coarse,
        small[0],
        small[1],
        grad_attend,
        small[4],
        small[5],
        grad_output,
        small[6],
        small[2],
        small[3],
        grad_up,
        packed[8 * share :],
        grad_down,
        small[7],
    )


def solution(mesh):
    return jax.shard_map(
        shards,
        mesh=mesh,
        in_specs=(
            P("tok", "hid"),
            P("tok", "hid"),
            P("tok", "hid"),
            P("hid"),
            P("hid"),
            P("tok", None, "hid"),
            P("hid"),
            P("hid"),
            P("hid", "tok"),
            P("hid"),
            P("hid"),
            P("hid"),
            P("tok", "hid"),
            P("hid"),
            P("hid", "tok"),
            P("hid"),
            P("tok", "hid"),
        ),
        out_specs=(
            P("tok", "hid"),
            P("tok", "hid"),
            P("tok", "hid"),
            P("tok", "hid"),
            P(("hid", "tok")),
            P(("hid", "tok")),
            P("tok", None, "hid"),
            P(("hid", "tok")),
            P(("hid", "tok")),
            P("hid", "tok"),
            P(("hid", "tok")),
            P(("hid", "tok")),
            P(("hid", "tok")),
            P("tok", "hid"),
            P(("hid", "tok")),
            P("hid", "tok"),
            P(("hid", "tok")),
        ),
        check_vma=False,
    )
```

time: 1440 us -> 1030 us (0.72)
  waiting for transfers between devices: 912 us -> 359 us
  local copies, waits for them, and re-layouts: 137 us -> 209 us
  blocking collectives: 89.6 us -> 147 us
  starting transfers between devices: 0.65 us -> 18.7 us
    reduce_scatter x6 -> x4, waiting for transfers between devices: 597 us -> 263 us  [scatter_all(): lax.psum_scatter(partial_value.astype(jnp.bfloat16), ('hid', 'tok'), scat...]
    all_gather x7 -> x4, waiting for transfers between devices: 306 us -> 69 us  [gather_all(): return lax.all_gather(part, ('hid', 'tok'), axis=0)]
    all_gather x1 -> x9, blocking collectives: 14.4 us -> 92.8 us  [whole(): return lax.all_gather(vector, 'hid', axis=0, tiled=True)]
    psum x4 -> x0, blocking collectives: 62.1 us -> none  [the longest x2 31.9 us: norm_forward(): lax.psum((jnp.sum(summed, axis=1), jnp.sum(summed * summed, axis=1)), 'hid')]
    unnamed x1, blocking collectives: 13.2 us -> 54.1 us
    reshape x1 -> x5, local copies, waits for them, and re-layouts: 5.19 us -> 37.3 us  [the longest x2 21.7 us: shards(): attend_full = gather_all(attend_weight).reshape(n_hid, D, 3, features).tr...]
    all_to_all x0 -> x4, waiting for transfers between devices: none -> 24.8 us  [the longest x2 24.8 us: unspread(): lax.all_to_all(values, 'hid', split_axis=1, concat_axis=0, tiled=True)]
    slice x0 -> x7, local copies, waits for them, and re-layouts: none -> 23.1 us  [the longest x5 21.9 us: shards(): down_full[chunk]]
  transfers between devices with their start and end apart: 16 -> 12, of which waited for: 12 -> 5; matrix products, arithmetic and copies ran while one was open for 22% -> 36% of each run, Pallas kernels for 0% -> 0%
where the time goes in v1:
time: 1030 us; the launch traced here: 1020 us
  waiting for transfers between devices  359 us (35%)
  matrix products  213 us (21%)
  local copies, waits for them, and re-layouts  209 us (20%)
  blocking collectives  147 us (14%)
  other arithmetic  56.6 us (5%)
  starting transfers between devices  18.7 us (2%)
  between operations  15.6 us (2%)
    reduce_scatter x4, waiting for transfers between devices, scatter_all(): lax.psum_scatter(partial_value.astype(jnp.bfloat16), ('hid', 'tok'), scat...  263 us
    all_gather x9, blocking collectives, whole(): return lax.all_gather(vector, 'hid', axis=0, tiled=True)  92.8 us
    all_gather x4, waiting for transfers between devices, gather_all(): return lax.all_gather(part, ('hid', 'tok'), axis=0)  69 us
    unnamed x1, blocking collectives  54.1 us
    another operation x6, local copies, waits for them, and re-layouts, split_heads(): return values.reshape(positions // BLOCK, BLOCK, features // HEAD, HEAD)  37.1 us
    dot_general x4, matrix products, shards(): jnp.einsum('td,fd->tf', upstream_low, down_full[chunk], preferred_element...  36.2 us
    another operation x6, local copies, waits for them, and re-layouts, attend_backward(): return jnp.stack(pieces, axis=1).astype(jnp.bfloat16)  28.8 us
    all_to_all x2, waiting for transfers between devices, unspread(): lax.all_to_all(values, 'hid', split_axis=1, concat_axis=0, tiled=True)  24.8 us
  transfers between devices with their start and end apart: 12, of which 5 were waited for; matrix products, arithmetic and copies ran while one was open for 36% of the time, Pallas kernels for 0%

profile of v1, /device:TPU:8, one launch (start us, length us, event | category | flops | bytes accessed | tf_op | source)
XLA Modules:
  0.0 1019.3 jit_solution(813149926506061994)
XLA Ops:
  38.9 30.3 %all-gather.5 = f32[4,1,256]{2,1,0:T(1,128)S(1)} all-gather(f32[1,1,256]{2,1,0:T(1,128)S(1)} %bitcast.342), channel_id=1, replica_groups=mesh['tok'=8,'hid'=4] {'hid'}, dimensions={0}, use_global_device_ids=true | all-gather | bytes 5120 | tf_op jit(solution)/shard_map/all_gather | solution.py:94
  69.7 8.6 all-gather.4
  83.0 8.0 all-gather.8
  98.1 8.0 all-gather.6
  113.3 8.0 all-gather.9
  140.6 23.8 %all-gather.17.cloned.1.call-done = bf16[4096,3,256]{2,0,1:T(8,128)(2,1)} async-done(((bf16[128,3,256]{2,0,1:T(8,128)(2,1)}), bf16[4096,3,256]{2,0,1:T(8,128)(2,1)}) %all-gather.17.cloned.1.call-update) | async-done | bytes 6291472 | tf_op jit(solution)/shard_map/all_gather | solution.py:84
  164.4 10.4 %copy.229 = bf16[4,1024,3,256]{3,0,1,2:T(4,128)(2,1)} copy(bf16[4,1024,3,256]{3,1,0,2:T(8,128)(2,1)} %bitcast.306) | data formatting | bytes 12582912 | tf_op jit(solution)/shard_map/reshape | solution.py:149
  174.7 11.3 %reshape.314 = bf16[1024,3,1024]{2,0,1:T(8,128)(2,1)} reshape(bf16[1024,3,4,256]{3,2,0,1:T(4,128)(2,1)} %bitcast.297) | data formatting | bytes 12582912 | tf_op jit(solution)/shard_map/reshape | solution.py:151
  186.1 9.5 add_convert_fusion
  276.3 45.2 %all-gather.21.cloned.1.call-done = bf16[4096,1024]{1,0:T(8,128)(2,1)} async-done(((bf16[128,1024]{1,0:T(8,128)(2,1)}), bf16[4096,1024]{1,0:T(8,128)(2,1)}) %all-gather.21.cloned.1.call-update) | async-done | bytes 8388624 | tf_op jit(solution)/shard_map/all_gather | solution.py:84
  328.1 9.3 convert_reduce_fusion.1
  339.9 8.8 convert_reduce_fusion.2
  351.2 8.8 convert_reduce_fusion.4
  362.5 9.2 convert_reduce_fusion.3
  438.3 17.2 %convert_bitcast_fusion.10 = bf16[8,128,16,64]{1,3,2,0:T(8,128)(2,1)} fusion(bf16[8,128,16,64]{1,3,2,0:T(8,128)(2,1)} %copy.140, f32[8,16,128,128]{2,3,1,0:T(8,128)} %fusion.163, f32[8,16,128,128]{2,3,1,0:T(8,128)} %copy-done.3, f32[8,16,128]{2,1,0:T(8,128)S(1)} %log_add_fusion, pred[128,128]{0,1:T(8,128)(4,1)S(1)} %iota_compare_fusion), kind=kOutput, calls=%fused_computation.137 | convolution fusion | flops 292569216 | bytes 21053440 | tf_op jit(solution)/shard_map/bhqk,bqhd->bkhd/dot_general | solution.py:66
  467.6 17.3 %convert_bitcast_fusion.11 = bf16[8,128,16,64]{1,3,2,0:T(8,128)(2,1)} fusion(bf16[8,128,16,64]{1,3,2,0:T(8,128)(2,1)} %copy.141, f32[8,16,128,128]{2,3,1,0:T(8,128)} %fusion.163, f32[8,16,128,128]{2,3,1,0:T(8,128)} %copy-done.3, f32[8,16,128]{2,1,0:T(8,128)S(1)} %log_add_fusion, pred[128,128]{0,1:T(8,128)(4,1)S(1)} %iota_compare_fusion), kind=kOutput, calls=%fused_computation.138 | convolution fusion | flops 292569216 | bytes 21053440 | tf_op jit(solution)/shard_map/bhqk,bkhd->bqhd/dot_general | solution.py:63
  498.3 14.1 %fusion.55 = (f32[1024]{0:T(1024)S(1)}, f32[1024]{0:T(1024)S(1)}, f32[1024]{0:T(1024)S(1)}, f32[1024]{0:T(1024)S(1)}, bf16[1024,1024]{0,1:T(8,128)(2,1)S(1)}, /*index=5*/f32[1024,1024,1]{0,1,2:T(8,128)}) fusion(bf16[4,1024,256]{1,2,0:T(8,128)(2,1)S(1)} %all-to-all-done, f32[1024]{0:T(1024)S(1)} %copy-done.28, f32[1024]{0:T(1024)S(1)} %copy-done.30, ...), kind=kOutput, calls=%fused_computation.72 | convolution fusion | flops 6462369792 | bytes 21004288 | tf_op jit(solution)/shard_map/tck,dck->td/dot_general | solution.py:239
  512.4 8.6 convolution_convert_fusion
  521.0 11.2 %reshape.320 = bf16[8,128,3,4,256]{4,3,1,0,2:T(4,128)(2,1)} reshape(bf16[1024,3,1024]{2,0,1:T(8,128)(2,1)} %convolution_convert_fusion) | data formatting | bytes 12582912 | tf_op jit(solution)/shard_map/reshape | solution.py:235
  582.5 8.3 all-gather.11
  626.1 24.7 %all-to-all-done.1 = bf16[1024,4,256]{0,2,1:T(8,128)(2,1)} async-done(((bf16[1024,4,256]{0,2,1:T(8,128)(2,1)}), bf16[1024,4,256]{0,2,1:T(8,128)(2,1)}, u32[]{:S(2)}, u32[]{:S(2)}) %all-to-all-start.1) | async-done | bytes 2097184 | tf_op jit(solution)/shard_map/all_to_all | solution.py:80
  661.6 54.1 %all-reduce = f32[32,384]{1,0:T(8,128)S(1)} all-reduce(f32[32,384]{1,0:T(8,128)S(1)} %maximum_maximum_fusion), channel_id=6, replica_groups=mesh['tok'=8,'hid'=4] {'hid','tok'}, use_global_device_ids=true, to_apply=%region_25.26.clone | all-reduce | flops 12288 | bytes 98304
  745.7 112.7 %reduce-scatter.9.cloned.1.call-done = bf16[1,128,1024]{2,1,0:T(8,128)(2,1)} async-done(((bf16[32,128,1024]{2,1,0:T(8,128)(2,1)}), bf16[1,128,1024]{2,1,0:T(8,128)(2,1)}) %reduce-scatter.9.cloned.1.call-update) | async-done | bytes 262160 | tf_op jit(solution)/shard_map/reduce_scatter | solution.py:88
  860.2 150.0 %reduce-scatter.11.cloned.1.call-done = bf16[1,1024,128]{2,1,0:T(8,128)(2,1)} async-done(((bf16[32,1024,128]{2,1,0:T(8,128)(2,1)}), bf16[1,1024,128]{2,1,0:T(8,128)(2,1)}) %reduce-scatter.11.cloned.1.call-update) | async-done | bytes 262160 | tf_op jit(solution)/shard_map/reduce_scatter | solution.py:88
  (283 shorter events, 386.1 us)
Async XLA Ops:
  7.2 129.1 %all-gather.19.cloned.1.call-start = ((), (), s32[]{:S(2)}) async-start(), calls=%async_computation.13 | async-start | bytes 2162688 | tf_op jit(solution)/shard_map/all_gather | solution.py:84
  7.9 156.4 %all-gather.17.cloned.1.call-start = ((), (), s32[]{:S(2)}) async-start(), calls=%async_computation.12 | async-start | bytes 6488064 | tf_op jit(solution)/shard_map/all_gather | solution.py:84
  8.7 245.7 %all-gather.23.cloned.1.call-start = ((), (), s32[]{:S(2)}) async-start(), calls=%async_computation.15 | async-start | bytes 8650752 | tf_op jit(solution)/shard_map/all_gather | solution.py:84
  9.4 312.2 %all-gather.21.cloned.1.call-start = ((), (), s32[]{:S(2)}) async-start(), calls=%async_computation.14 | async-start | bytes 8650752 | tf_op jit(solution)/shard_map/all_gather | solution.py:84
  32.6 37.1 %copy-start.48 = (f32[256]{0:T(256)S(1)}, f32[256]{0:T(256)}, u32[]{:S(2)}) copy-start(f32[256]{0:T(256)} %param.20) | copy-start | bytes 3076
  35.0 48.1 %copy-start.49 = (f32[256]{0:T(256)S(1)}, f32[256]{0:T(256)}, u32[]{:S(2)}) copy-start(f32[256]{0:T(256)} %param.26) | copy-start | bytes 3076
  35.0 56.1 %copy-start.50 = (f32[256]{0:T(256)S(1)}, f32[256]{0:T(256)}, u32[]{:S(2)}) copy-start(f32[256]{0:T(256)} %param.24) | copy-start | bytes 3076
  35.0 63.2 %copy-start.51 = (f32[256]{0:T(256)S(1)}, f32[256]{0:T(256)}, u32[]{:S(2)}) copy-start(f32[256]{0:T(256)} %param.23) | copy-start | bytes 3076
  35.0 71.2 %copy-start.52 = (f32[256]{0:T(256)S(1)}, f32[256]{0:T(256)}, u32[]{:S(2)}) copy-start(f32[256]{0:T(256)} %param.28) | copy-start | bytes 3076
  35.0 78.3 %copy-start.53 = (f32[256]{0:T(256)S(1)}, f32[256]{0:T(256)}, u32[]{:S(2)}) copy-start(f32[256]{0:T(256)} %param.27) | copy-start | bytes 3076
  35.0 86.3 %copy-start.36 = (f32[1024]{0:T(1024)S(1)}, f32[1024]{0:T(1024)}, u32[]{:S(2)}) copy-start(f32[1024]{0:T(1024)} %param.30) | copy-start | bytes 12292
  35.0 93.8 %all-to-all-start = ((bf16[4,1024,256]{1,2,0:T(8,128)(2,1)}), bf16[4,1024,256]{1,2,0:T(8,128)(2,1)S(1)}, u32[]{:S(2)}, u32[]{:S(2)}) async-start(bf16[4,1024,256]{1,2,0:T(8,128)(2,1)} %copy.134), calls=%async_computation | async-start | bytes 4194304 | tf_op jit(solution)/shard_map/all_to_all | solution.py:76
  128.8 199.3 %copy-start.41 = (f32[1024]{0:T(1024)}, f32[1024]{0:T(1024)S(1)}, u32[]{:S(2)}) copy-start(f32[1024]{0:T(1024)S(1)} %get-tuple-element.57) | copy-start | bytes 12292
  128.8 211.1 %copy-start.45 = (f32[1024]{0:T(1024)}, f32[1024]{0:T(1024)S(1)}, u32[]{:S(2)}) copy-start(f32[1024]{0:T(1024)S(1)} %get-tuple-element.58) | copy-start | bytes 12292
  128.8 222.4 %copy-start.43 = (f32[1024]{0:T(1024)}, f32[1024]{0:T(1024)S(1)}, u32[]{:S(2)}) copy-start(f32[1024]{0:T(1024)S(1)} %get-tuple-element.60) | copy-start | bytes 12292
  128.8 199.3 %all-to-all-start.2 = ((bf16[4,1024,256]{1,2,0:T(8,128)(2,1)}), bf16[4,1024,256]{1,2,0:T(8,128)(2,1)}, u32[]{:S(2)}, u32[]{:S(2)}) async-start(bf16[4,1024,256]{1,2,0:T(8,128)(2,1)} %copy.151), calls=%async_computation.2 | async-start | bytes 4194304 | tf_op jit(solution)/shard_map/all_to_all | solution.py:76
  133.3 609.2 %reduce-scatter.7.cloned.1.call-start = ((), (), s32[]{:S(2)}) async-start(), calls=%async_computation.9 | async-start | bytes 2162688 | tf_op jit(solution)/shard_map/reduce_scatter | solution.py:88
  337.5 41.5 %copy-start.22 = (bf16[1024,1024]{1,0:T(8,128)(2,1)}, bf16[1024,1024]{1,0:T(8,128)(2,1)S(1)}, u32[]{:S(2)}) copy-start(bf16[1024,1024]{1,0:T(8,128)(2,1)S(1)} %get-tuple-element.38) | copy-start | bytes 6291460
  431.2 312.8 %reduce-scatter.5.cloned.1.call-start = ((), (), s32[]{:S(2)}) async-start(), calls=%async_computation.8 | async-start | bytes 6488064 | tf_op jit(solution)/shard_map/reduce_scatter | solution.py:88
  538.9 319.5 %reduce-scatter.9.cloned.1.call-start = ((), (), s32[]{:S(2)}) async-start(), calls=%async_computation.10 | async-start | bytes 8650752 | tf_op jit(solution)/shard_map/reduce_scatter | solution.py:88
  554.9 455.3 %reduce-scatter.11.cloned.1.call-start = ((), (), s32[]{:S(2)}) async-start(), calls=%async_computation.11 | async-start | bytes 8650752 | tf_op jit(solution)/shard_map/reduce_scatter | solution.py:88
  611.5 39.3 %all-to-all-start.1 = ((bf16[1024,4,256]{0,2,1:T(8,128)(2,1)}), bf16[1024,4,256]{0,2,1:T(8,128)(2,1)}, u32[]{:S(2)}, u32[]{:S(2)}) async-start(bf16[1024,4,256]{0,2,1:T(8,128)(2,1)} %bitcast.322), calls=%async_computation.1 | async-start | bytes 4194304 | tf_op jit(solution)/shard_map/all_to_all | solution.py:80
  626.1 34.6 %copy-start.4 = (bf16[1024,1,1024]{0,2,1:T(8,128)(2,1)S(1)}, bf16[1024,1,1024]{0,2,1:T(8,128)(2,1)}, u32[]{:S(2)}) copy-start(bf16[1024,1,1024]{0,2,1:T(8,128)(2,1)} %stack_reshape.14) | copy-start | bytes 6291460
  650.8 71.4 %all-to-all-start.3 = ((bf16[1024,4,256]{2,0,1:T(8,128)(2,1)}), bf16[1024,4,256]{2,0,1:T(8,128)(2,1)}, u32[]{:S(2)}, u32[]{:S(2)}) async-start(bf16[1024,4,256]{2,0,1:T(8,128)(2,1)} %copy.167), calls=%async_computation.3 | async-start | bytes 4194304 | tf_op jit(solution)/shard_map/all_to_all | solution.py:80
  (59 other events, 429.7 us)
Sparse Core Ops, SparseCore 0:
  11.0 59.6 all-gather.18
  73.8 90.5 all-gather.16
  167.4 75.2 all-gather.22
  245.5 75.9 all-gather.20
  431.3 130.1 reduce-scatter.6
  567.9 142.7 reduce-scatter.4
  713.0 145.3 reduce-scatter.8
  860.7 149.4 reduce-scatter.10

commit v2 on v0

v2 whole, which is shorter than its diff:
```python
import functools

import jax
import jax.numpy as jnp
from jax import lax
from jax.experimental import pallas as pl
from jax.experimental.pallas import tpu as pltpu
from jax.sharding import PartitionSpec as P

HEAD = 64
BLOCK = 128
PAIR = 2 * HEAD
EPSILON = 1e-05
MESH = pl.DeviceIdType.MESH
BF16 = jnp.bfloat16
F32 = jnp.float32
SMALL_ROWS = 16


class Tree:
    def __init__(self, n_hid):
        self.n = n_hid
        self.bits = n_hid.bit_length() - 1
        units = [(r, f) for r in range(n_hid) for f in (0, 1)]
        self.units = sorted(units, key=lambda u: (u[0].bit_count(), len(self.children(*u)), u))
        self.pos = {u: k for k, u in enumerate(self.units)}

    def children(self, r, f):
        held = [b for b in range(self.bits) if r >> b & 1]
        free = [b for b in range(self.bits) if not r >> b & 1]
        if held:
            free = [b for b in free if (b < held[0] if f == 0 else b > held[-1])]
        return [(r | 1 << b, b) for b in free]

    def parent(self, r, f):
        held = [b for b in range(self.bits) if r >> b & 1]
        return held[0] if f == 0 else held[-1]


class Schedule:
    def __init__(self, tree, done, weights_lag, last_point):
        self.at = {}
        self.turn = {}
        self.before = {}
        self.first = set()
        sent = {}
        holders = [None, None]
        waiting = sorted(done, key=lambda u: done[u])
        held = None
        point = 0
        while waiting or held is not None:
            actions = []
            if held is not None:
                actions.append(("finish", held))
                sent[held] = point
                held = None
            for unit in waiting:
                kind, r, f = unit
                kids = [(kind, k, f) for k, _ in tree.children(r, f)]
                if point <= done[unit] or any(k not in sent for k in kids):
                    continue
                if point < last_point and any(point < sent[k] + weights_lag[kind] for k in kids):
                    continue
                actions.append(("fetch", unit))
                held = unit
                self.turn[unit] = k = len(self.turn) % 2
                self.before[unit] = holders[k]
                if (kind, r) not in {(other[0], other[1]) for other in self.turn if other != unit}:
                    self.first.add(unit)
                holders[k] = unit
                waiting.remove(unit)
                break
            if actions:
                self.at[point] = actions
            point += 1
        self.end = point
        self.holders = holders


def dot(a, b):
    return jnp.dot(a, b, preferred_element_type=F32)


def dot_t(a, b):
    return lax.dot_general(a, b, (((1,), (1,)), ((), ())), preferred_element_type=F32)


def dot_l(a, b):
    return lax.dot_general(a, b, (((0,), (0,)), ((), ())), preferred_element_type=F32)


def repeat_matrix(rows, times):
    row = lax.broadcasted_iota(jnp.int32, (rows, rows // times), 0)
    column = lax.broadcasted_iota(jnp.int32, (rows, rows // times), 1) * times
    return ((row >= column) & (row < column + times)).astype(BF16)


def group_matrix(rows, times):
    row = lax.broadcasted_iota(jnp.int32, (rows // times, rows), 0) * times
    column = lax.broadcasted_iota(jnp.int32, (rows // times, rows), 1)
    return ((column >= row) & (column < row + times)).astype(BF16)


def scaled_rows(values):
    width = values.shape[1]
    average = jnp.sum(values, axis=1, keepdims=True) / width
    square = jnp.sum(values * values, axis=1, keepdims=True) / width
    inverse = lax.rsqrt(square - average * average + EPSILON)
    return (values - average) * inverse, inverse


def norm_pull(grad, gain, scaled, inverse):
    width = grad.shape[1]
    weighted = grad * gain
    mean = jnp.sum(weighted, axis=1, keepdims=True) / width
    along = jnp.sum(weighted * scaled, axis=1, keepdims=True) / width
    return inverse * (weighted - mean - scaled * along)


def row_sum(values):
    return jnp.sum(values, axis=0, keepdims=True)


def two_heads(values):
    low = lax.broadcasted_iota(jnp.int32, values.shape, 1) < HEAD
    zero = jnp.zeros_like(values)
    return jnp.concatenate([jnp.where(low, values, zero), jnp.where(low, zero, values)], axis=0)


def pick_heads(both):
    low = lax.broadcasted_iota(jnp.int32, (BLOCK, PAIR), 1) < HEAD
    return jnp.where(low, both[:BLOCK], both[BLOCK:])


INPUTS = ("tokens", "middle", "coarse", "cotangent", "a_own", "m_own", "params")
OUTPUTS = (
    "layer_out",
    "grad_rows",
    "grad_a",
    "grad_m",
    "small",
    "all_a",
    "all_m",
    "own_ga",
    "sib_ga",
    "got_ga",
    "own_gm",
    "sib_gm",
    "got_gm",
    "z_ga",
    "z_gm",
)


class Sizes:
    def __init__(self, positions, features, d, ff, n_tok, n_hid):
        self.d, self.n_hid, self.n_tok = d, n_hid, n_tok
        self.z = n_tok // 2
        self.n = positions // n_hid
        self.kh = features
        self.fs = ff // n_hid // 2
        self.tb = d // n_tok
        self.half = self.tb // 2
        self.wide = 4 * features
        self.pairs = features // PAIR
        self.tile = min(256, self.n)
        self.tiles = self.n // self.tile
        self.blocks = self.n // BLOCK
        self.positions = positions


def layer_kernel(size, tree, *refs):
    names = list(INPUTS) + list(OUTPUTS) + list(scratch(size, tree))
    ref = dict(zip(names, refs, strict=True))
    s_ = size
    n_units = len(tree.units)
    tok, h = lax.axis_index("tok"), lax.axis_index("hid")
    z, c = tok // 2, lax.rem(tok, 2)

    def block_of(r):
        total = 0
        for b in range(tree.bits):
            total = total + lax.rem(h // (1 << b) + r // (1 << b), 2) * (1 << b)
        return total

    def peer(r):
        return (tok, block_of(r))

    sibling = (tok + 1 - 2 * c, h)

    def z_peer(step):
        return (lax.rem(z + step, s_.z) * 2 + c, h)

    def columns(j, width):
        return pl.ds(pl.multiple_of(j * width, width), width)

    def remote(name, index, src, dst, device):
        return pltpu.make_async_remote_copy(
            src_ref=src,
            dst_ref=dst,
            send_sem=ref[name + "_s"].at[index],
            recv_sem=ref[name + "_r"].at[index],
            device_id=device,
            device_id_type=MESH,
        )

    def send(name, index, src, dst, device):
        remote(name, index, src, dst, device).start()

    def arrived(name, index, dst):
        remote(name, index, dst, dst, sibling).wait_recv()

    def left(name, index, src):
        remote(name, index, src, src, sibling).wait_send()

    def local(index, src, dst):
        return pltpu.make_async_copy(src, dst, ref["local"].at[index])

    barrier = pltpu.get_barrier_semaphore()
    everyone = [peer(r) for r in range(1, s_.n_hid)] + [sibling]
    everyone += [z_peer(k) for k in range(1, s_.z)]
    for device in everyone:
        pl.semaphore_signal(barrier, inc=1, device_id=device, device_id_type=MESH)
    pl.semaphore_wait(barrier, len(everyone))

    def z_send(name, index, src, dst):
        for step in range(1, s_.z):
            send(name, index * s_.z + step, src, dst, z_peer(step))

    def z_arrived(name, index, dst):
        for step in range(1, s_.z):
            arrived(name, index * s_.z + step, dst)

    def z_left(name, index, src):
        for step in range(1, s_.z):
            left(name, index * s_.z + step, src)

    def a_part(r, f, core):
        return ref["all_a"].at[r, :, core, pl.ds(f * s_.half, s_.half)]

    def m_part(r, f, core):
        return ref["all_m"].at[tree.pos[r, f], :, core]

    part = {"a": a_part, "m": m_part}

    for r in range(1, s_.n_hid):
        here = ref["params_all"].at[:, columns(h, s_.kh)]
        send("params", r, ref["params"], here, peer(r))
    own_params = local(0, ref["params"], ref["params_all"].at[:, columns(h, s_.kh)])
    own_params.start()
    z_send("za", 0, ref["a_own"], ref["all_a"].at[0, z, c])
    own_a = local(1, ref["a_own"], ref["all_a"].at[0, z, c])
    own_a.start()
    own_m = []
    for f in (0, 1):
        own_m.append(local(2 + f, ref["m_own"].at[f], ref["all_m"].at[tree.pos[0, f], z, c]))
        own_m[f].start()

    kh, n, tile = s_.kh, s_.n, s_.tile
    rows_m, rows_c = n // 4, n // 16
    loads = {}
    order = list(range(1, s_.n_hid)) + [0]
    for r in order:
        j = block_of(r)
        sources = (
            (ref["tokens"].at[columns(j, n)], ref["pj"].at[r, :, pl.ds(0, kh)]),
            (ref["middle"].at[columns(j, rows_m)], ref["pj"].at[r, pl.ds(0, rows_m), pl.ds(2 * kh, kh)]),
            (ref["coarse"].at[columns(j, rows_c)], ref["pj"].at[r, pl.ds(rows_m, rows_c), pl.ds(2 * kh, kh)]),
        )
        loads[r] = [local(4 + 3 * r + k, *pair) for k, pair in enumerate(sources)]
        for copy in loads[r]:
            copy.start()
    repeat_4, repeat_16 = repeat_matrix(tile, 4), repeat_matrix(tile, 16)

    def xs_rows(i, j):
        return ref["xs"].at[pl.ds(i * tile, tile), columns(j, kh)]

    own_xs = []
    for i in range(s_.tiles):
        for r in order:
            if i == 0:
                for copy in loads[r]:
                    copy.wait()
            rows = pl.ds(i * tile, tile)
            middle = ref["pj"][r, pl.ds(i * (tile // 4), tile // 4), pl.ds(2 * kh, kh)]
            coarse = ref["pj"][r, pl.ds(rows_m + i * (tile // 16), tile // 16), pl.ds(2 * kh, kh)]
            total = ref["pj"][r, rows, pl.ds(0, kh)].astype(F32)
            total = total + dot(repeat_4, middle) + dot(repeat_16, coarse)
            ref["pj"][r, rows, pl.ds(kh, kh)] = total.astype(BF16)
            source = ref["pj"].at[r, rows, pl.ds(kh, kh)]
            if r:
                send("xs", i * s_.n_hid + r, source, xs_rows(i, h), peer(r))
            else:
                copy = local(4 + 3 * s_.n_hid + i, source, xs_rows(i, h))
                copy.start()
                own_xs.append(copy)

    for f in (0, 1):
        z_send("zm", f, ref["m_own"].at[f], ref["all_m"].at[tree.pos[0, f], z, c])

    def pass_on(kind, r, f):
        k = tree.pos[r, f]
        for child, b in tree.children(r, f):
            send(kind + "x", tree.pos[child, f], part[kind](r, f, c), part[kind](child, f, c), peer(1 << b))
        send(kind + "c", k, part[kind](r, f, c), part[kind](r, f, c), sibling)

    def take(kind, r, f):
        arrived(kind + "x", tree.pos[r, f], part[kind](r, f, c))
        pass_on(kind, r, f)

    def take_sibling(kind, r, f):
        arrived(kind + "c", tree.pos[r, f], part[kind](r, f, 1 - c))

    own_a.wait()
    z_arrived("za", 0, ref["all_a"].at[0, z, c])
    for f in (0, 1):
        pass_on("a", 0, f)

    own_params.wait()
    for r in range(1, s_.n_hid):
        arrived("params", r, ref["params_all"].at[:, columns(h, kh)])

    def gain_row(k):
        return ref["params_all"][pl.ds(k, 1), :]

    for k, (r, f) in enumerate(tree.units):
        parts = [
            ref["params_all"][pl.ds(8 + 2 * f + i, 1), columns(block_of(r), kh)] for i in range(s_.fs // kh)
        ]
        ref["hidden_bias"][k] = jnp.concatenate(parts, axis=1)
        ref["hidden_sum"][k] = jnp.zeros((1, s_.fs), F32)
    ref["sums"][...] = jnp.zeros_like(ref["sums"])

    def add_sum(k, values):
        ref["sums"][pl.ds(k, 1), :] = ref["sums"][pl.ds(k, 1), :] + row_sum(values)

    for i in range(s_.tiles):
        own_xs[i].wait()
        for r in range(1, s_.n_hid):
            arrived("xs", i * s_.n_hid + r, xs_rows(i, h))
        rows = pl.ds(i * tile, tile)
        scaled, _ = scaled_rows(ref["xs"][rows, :].astype(F32))
        normed = (scaled * gain_row(0) + gain_row(1)).astype(BF16)
        ref["nrm"][rows, :] = normed
        ref["nrm_t"][:, rows] = normed.T

    for i in range(s_.tiles):
        for r in range(1, s_.n_hid):
            left("xs", i * s_.n_hid + r, xs_rows(i, h))

    def weight_load(slot, source):
        return pltpu.make_async_copy(source, ref["wa"].at[slot], ref["wload"].at[slot])

    def matrix(slot, first, width):
        return ref["wa"][slot, :, :, :, pl.ds(first, width)].reshape(s_.d, width)

    def put_rows(slot, zz, first, values):
        width = values.shape[1]
        ref["wa"][slot, zz, :, :, pl.ds(first, width)] = values.reshape(2, s_.tb, width)

    def cot_rows(j):
        return ref["ct"].at[:, columns(j, kh)]

    own_ct = local(0, ref["cotangent"].at[columns(h, n)], cot_rows(h))

    def before_chunk(r):
        if r == 0:
            pass
        elif r.bit_count() == 1:
            if r == 1:
                for u, f in tree.units:
                    if u.bit_count() == 1:
                        take("a", u, f)
                own_ct.start()
                for k in range(1, s_.n_hid):
                    send("ct", k, ref["cotangent"].at[columns(block_of(k), n)], cot_rows(h), peer(k))
        else:
            for f in (0, 1):
                take("a", r, f)
        if r == s_.n_hid - 1:
            for f in (0, 1):
                own_m[f].wait()
                z_arrived("zm", f, ref["all_m"].at[tree.pos[0, f], z, c])
            for f in (0, 1):
                pass_on("m", 0, f)
        for f in (0, 1):
            take_sibling("a", r, f)
        load = weight_load(r, ref["all_a"].at[r])
        load.start()
        load.wait()

    causal_row = lax.broadcasted_iota(jnp.int32, (BLOCK, 2 * BLOCK), 0)
    causal_col = lax.rem(lax.broadcasted_iota(jnp.int32, (BLOCK, 2 * BLOCK), 1), BLOCK)
    allowed = causal_row >= causal_col

    def halves(values, f):
        return [f(values[:, :BLOCK]), f(values[:, BLOCK:])]

    def spread(pair):
        return jnp.concatenate([jnp.broadcast_to(v, (BLOCK, BLOCK)) for v in pair], axis=1)

    def row_max(v):
        return jnp.max(v, axis=1, keepdims=True)

    def row_add(v):
        return jnp.sum(v, axis=1, keepdims=True)

    def attend_chunk(r):
        for k in range(s_.n_hid):
            pl.when(r == k)(functools.partial(before_chunk, k))
        cols = columns(block_of(r), kh)
        bias = jnp.concatenate(
            [ref["params_all"][4:5, cols], jnp.zeros((1, kh), F32), ref["params_all"][5:6, cols]], axis=1
        )

        def project(i, _):
            rows = pl.ds(pl.multiple_of(i * tile, tile), tile)
            values = dot(ref["nrm"][rows, :], matrix(r, 0, 3 * kh)) + bias
            ref["pj"][r, rows, :] = values.astype(BF16)
            return 0

        lax.fori_loop(0, s_.tiles, project, 0)

        def attend(i, _):
            rows = pl.ds(pl.multiple_of(i * BLOCK, BLOCK), BLOCK)
            for p in range(s_.pairs):
                query, key, value = (ref["pj"][r, rows, pl.ds(k * kh + p * PAIR, PAIR)] for k in range(3))
                logits = jnp.where(allowed, dot_t(query, two_heads(key)) * HEAD ** (-0.5), -1e30)
                powers = jnp.exp(logits - spread(halves(logits, row_max)))
                shares = [1.0 / v for v in halves(powers, row_add)]
                attention = (powers * spread(shares)).astype(BF16)
                ref["probs"][r, p, rows, :] = attention
                out = dot(attention, two_heads(value))
                ref["att"][r, rows, pl.ds(p * PAIR, PAIR)] = out.astype(BF16)
            return 0

        lax.fori_loop(0, s_.blocks, attend, 0)

    lax.fori_loop(0, s_.n_hid, lambda r, _: (attend_chunk(r), 0)[1], 0)

    def mix(i, _):
        rows = pl.ds(pl.multiple_of(i * tile, tile), tile)
        total = ref["xs"][rows, :].astype(F32) + gain_row(6)
        for r in range(s_.n_hid):
            total = total + dot_t(ref["att"][r, rows, :], matrix(r, 3 * kh, kh))
        ref["res"][rows, :] = total
        scaled, _inverse = scaled_rows(total)
        normed = (scaled * gain_row(2) + gain_row(3)).astype(BF16)
        ref["n2"][rows, :] = normed
        return 0

    lax.fori_loop(0, s_.tiles, mix, 0)

    own_ct.wait()
    for k in range(1, s_.n_hid):
        arrived("ct", k, cot_rows(h))
    for i in range(s_.tiles):
        rows = pl.ds(i * tile, tile)
        ref["n2_t"][:, rows] = ref["n2"][rows, :].T
        upstream = ref["ct"][rows, :]
        ref["ct_t"][:, rows] = upstream.T
        add_sum(7, upstream.astype(F32))
        ref["facc"][rows, :] = jnp.zeros((tile, s_.d), F32)
        ref["gacc"][rows, :] = jnp.zeros((tile, s_.d), F32)

    mlp_points = 2 * n_units
    chunk_points = mlp_points + 2
    last_point = chunk_points + 4 * s_.n_hid
    done = {("m", r, f): 2 * k + 1 for k, (r, f) in enumerate(tree.units)}
    for r in range(s_.n_hid):
        for f in (0, 1):
            done["a", r, f] = chunk_points + 4 * (s_.n_hid - 1 - r) + 3
    plan = Schedule(tree, done, {"m": 6, "a": 4}, last_point)

    def own_grad(kind, r, f):
        if kind == "a":
            return ref["own_ga"].at[r, :, pl.ds(f * s_.half, s_.half)]
        return ref["own_gm"].at[tree.pos[r, f]]

    def sib_grad(kind, r, f):
        if kind == "a":
            return ref["sib_ga"].at[r, :, pl.ds(f * s_.half, s_.half)]
        return ref["sib_gm"].at[tree.pos[r, f]]

    def got_grad(kind, r, f):
        if kind == "a":
            return ref["got_ga"].at[tree.pos[r, f]]
        return ref["got_gm"].at[tree.pos[r, f]]

    def buffer(name, kind, k=None):
        whole = ref[name] if k is None else ref[name].at[k]
        return whole.at[:, pl.ds(0, s_.half)] if kind == "a" else whole

    def z_name(kind):
        return ("zga", 0) if kind == "a" else ("zgm", 1)

    def z_slot(kind, f, step):
        if kind == "a":
            return ref["z_ga"].at[f, step]
        return ref["z_gm"].at[f, step]

    def free_buffer(k, holder):
        if holder is None:
            return
        kind, r, f = holder
        source = buffer("acc", kind, k)
        if r:
            left("g" + kind, tree.pos[r, f], source)
        else:
            for step in range(1, s_.z):
                left("zg" + kind, f * s_.z + step, source.at[0])
            local(40 + k, source.at[0], source.at[0]).wait()

    def fetches(unit, k):
        kind, r, f = unit
        kids = tree.children(r, f)
        out = [(30 + 3 * k, own_grad(*unit), buffer("acc", kind, k))]
        out.append((31 + 3 * k, sib_grad(*unit), buffer("tmp", kind, k)))
        if kids:
            out.append((32 + 3 * k, got_grad(kind, kids[0][0], f), buffer("more", kind)))
        return out

    def fetch(unit):
        kind, r, f = unit
        k = plan.turn[unit]
        free_buffer(k, plan.before[unit])
        if kind == "m" or unit in plan.first:
            slot = tree.pos[r, f] if kind == "m" else r
            whole = ref["sib_gm"].at[slot] if kind == "m" else ref["sib_ga"].at[r]
            arrived("s" + kind, slot, whole)
        for kid, _ in tree.children(r, f)[:1]:
            arrived("g" + kind, tree.pos[kid, f], got_grad(kind, kid, f))
        for item in fetches(unit, k):
            local(*item).start()

    def finish(unit):
        kind, r, f = unit
        k = plan.turn[unit]
        kids = tree.children(r, f)
        for item in fetches(unit, k):
            local(*item).wait()
        acc, tmp, more = buffer("acc", kind, k), buffer("tmp", kind, k), buffer("more", kind)
        for zz in range(s_.z):
            total = acc[zz].astype(F32) + tmp[zz].astype(F32)
            if kids:
                total = total + more[zz].astype(F32)
            acc[zz] = total.astype(BF16)
        for kid, _ in kids[1:]:
            source = got_grad(kind, kid, f)
            arrived("g" + kind, tree.pos[kid, f], source)
            copy = local(36, source, more)
            copy.start()
            copy.wait()
            for zz in range(s_.z):
                acc[zz] = (acc[zz].astype(F32) + more[zz].astype(F32)).astype(BF16)
        if r:
            send("g" + kind, tree.pos[r, f], acc, got_grad(kind, r, f), peer(1 << tree.parent(r, f)))
        else:
            for step in range(1, s_.z):
                to = lax.rem(z + step, s_.z)
                send("zg" + kind, f * s_.z + step, acc.at[to], z_slot(kind, f, step), z_peer(step))
            local(40 + k, acc.at[z], z_slot(kind, f, 0)).start()

    def act(point):
        for verb, unit in plan.at.get(point, ()):
            (fetch if verb == "fetch" else finish)(unit)

    def loop_point(step, first, stride, offset, count):
        for k in range(count):
            if first + stride * k + offset in plan.at:
                pl.when(step == k)(functools.partial(act, first + stride * k + offset))

    def stage_copies(kind, index, slot):
        own = ref["own_g" + kind].at[index]
        theirs = ref["sib_g" + kind].at[index]
        keep = pltpu.make_async_copy(ref["wa"].at[slot, :, c], own, ref["keep"].at[slot - 2])
        give = pltpu.make_async_remote_copy(
            src_ref=ref["wa"].at[slot, :, 1 - c],
            dst_ref=theirs,
            send_sem=ref["s" + kind + "_s"].at[index],
            recv_sem=ref["s" + kind + "_r"].at[index],
            device_id=sibling,
            device_id_type=MESH,
        )
        return keep, give

    def stage_out(kind, index, slot):
        for copy in stage_copies(kind, index, slot):
            copy.start()

    def stage_kept(kind, index, slot):
        stage_copies(kind, index, slot)[0].wait()

    def stage_free(kind, index, slot):
        stage_copies(kind, index, slot)[1].wait_send()

    fs = s_.fs
    for k in (0, 1):
        take_sibling("m", *tree.units[k])
    weight_load(0, ref["all_m"].at[0]).start()
    gelu_scale = (2.0 / jnp.pi) ** 0.5

    def feed(step, _):
        slot = lax.rem(step, 2)
        weight_load(slot, ref["all_m"].at[step]).wait()

        def rows_of(i, _):
            rows = pl.ds(pl.multiple_of(i * tile, tile), tile)
            up, down = matrix(slot, 0, fs), matrix(slot, fs, fs)
            before = dot(ref["n2"][rows, :], up) + ref["hidden_bias"][step]
            square = before * before
            bent = jnp.tanh(before * (gelu_scale + (gelu_scale * 0.044715) * square))
            share = 0.5 + 0.5 * bent
            hidden = (before * share).astype(BF16)
            slope = share + 0.5 * before * (1.0 - bent * bent) * (
                gelu_scale + (3.0 * gelu_scale * 0.044715) * square
            )
            grad_before = (dot(ref["ct"][rows, :], down) * slope).astype(BF16)
            ref["hid"][rows, :] = hidden
            ref["gb"][rows, :] = grad_before
            ref["facc"][rows, :] = ref["facc"][rows, :] + dot_t(hidden, down)
            ref["gacc"][rows, :] = ref["gacc"][rows, :] + dot_t(grad_before, up)
            ref["hidden_sum"][step] = ref["hidden_sum"][step] + row_sum(grad_before.astype(F32))
            return 0

        lax.fori_loop(0, s_.tiles, rows_of, 0)
        for k in range(1, n_units - 1):
            pl.when(step == k)(functools.partial(take, "m", *tree.units[k + 1]))

        @pl.when(step >= 1)
        def _():
            stage_kept("m", step - 1, 3 - slot)

        loop_point(step, 0, 2, 0, n_units)
        stage = 2 + slot

        @pl.when(step >= 2)
        def _():
            stage_free("m", step - 2, stage)

        def grads(zz, _):
            rows = pl.ds(pl.multiple_of(zz * (2 * s_.tb), 2 * s_.tb), 2 * s_.tb)
            put_rows(stage, zz, 0, dot(ref["n2_t"][rows, :], ref["gb"][...]).astype(BF16))
            put_rows(stage, zz, fs, dot(ref["ct_t"][rows, :], ref["hid"][...]).astype(BF16))
            return 0

        lax.fori_loop(0, s_.z // 2, grads, 0)
        for k in range(n_units - 1):

            def load_next(k=k):
                if k:
                    take_sibling("m", *tree.units[k + 1])
                weight_load((k + 1) % 2, ref["all_m"].at[k + 1]).start()

            pl.when(step == k)(load_next)
        lax.fori_loop(s_.z // 2, s_.z, grads, 0)
        stage_out("m", step, stage)
        loop_point(step, 0, 2, 1, n_units)
        return 0

    lax.fori_loop(0, n_units, feed, 0)

    stage_kept("m", n_units - 1, 2 + (n_units - 1) % 2)
    act(mlp_points)
    weight_load(0, ref["all_a"].at[s_.n_hid - 1]).start()

    def back_two(i, _):
        rows = pl.ds(pl.multiple_of(i * tile, tile), tile)
        residual = ref["res"][rows, :]
        ref["n2"][rows, :] = (residual + (ref["facc"][rows, :] + gain_row(7))).astype(BF16)
        scaled, inverse = scaled_rows(residual)
        grad = ref["gacc"][rows, :]
        add_sum(2, grad * scaled)
        add_sum(3, grad)
        grad = ref["ct"][rows, :].astype(F32) + norm_pull(grad, gain_row(2), scaled, inverse)
        mixed = grad.astype(BF16)
        add_sum(6, mixed.astype(F32))
        ref["facc"][rows, :] = grad
        ref["gacc"][rows, :] = jnp.zeros((tile, s_.d), F32)
        ref["nrm"][rows, :] = mixed
        return 0

    lax.fori_loop(0, s_.tiles, back_two, 0)

    def out_rows(name, j):
        return ref[name].at[columns(j, n)]

    for r in range(1, s_.n_hid):
        j = block_of(r)
        send("lo", r, ref["n2"].at[:, columns(j, kh)], out_rows("layer_out", h), peer(r))
    own_lo = local(0, ref["n2"].at[:, columns(h, kh)], out_rows("layer_out", h))
    own_lo.start()
    for i in range(s_.tiles):
        rows = pl.ds(i * tile, tile)
        ref["n2_t"][:, rows] = ref["nrm"][rows, :].T
    act(mlp_points + 1)
    for k in range(n_units - 2, n_units):
        stage_free("m", k, 2 + k % 2)

    def back_chunk(step, _):
        r = s_.n_hid - 1 - step
        slot = lax.rem(step, 2)
        stage = 2 + slot
        weight_load(slot, ref["all_a"].at[r]).wait()

        @pl.when(step + 1 < s_.n_hid)
        def _():
            weight_load(1 - slot, ref["all_a"].at[lax.rem(2 * s_.n_hid - 2 - step, s_.n_hid)]).start()

        def pull_out(i, _):
            rows = pl.ds(pl.multiple_of(i * tile, tile), tile)
            ref["hid"][rows, pl.ds(0, kh)] = dot(ref["nrm"][rows, :], matrix(slot, 3 * kh, kh)).astype(BF16)
            return 0

        lax.fori_loop(0, s_.tiles, pull_out, 0)

        @pl.when(step >= 1)
        def _():
            stage_kept("a", r + 1, 3 - slot)

        loop_point(step, chunk_points, 4, 0, s_.n_hid)

        def pull_attention(i, _):
            rows = pl.ds(pl.multiple_of(i * BLOCK, BLOCK), BLOCK)
            for p in range(s_.pairs):
                query, key, value = (ref["pj"][r, rows, pl.ds(k * kh + p * PAIR, PAIR)] for k in range(3))
                grad = ref["hid"][rows, pl.ds(p * PAIR, PAIR)]
                attention = ref["probs"][r, p, rows, :]
                weights = attention.astype(F32)
                grad_attention = dot_t(grad, two_heads(value))
                centre = spread(halves(weights * grad_attention, row_add))
                grad_scores = (weights * (grad_attention - centre) * HEAD ** (-0.5)).astype(BF16)
                grad_query = dot(grad_scores, two_heads(key))
                grad_key = pick_heads(dot_l(grad_scores, query))
                grad_value = pick_heads(dot_l(attention, grad))
                for k, values in enumerate((grad_query, grad_key, grad_value)):
                    ref["pj"][r, rows, pl.ds(k * kh + p * PAIR, PAIR)] = values.astype(BF16)
            return 0

        lax.fori_loop(0, s_.blocks, pull_attention, 0)
        loop_point(step, chunk_points, 4, 1, s_.n_hid)

        @pl.when(step >= 2)
        def _():
            stage_free("a", r + 2, stage)

        cols = columns(block_of(r), kh)

        def grads(zz, _):
            rows = pl.ds(pl.multiple_of(zz * (2 * s_.tb), 2 * s_.tb), 2 * s_.tb)
            put_rows(stage, zz, 0, dot(ref["nrm_t"][rows, :], ref["pj"][r]).astype(BF16))
            put_rows(stage, zz, 3 * kh, dot(ref["n2_t"][rows, :], ref["att"][r]).astype(BF16))
            return 0

        lax.fori_loop(0, s_.z, grads, 0)
        stage_out("a", r, stage)
        loop_point(step, chunk_points, 4, 2, s_.n_hid)

        def pull_rows(i, _):
            rows = pl.ds(pl.multiple_of(i * tile, tile), tile)
            grad = ref["pj"][r, rows, :]
            ref["gacc"][rows, :] = ref["gacc"][rows, :] + dot_t(grad, matrix(slot, 0, 3 * kh))
            for k, first in ((4, 0), (5, 2 * kh)):
                part_sum = row_sum(ref["pj"][r, rows, pl.ds(first, kh)].astype(F32))
                ref["sums"][pl.ds(k, 1), cols] = ref["sums"][pl.ds(k, 1), cols] + part_sum
            return 0

        lax.fori_loop(0, s_.tiles, pull_rows, 0)
        loop_point(step, chunk_points, 4, 3, s_.n_hid)
        return 0

    lax.fori_loop(0, s_.n_hid, back_chunk, 0)
    stage_kept("a", 0, 2 + (s_.n_hid - 1) % 2)

    def back_one(i, _):
        rows = pl.ds(pl.multiple_of(i * tile, tile), tile)
        scaled, inverse = scaled_rows(ref["xs"][rows, :].astype(F32))
        grad = ref["gacc"][rows, :]
        add_sum(0, grad * scaled)
        add_sum(1, grad)
        total = ref["facc"][rows, :] + norm_pull(grad, gain_row(0), scaled, inverse)
        ref["ct"][rows, :] = total.astype(BF16)
        return 0

    lax.fori_loop(0, s_.tiles, back_one, 0)
    for k, (r, f) in enumerate(tree.units):
        for i in range(s_.fs // kh):
            ref["sums"][pl.ds(8 + 2 * f + i, 1), columns(block_of(r), kh)] = ref["hidden_sum"][
                k, :, pl.ds(i * kh, kh)
            ]
    for r in range(1, s_.n_hid):
        send("sum1", r, ref["sums"].at[:, columns(block_of(r), kh)], ref["sum1"].at[r], peer(r))
    for r in range(1, s_.n_hid):
        send("gt", r, ref["ct"].at[:, columns(block_of(r), kh)], out_rows("grad_rows", h), peer(r))
    own_gt = local(1, ref["ct"].at[:, columns(h, kh)], out_rows("grad_rows", h))
    own_gt.start()

    total = ref["sums"][:, columns(h, kh)]
    for r in range(1, s_.n_hid):
        arrived("sum1", r, ref["sum1"].at[r])
        total = total + ref["sum1"][r]
    ref["sum2"][0] = total
    send("sum2", 0, ref["sum2"].at[0], ref["sum2"].at[1], sibling)
    for point in range(last_point, plan.end):
        act(point)
    arrived("sum2", 0, ref["sum2"].at[1])
    ref["sum3"][0] = ref["sum2"][0] + ref["sum2"][1]
    for step in range(1, s_.z):
        send("sum3", step, ref["sum3"].at[0], ref["sum3"].at[step], z_peer(step))
    for k in (0, 1):
        free_buffer(k, plan.holders[k])

    finals = [("m", 0), ("m", 1), ("a", 0), ("a", 1)]

    def final_load(k, kind, f):
        return local(30 + k, ref["z_g" + kind].at[f], buffer("acc", kind, k))

    def final_store(k, kind, f):
        if kind == "a":
            source = ref["final"].at[k, pl.ds(0, s_.half)]
            return local(34 + k, source, ref["grad_a"].at[pl.ds(f * s_.half, s_.half)])
        return local(34 + k, ref["final"].at[k], ref["grad_m"].at[f])

    for number, (kind, f) in enumerate(finals):
        k = number % 2
        for step in range(1, s_.z):
            arrived("zg" + kind, f * s_.z + step, z_slot(kind, f, step))
        load = final_load(k, kind, f)
        load.start()
        load.wait()
        total = ref["acc"][k, 0].astype(F32) if kind == "m" else ref["acc"][k, 0, pl.ds(0, s_.half)].astype(F32)
        for step in range(1, s_.z):
            more = ref["acc"][k, step] if kind == "m" else ref["acc"][k, step, pl.ds(0, s_.half)]
            total = total + more.astype(F32)
        if number >= 2:
            final_store(k, *finals[number - 2]).wait()
        if kind == "a":
            ref["final"][k, pl.ds(0, s_.half)] = total
        else:
            ref["final"][k] = total
        final_store(k, kind, f).start()
    total = ref["sum3"][0]
    for step in range(1, s_.z):
        arrived("sum3", step, ref["sum3"].at[step])
        total = total + ref["sum3"][step]
    ref["sum2"][2] = total
    small = local(2, ref["sum2"].at[2], ref["small"])
    small.start()

    small.wait()
    for number in (2, 3):
        final_store(number % 2, *finals[number]).wait()
    own_lo.wait()
    own_gt.wait()
    for r in range(1, s_.n_hid):
        arrived("lo", r, out_rows("layer_out", h))
        arrived("gt", r, out_rows("grad_rows", h))
        left("params", r, ref["params"])
        left("ct", r, cot_rows(h))
        left("lo", r, cot_rows(h))
        left("gt", r, cot_rows(h))
        left("sum1", r, ref["sum1"].at[r])
    left("sum2", 0, ref["sum2"].at[0])
    for step in range(1, s_.z):
        left("sum3", step, ref["sum3"].at[0])
    z_left("za", 0, ref["a_own"])
    for f in (0, 1):
        z_left("zm", f, ref["m_own"].at[f])
    for kind in ("a", "m"):
        for r, f in tree.units:
            source = part[kind](r, f, c)
            left(kind + "c", tree.pos[r, f], source)
            for child, _ in tree.children(r, f):
                left(kind + "x", tree.pos[child, f], source)
    for k in range(max(0, s_.n_hid - 2), s_.n_hid):
        stage_free("a", s_.n_hid - 1 - k, 2 + k % 2)


def scratch(size, tree):
    s_ = size
    units = len(tree.units)
    vmem = {
        "params_all": ((SMALL_ROWS, s_.d), F32),
        "xs": ((s_.n, s_.d), BF16),
        "ct": ((s_.n, s_.d), BF16),
        "nrm": ((s_.n, s_.d), BF16),
        "nrm_t": ((s_.d, s_.n), BF16),
        "n2": ((s_.n, s_.d), BF16),
        "n2_t": ((s_.d, s_.n), BF16),
        "ct_t": ((s_.d, s_.n), BF16),
        "pj": ((s_.n_hid, s_.n, 3 * s_.kh), BF16),
        "probs": ((s_.n_hid, s_.pairs, s_.n, 2 * BLOCK), BF16),
        "att": ((s_.n_hid, s_.n, s_.kh), BF16),
        "res": ((s_.n, s_.d), F32),
        "facc": ((s_.n, s_.d), F32),
        "gacc": ((s_.n, s_.d), F32),
        "wa": ((s_.n_hid, s_.z, 2, s_.tb, s_.wide), BF16),
        "hid": ((s_.n, s_.fs), BF16),
        "gb": ((s_.n, s_.fs), BF16),
        "acc": ((2, s_.z, s_.tb, s_.wide), BF16),
        "tmp": ((2, s_.z, s_.tb, s_.wide), BF16),
        "more": ((s_.z, s_.tb, s_.wide), BF16),
        "final": ((2, s_.tb, s_.wide), F32),
        "hidden_bias": ((units, 1, s_.fs), F32),
        "hidden_sum": ((units, 1, s_.fs), F32),
        "sums": ((SMALL_ROWS, s_.d), F32),
        "sum1": ((s_.n_hid, SMALL_ROWS, s_.kh), F32),
        "sum2": ((3, SMALL_ROWS, s_.kh), F32),
        "sum3": ((s_.z, SMALL_ROWS, s_.kh), F32),
    }
    pairs = {
        "params": s_.n_hid,
        "za": s_.z,
        "zm": 2 * s_.z,
        "xs": s_.tiles * s_.n_hid,
        "ax": units,
        "ac": units,
        "mx": units,
        "mc": units,
        "ct": s_.n_hid,
        "sa": s_.n_hid,
        "sm": units,
        "ga": units,
        "gm": units,
        "zga": 2 * s_.z,
        "zgm": 2 * s_.z,
        "lo": s_.n_hid,
        "gt": s_.n_hid,
        "sum1": s_.n_hid,
        "sum2": 1,
        "sum3": s_.z,
    }
    out = {name: pltpu.VMEM(shape, kind) for name, (shape, kind) in vmem.items()}
    for name, count in pairs.items():
        out[name + "_s"] = pltpu.SemaphoreType.DMA((count,))
        out[name + "_r"] = pltpu.SemaphoreType.DMA((count,))
    out["local"] = pltpu.SemaphoreType.DMA((48,))
    out["wload"] = pltpu.SemaphoreType.DMA((s_.n_hid,))
    out["keep"] = pltpu.SemaphoreType.DMA((2,))
    return out


def finish_kernel(grad_ref, tokens_ref, middle_ref, coarse_ref):
    grad = grad_ref[...]
    rows = grad.shape[0]
    tokens_ref[...] = grad.astype(F32)
    middle_ref[...] = dot(group_matrix(rows, 4), grad)
    coarse_ref[...] = dot(group_matrix(rows, 16), grad)


def finish(grad):
    positions, features = grad.shape
    rows = 256
    return pl.pallas_call(
        finish_kernel,
        grid=(positions // rows,),
        in_specs=[pl.BlockSpec((rows, features), lambda i: (i, 0))],
        out_specs=[pl.BlockSpec((rows // t, features), lambda i: (i, 0)) for t in (1, 4, 16)],
        out_shape=[jax.ShapeDtypeStruct((positions // t, features), F32) for t in (1, 4, 16)],
        name="token_gradients",
    )(grad)


def shards(
    tokens,
    middle_cond,
    coarse_cond,
    first_gain,
    first_shift,
    attend_weight,
    query_bias,
    value_bias,
    output_weight,
    mixer_bias,
    second_gain,
    second_shift,
    up_weight,
    hidden_bias,
    down_weight,
    down_bias,
    cotangent,
):
    positions, features = tokens.shape
    n_hid, n_tok = lax.axis_size("hid"), lax.axis_size("tok")
    d = features * n_hid
    ff = up_weight.shape[1] * n_hid
    size = Sizes(positions, features, d, ff, n_tok, n_hid)
    tree = Tree(n_hid)
    tb, fs, wide, z = size.tb, size.fs, size.wide, size.z
    a_own = jnp.concatenate([attend_weight.reshape(tb, 3 * features), output_weight.T], axis=1)
    m_own = jnp.stack(
        [
            jnp.concatenate([up_weight[:, f * fs : f * fs + fs], down_weight[f * fs : f * fs + fs].T], axis=1)
            for f in (0, 1)
        ]
    )
    vectors = (first_gain, first_shift, second_gain, second_shift, query_bias, value_bias, mixer_bias, down_bias)
    params = jnp.concatenate(
        [
            jnp.stack(vectors),
            hidden_bias.reshape(ff // d, features),
            jnp.zeros((SMALL_ROWS - 8 - ff // d, features), F32),
        ]
    )
    units = len(tree.units)
    outputs = {
        "layer_out": ((positions, features), BF16),
        "grad_rows": ((positions, features), BF16),
        "grad_a": ((tb, wide), F32),
        "grad_m": ((2, tb, wide), F32),
        "small": ((SMALL_ROWS, features), F32),
        "all_a": ((n_hid, z, 2, tb, wide), BF16),
        "all_m": ((units, z, 2, tb, wide), BF16),
        "own_ga": ((n_hid, z, tb, wide), BF16),
        "sib_ga": ((n_hid, z, tb, wide), BF16),
        "got_ga": ((units, z, size.half, wide), BF16),
        "own_gm": ((units, z, tb, wide), BF16),
        "sib_gm": ((units, z, tb, wide), BF16),
        "got_gm": ((units, z, tb, wide), BF16),
        "z_ga": ((2, z, size.half, wide), BF16),
        "z_gm": ((2, z, tb, wide), BF16),
    }
    hbm = pl.BlockSpec(memory_space=pltpu.HBM)
    results = pl.pallas_call(
        functools.partial(layer_kernel, size, tree),
        out_shape=[jax.ShapeDtypeStruct(*outputs[name]) for name in OUTPUTS],
        in_specs=[hbm] * len(INPUTS),
        out_specs=[hbm] * len(OUTPUTS),
        scratch_shapes=list(scratch(size, tree).values()),
        compiler_params=pltpu.CompilerParams(
            collective_id=0, has_side_effects=True, vmem_limit_bytes=62 * 2**20
        ),
        cost_estimate=pl.CostEstimate(flops=80 * 10**9, bytes_accessed=2 * 10**8, transcendentals=10**7),
        name="layer",
    )(tokens, middle_cond, coarse_cond, cotangent, a_own, m_own, params)
    layer_out, grad_rows, grad_a, grad_m, small = results[:5]
    grad_tokens, grad_middle, grad_coarse = finish(grad_rows)
    tok = lax.axis_index("tok")
    share = features // n_tok
    mine = lax.dynamic_slice_in_dim(small[:8], tok * share, share, 1)
    hidden_share = fs * 2 // n_tok
    grad_hidden_bias = lax.dynamic_slice_in_dim(
        small[8 : 8 + ff // d].reshape(-1), tok * hidden_share, hidden_share, 0
    )
    grad_up = jnp.concatenate([grad_m[0, :, :fs], grad_m[1, :, :fs]], axis=1)
    grad_down = jnp.concatenate([grad_m[0, :, fs:].T, grad_m[1, :, fs:].T], axis=0)
    return (
        layer_out,
        grad_tokens,
        grad_middle,
        grad_coarse,
        mine[0],
        mine[1],
        grad_a[:, : 3 * features].reshape(tb, 3, features),
        mine[4],
        mine[5],
        grad_a[:, 3 * features :].T,
        mine[6],
        mine[2],
        mine[3],
        grad_up,
        grad_hidden_bias,
        grad_down,
        mine[7],
    )


def solution(mesh):
    return jax.shard_map(
        shards,
        mesh=mesh,
        in_specs=(
            P("tok", "hid"),
            P("tok", "hid"),
            P("tok", "hid"),
            P("hid"),
            P("hid"),
            P("tok", None, "hid"),
            P("hid"),
            P("hid"),
            P("hid", "tok"),
            P("hid"),
            P("hid"),
            P("hid"),
            P("tok", "hid"),
            P("hid"),
            P("hid", "tok"),
            P("hid"),
            P("tok", "hid"),
        ),
        out_specs=(
            P("tok", "hid"),
            P("tok", "hid"),
            P("tok", "hid"),
            P("tok", "hid"),
            P(("hid", "tok")),
            P(("hid", "tok")),
            P("tok", None, "hid"),
            P(("hid", "tok")),
            P(("hid", "tok")),
            P("hid", "tok"),
            P(("hid", "tok")),
            P(("hid", "tok")),
            P(("hid", "tok")),
            P("tok", "hid"),
            P(("hid", "tok")),
            P("hid", "tok"),
            P(("hid", "tok")),
        ),
        check_vma=False,
    )
```

time: 1440 us -> 461 us (0.32)
  waiting for transfers between devices: 912 us -> 0 us
  Pallas kernels: 0 us -> 442 us
  matrix products: 209 us -> 0 us
  local copies, waits for them, and re-layouts: 137 us -> 13.5 us
  blocking collectives: 89.6 us -> 0 us
  other arithmetic: 62.6 us -> 2.5 us
  between operations: 15.4 us -> 0.92 us
    reduce_scatter x6 -> x0, waiting for transfers between devices: 597 us -> none  [the longest x3 432 us: feature_share(): lax.psum_scatter(partial_value, 'hid', scatter_dimension=1, tiled=True)]
    pallas_call x0 -> x2, Pallas kernels: none -> 442 us  [the longest x1 432 us: shards(): pl.pallas_call(functools.partial(layer_kernel, size, tree), out_shape=[ja...]
    all_gather x7 -> x0, waiting for transfers between devices: 306 us -> none  [the longest x4 284 us: full_features(): return lax.all_gather(values, 'hid', axis=1, tiled=True)]
    dot_general x18 -> x0, matrix products: 209 us -> none  [the longest x1 24 us: shards(): jnp.einsum('td,fd->tf', upstream_full, down_full, preferred_element_type=...]
    another operation x23 -> x0, local copies, waits for them, and re-layouts: 79.8 us -> none  [the longest x7 42.5 us: attend_backward(): return jnp.stack(pieces, axis=1).astype(jnp.bfloat16)]
    psum x4 -> x0, blocking collectives: 62.1 us -> none  [the longest x2 31.9 us: norm_forward(): lax.psum((jnp.sum(summed, axis=1), jnp.sum(summed * summed, axis=1)), 'hid')]
    reduce_sum x8 -> x0, other arithmetic: 49.1 us -> none  [the longest x2 12.2 us: norm_forward(): jnp.sum(summed, axis=1)]
    add x5 -> x0, local copies, waits for them, and re-layouts: 17.9 us -> none  [shards(): tokens.astype(jnp.float32).reshape(positions // 16, 4, 4, features)]
  transfers between devices with their start and end apart: 16 -> 0, of which waited for: 12 -> 0; matrix products, arithmetic and copies ran while one was open for 22% -> 0% of each run, Pallas kernels for 0% -> 0%
where the time goes in v2:
time: 461 us; the launch traced here: 459 us
  Pallas kernels  442 us (96%)
  local copies, waits for them, and re-layouts  13.5 us (3%)
    pallas_call x1, Pallas kernels, shards(): pl.pallas_call(functools.partial(layer_kernel, size, tree), out_shape=[ja...  432 us
    pallas_call x1, Pallas kernels, finish(): pl.pallas_call(finish_kernel, grid=(positions // rows,), in_specs=[pl.Blo...  10.3 us

profile of v2, /device:TPU:8, one launch (start us, length us, event | category | flops | bytes accessed | tf_op | source)
XLA Modules:
  0.0 458.9 jit_solution(8029557041287460129)
XLA Ops:
  0.8 1.1 fusion.1
  1.8 0.1 copy.50
  1.9 0.1 copy.51
  2.1 1.0 fusion
  3.1 0.8 pad_maximum_fusion.refs_5_
  4.0 1.1 copy.41
  5.1 0.2 copy.43
  5.2 0.1 copy.42
  5.3 0.7 pad_maximum_fusion.3.refs_4_
  6.2 1.2 concatenate.21.refs_6_
  7.4 431.7 %layer.1 = (bf16[4096,256]{1,0:T(8,128)(2,1)}, bf16[4096,256]{1,0:T(8,128)(2,1)}, f32[128,1024]{1,0:T(8,128)}, f32[2,128,1024]{2,1,0:T(8,128)}, f32[16,256]{1,0:...) custom-call(bf16[4096,256]{1,0:T(8,128)(2,1)} %refs_0_.1, ...), custom_call_target="tpu_custom_call" | custom-call | flops 80000000000 | bytes 200000000 | tf_op jit(solution)/shard_map/layer/pallas_call | solution.py:1024
  439.1 1.3 slice_bitcast_fusion.1
  440.5 1.0 copy.49
  441.5 0.8 pad_maximum_fusion.1
  442.3 0.1 constant_dynamic-slice_fusion
  442.4 0.5 slice_bitcast_fusion.6
  443.0 0.6 dynamic_slice.7
  443.5 10.3 %token_gradients.1 = (f32[4096,256]{1,0:T(8,128)}, f32[1024,256]{1,0:T(8,128)}, f32[256,256]{1,0:T(8,128)}) custom-call(bf16[4096,256]{1,0:T(8,128)(2,1)} %get-tuple-element.26.grad_ref), custom_call_target="tpu_custom_call" | custom-call | tf_op jit(solution)/shard_map/token_gradients/pallas_call | solution.py:954
  453.8 1.0 slice.67
  454.9 0.2 copy.46
  455.0 0.9 copy.47
  455.9 0.9 slice_bitcast_fusion.4
  456.9 0.8 copy.48
  457.6 1.3 copy.54
  (31 shorter events, 0.2 us)
Async XLA Ops:
  0.7 4.5 copy-start.1
  0.7 5.4 %copy-start.3 = (f32[1024]{0:T(1024)S(1)}, f32[1024]{0:T(1024)}, u32[]{:S(2)}) copy-start(f32[1024]{0:T(1024)} %param.30) | copy-start | bytes 12292
  0.7 5.4 %copy-start.8 = (f32[256]{0:T(256)S(1)}, f32[256]{0:T(256)}, u32[]{:S(2)}) copy-start(f32[256]{0:T(256)} %param.23) | copy-start | bytes 3076
  0.7 5.4 %copy-start.9 = (f32[256]{0:T(256)S(1)}, f32[256]{0:T(256)}, u32[]{:S(2)}) copy-start(f32[256]{0:T(256)} %param.24) | copy-start | bytes 3076
  0.7 5.4 %copy-start.10 = (f32[256]{0:T(256)S(1)}, f32[256]{0:T(256)}, u32[]{:S(2)}) copy-start(f32[256]{0:T(256)} %param.26) | copy-start | bytes 3076
  0.7 5.4 %copy-start.11 = (f32[256]{0:T(256)S(1)}, f32[256]{0:T(256)}, u32[]{:S(2)}) copy-start(f32[256]{0:T(256)} %param.32) | copy-start | bytes 3076
  0.7 5.4 %copy-start.4 = (f32[256]{0:T(256)S(1)}, f32[256]{0:T(256)}, u32[]{:S(2)}) copy-start(f32[256]{0:T(256)} %param.20) | copy-start | bytes 3076
  0.7 5.4 %copy-start.5 = (f32[256]{0:T(256)S(1)}, f32[256]{0:T(256)}, u32[]{:S(2)}) copy-start(f32[256]{0:T(256)} %param.21) | copy-start | bytes 3076
  0.7 5.4 %copy-start.6 = (f32[256]{0:T(256)S(1)}, f32[256]{0:T(256)}, u32[]{:S(2)}) copy-start(f32[256]{0:T(256)} %param.27) | copy-start | bytes 3076
  0.8 5.4 %copy-start.7 = (f32[256]{0:T(256)S(1)}, f32[256]{0:T(256)}, u32[]{:S(2)}) copy-start(f32[256]{0:T(256)} %param.28) | copy-start | bytes 3076
  439.1 3.2 copy-start.2
  440.4 17.2 %copy-start = (bf16[4096,256]{1,0:T(8,128)(2,1)S(1)}, bf16[4096,256]{1,0:T(8,128)(2,1)}, u32[]{:S(2)}) copy-start(bf16[4096,256]{1,0:T(8,128)(2,1)} %get-tuple-element.102) | copy-start | bytes 6291460

commit v3 on v2

--- a/solution.py
+++ b/solution.py
@@ -24,6 +24,13 @@
         units = [(r, f) for r in range(n_hid) for f in (0, 1)]
         self.units = sorted(units, key=lambda u: (u[0].bit_count(), len(self.children(*u)), u))
         self.pos = {u: k for k, u in enumerate(self.units)}
+        self.near = [1 << b for b in range(self.bits)]
+        self.far = [r for r in range(n_hid) if r.bit_count() > 1]
+        first = [(1 << b, b % 2) for b in range(self.bits)]
+        second = [(1 << b, 1 - b % 2) for b in range(self.bits)]
+        self.m_near = first + second
+        self.m_units = [(0, 0), (0, 1)] + first + [(r, f) for r in self.far for f in (0, 1)] + second
+        self.m_pos = {u: k for k, u in enumerate(self.m_units)}
 
     def children(self, r, f):
         held = [b for b in range(self.bits) if r >> b & 1]
@@ -38,12 +45,13 @@
 
 
 class Schedule:
-    def __init__(self, tree, done, weights_lag, last_point):
+    def __init__(self, done, kids, lag, last_point):
         self.at = {}
         self.turn = {}
         self.before = {}
         self.first = set()
         sent = {}
+        seen = set()
         holders = [None, None]
         waiting = sorted(done, key=lambda u: done[u])
         held = None
@@ -55,19 +63,18 @@
                 sent[held] = point
                 held = None
             for unit in waiting:
-                kind, r, f = unit
-                kids = [(kind, k, f) for k, _ in tree.children(r, f)]
-                if point <= done[unit] or any(k not in sent for k in kids):
+                if point <= done[unit] or any(k not in sent for k in kids[unit]):
                     continue
-                if point < last_point and any(point < sent[k] + weights_lag[kind] for k in kids):
+                if point < last_point and any(point < sent[k] + lag[unit[0]] for k in kids[unit]):
                     continue
                 actions.append(("fetch", unit))
                 held = unit
                 self.turn[unit] = k = len(self.turn) % 2
                 self.before[unit] = holders[k]
-                if (kind, r) not in {(other[0], other[1]) for other in self.turn if other != unit}:
+                holders[k] = unit
+                if unit[:2] not in seen:
                     self.first.add(unit)
-                holders[k] = unit
+                seen.add(unit[:2])
                 waiting.remove(unit)
                 break
             if actions:
@@ -149,6 +156,7 @@
     "got_gm",
     "z_ga",
     "z_gm",
+    "z_far",
 )
 
 
@@ -239,7 +247,7 @@
         return ref["all_a"].at[r, :, core, pl.ds(f * s_.half, s_.half)]
 
     def m_part(r, f, core):
-        return ref["all_m"].at[tree.pos[r, f], :, core]
+        return ref["all_m"].at[tree.m_pos[r, f], :, core]
 
     part = {"a": a_part, "m": m_part}
 
@@ -253,8 +261,15 @@
     own_a.start()
     own_m = []
     for f in (0, 1):
-        own_m.append(local(2 + f, ref["m_own"].at[f], ref["all_m"].at[tree.pos[0, f], z, c]))
+        own_m.append(local(2 + f, ref["m_own"].at[f], ref["all_m"].at[tree.m_pos[0, f], z, c]))
         own_m[f].start()
+
+    def m_block(r, f):
+        return ref["all_m"].at[tree.m_pos[r, f], z, c]
+
+    far_units = [(r, f) for r in tree.far for f in (0, 1)]
+    for r, f in far_units:
+        send("fs", tree.m_pos[r, f], ref["m_own"].at[f], m_block(r, f), peer(r))
 
     kh, n, tile = s_.kh, s_.n, s_.tile
     rows_m, rows_c = n // 4, n // 16
@@ -296,25 +311,39 @@
                 own_xs.append(copy)
 
     for f in (0, 1):
-        z_send("zm", f, ref["m_own"].at[f], ref["all_m"].at[tree.pos[0, f], z, c])
-
-    def pass_on(kind, r, f):
-        k = tree.pos[r, f]
+        z_send("zm", f, ref["m_own"].at[f], m_block(0, f))
+    for r, f in far_units:
+        arrived("fs", tree.m_pos[r, f], m_block(r, f))
+        z_send("zf", tree.m_pos[r, f], m_block(r, f), m_block(r, f))
+
+    def to_sibling(kind, r, f):
+        k = tree.pos[r, f] if kind == "a" else tree.m_pos[r, f]
+        send(kind + "c", k, part[kind](r, f, c), part[kind](r, f, c), sibling)
+
+    def take_a(r, f):
+        arrived("ax", tree.pos[r, f], a_part(r, f, c))
         for child, b in tree.children(r, f):
-            send(kind + "x", tree.pos[child, f], part[kind](r, f, c), part[kind](child, f, c), peer(1 << b))
-        send(kind + "c", k, part[kind](r, f, c), part[kind](r, f, c), sibling)
-
-    def take(kind, r, f):
-        arrived(kind + "x", tree.pos[r, f], part[kind](r, f, c))
-        pass_on(kind, r, f)
+            send("ax", tree.pos[child, f], a_part(r, f, c), a_part(child, f, c), peer(1 << b))
+        to_sibling("a", r, f)
+
+    def take_m(r, f):
+        if r in tree.far:
+            z_arrived("zf", tree.m_pos[r, f], m_block(r, f))
+        else:
+            arrived("mx", tree.m_pos[r, f], m_part(r, f, c))
+        to_sibling("m", r, f)
 
     def take_sibling(kind, r, f):
-        arrived(kind + "c", tree.pos[r, f], part[kind](r, f, 1 - c))
-
+        k = tree.pos[r, f] if kind == "a" else tree.m_pos[r, f]
+        arrived(kind + "c", k, part[kind](r, f, 1 - c))
+
+    a_near = sorted([u for u in tree.units if u[0] in tree.near], key=lambda u: -len(tree.children(*u)))
     own_a.wait()
     z_arrived("za", 0, ref["all_a"].at[0, z, c])
+    for r, f in a_near:
+        send("ax", tree.pos[r, f], a_part(0, f, c), a_part(r, f, c), peer(r))
     for f in (0, 1):
-        pass_on("a", 0, f)
+        to_sibling("a", 0, f)
 
     own_params.wait()
     for r in range(1, s_.n_hid):
@@ -323,7 +352,7 @@
     def gain_row(k):
         return ref["params_all"][pl.ds(k, 1), :]
 
-    for k, (r, f) in enumerate(tree.units):
+    for k, (r, f) in enumerate(tree.m_units):
         parts = [
             ref["params_all"][pl.ds(8 + 2 * f + i, 1), columns(block_of(r), kh)] for i in range(s_.fs // kh)
         ]
@@ -368,21 +397,22 @@
             pass
         elif r.bit_count() == 1:
             if r == 1:
-                for u, f in tree.units:
-                    if u.bit_count() == 1:
-                        take("a", u, f)
+                for u, f in a_near:
+                    take_a(u, f)
                 own_ct.start()
                 for k in range(1, s_.n_hid):
                     send("ct", k, ref["cotangent"].at[columns(block_of(k), n)], cot_rows(h), peer(k))
         else:
             for f in (0, 1):
-                take("a", r, f)
+                take_a(r, f)
         if r == s_.n_hid - 1:
             for f in (0, 1):
                 own_m[f].wait()
-                z_arrived("zm", f, ref["all_m"].at[tree.pos[0, f], z, c])
+                z_arrived("zm", f, m_block(0, f))
+            for u, f in tree.m_near:
+                send("mx", tree.m_pos[u, f], m_part(0, f, c), m_part(u, f, c), peer(u))
             for f in (0, 1):
-                pass_on("m", 0, f)
+                to_sibling("m", 0, f)
         for f in (0, 1):
             take_sibling("a", r, f)
         load = weight_load(r, ref["all_a"].at[r])
@@ -466,100 +496,129 @@
     mlp_points = 2 * n_units
     chunk_points = mlp_points + 2
     last_point = chunk_points + 4 * s_.n_hid
-    done = {("m", r, f): 2 * k + 1 for k, (r, f) in enumerate(tree.units)}
+    done, kids = {}, {}
+    for k, (r, f) in enumerate(tree.m_units):
+        done["m", r, f] = 2 * k + 1
+        kids["m", r, f] = [("m", u, f) for u in tree.near] if r == 0 else []
+    for r, f in far_units:
+        done["fold", r, f] = 0
+        kids["fold", r, f] = [("m", r, f)]
     for r in range(s_.n_hid):
         for f in (0, 1):
             done["a", r, f] = chunk_points + 4 * (s_.n_hid - 1 - r) + 3
-    plan = Schedule(tree, done, {"m": 6, "a": 4}, last_point)
+            kids["a", r, f] = [("a", child, f) for child, _ in tree.children(r, f)]
+    plan = Schedule(done, kids, {"m": 6, "a": 4, "fold": 9}, last_point)
+
+    def place(kind, r, f):
+        return tree.pos[r, f] if kind == "a" else tree.m_pos[r, f]
 
     def own_grad(kind, r, f):
         if kind == "a":
             return ref["own_ga"].at[r, :, pl.ds(f * s_.half, s_.half)]
-        return ref["own_gm"].at[tree.pos[r, f]]
+        return ref["own_gm"].at[tree.m_pos[r, f]]
 
     def sib_grad(kind, r, f):
         if kind == "a":
             return ref["sib_ga"].at[r, :, pl.ds(f * s_.half, s_.half)]
-        return ref["sib_gm"].at[tree.pos[r, f]]
+        return ref["sib_gm"].at[tree.m_pos[r, f]]
 
     def got_grad(kind, r, f):
-        if kind == "a":
-            return ref["got_ga"].at[tree.pos[r, f]]
-        return ref["got_gm"].at[tree.pos[r, f]]
+        return ref["got_g" + kind].at[place(kind, r, f)]
 
     def buffer(name, kind, k=None):
         whole = ref[name] if k is None else ref[name].at[k]
-        return whole.at[:, pl.ds(0, s_.half)] if kind == "a" else whole
-
-    def z_name(kind):
-        return ("zga", 0) if kind == "a" else ("zgm", 1)
+        return whole.at[pl.ds(0, s_.z), pl.ds(0, s_.half if kind == "a" else s_.tb)]
 
     def z_slot(kind, f, step):
-        if kind == "a":
-            return ref["z_ga"].at[f, step]
-        return ref["z_gm"].at[f, step]
+        return ref["z_g" + kind].at[f, step]
+
+    def scattered(kind, r, f):
+        if r == 0:
+            return "zg" + kind, f * s_.z, ref["z_g" + kind].at[f]
+        return "zfar", tree.m_pos[r, f] * s_.z, ref["z_far"].at[tree.m_pos[r, f]]
+
+    def scatters(kind, r):
+        return r == 0 or (kind == "m" and r in tree.far)
 
     def free_buffer(k, holder):
         if holder is None:
             return
         kind, r, f = holder
         source = buffer("acc", kind, k)
-        if r:
-            left("g" + kind, tree.pos[r, f], source)
+        if kind == "fold":
+            left("fold", tree.m_pos[r, f], source.at[0])
+        elif scatters(kind, r):
+            name, first, _ = scattered(kind, r, f)
+            for step in range(1, s_.z):
+                left(name, first + step, source.at[0])
         else:
-            for step in range(1, s_.z):
-                left("zg" + kind, f * s_.z + step, source.at[0])
-            local(40 + k, source.at[0], source.at[0]).wait()
+            left("g" + kind, place(kind, r, f), source)
 
     def fetches(unit, k):
         kind, r, f = unit
-        kids = tree.children(r, f)
+        if kind == "fold":
+            return [(30 + 3 * k, ref["z_far"].at[tree.m_pos[r, f]], buffer("acc", kind, k))]
         out = [(30 + 3 * k, own_grad(*unit), buffer("acc", kind, k))]
         out.append((31 + 3 * k, sib_grad(*unit), buffer("tmp", kind, k)))
-        if kids:
-            out.append((32 + 3 * k, got_grad(kind, kids[0][0], f), buffer("more", kind)))
+        if kids[unit]:
+            out.append((32 + 3 * k, got_grad(*kids[unit][0]), buffer("more", kind)))
         return out
 
     def fetch(unit):
         kind, r, f = unit
         k = plan.turn[unit]
         free_buffer(k, plan.before[unit])
-        if kind == "m" or unit in plan.first:
-            slot = tree.pos[r, f] if kind == "m" else r
-            whole = ref["sib_gm"].at[slot] if kind == "m" else ref["sib_ga"].at[r]
-            arrived("s" + kind, slot, whole)
-        for kid, _ in tree.children(r, f)[:1]:
-            arrived("g" + kind, tree.pos[kid, f], got_grad(kind, kid, f))
+        if kind == "fold":
+            for step in range(1, s_.z):
+                name, first, slots = scattered("m", r, f)
+                arrived(name, first + step, slots.at[step])
+        elif kind == "m" or unit in plan.first:
+            slot = tree.m_pos[r, f] if kind == "m" else r
+            arrived("s" + kind, slot, ref["sib_g" + kind].at[slot])
+        if kind != "fold":
+            for kid in kids[unit][:1]:
+                arrived("g" + kind, place(*kid), got_grad(*kid))
         for item in fetches(unit, k):
             local(*item).start()
 
     def finish(unit):
         kind, r, f = unit
         k = plan.turn[unit]
-        kids = tree.children(r, f)
         for item in fetches(unit, k):
             local(*item).wait()
         acc, tmp, more = buffer("acc", kind, k), buffer("tmp", kind, k), buffer("more", kind)
+        if kind == "fold":
+            total = acc[0].astype(F32)
+            for zz in range(1, s_.z):
+                total = total + acc[zz].astype(F32)
+            acc[0] = total.astype(BF16)
+            slot = ref["z_gm"].at[f, s_.z + tree.far.index(r)]
+            send("fold", tree.m_pos[r, f], acc.at[0], slot, peer(r))
+            return
         for zz in range(s_.z):
             total = acc[zz].astype(F32) + tmp[zz].astype(F32)
-            if kids:
+            if kids[unit]:
                 total = total + more[zz].astype(F32)
             acc[zz] = total.astype(BF16)
-        for kid, _ in kids[1:]:
-            source = got_grad(kind, kid, f)
-            arrived("g" + kind, tree.pos[kid, f], source)
+        for kid in kids[unit][1:]:
+            source = got_grad(*kid)
+            arrived("g" + kind, place(*kid), source)
             copy = local(36, source, more)
             copy.start()
             copy.wait()
             for zz in range(s_.z):
                 acc[zz] = (acc[zz].astype(F32) + more[zz].astype(F32)).astype(BF16)
-        if r:
-            send("g" + kind, tree.pos[r, f], acc, got_grad(kind, r, f), peer(1 << tree.parent(r, f)))
-        else:
+        if scatters(kind, r):
+            name, first, slots = scattered(kind, r, f)
+            keep = local(40, acc.at[z], slots.at[0])
+            keep.start()
             for step in range(1, s_.z):
                 to = lax.rem(z + step, s_.z)
-                send("zg" + kind, f * s_.z + step, acc.at[to], z_slot(kind, f, step), z_peer(step))
-            local(40 + k, acc.at[z], z_slot(kind, f, 0)).start()
+                send(name, first + step, acc.at[to], slots.at[step], z_peer(step))
+            keep.wait()
+        else:
+            to = r if kind == "m" else 1 << tree.parent(r, f)
+            send("g" + kind, place(kind, r, f), acc, got_grad(kind, r, f), peer(to))
 
     def act(point):
         for verb, unit in plan.at.get(point, ()):
@@ -596,7 +655,7 @@
 
     fs = s_.fs
     for k in (0, 1):
-        take_sibling("m", *tree.units[k])
+        take_sibling("m", *tree.m_units[k])
     weight_load(0, ref["all_m"].at[0]).start()
     gelu_scale = (2.0 / jnp.pi) ** 0.5
 
@@ -625,7 +684,7 @@
 
         lax.fori_loop(0, s_.tiles, rows_of, 0)
         for k in range(1, n_units - 1):
-            pl.when(step == k)(functools.partial(take, "m", *tree.units[k + 1]))
+            pl.when(step == k)(functools.partial(take_m, *tree.m_units[k + 1]))
 
         @pl.when(step >= 1)
         def _():
@@ -649,7 +708,7 @@
 
             def load_next(k=k):
                 if k:
-                    take_sibling("m", *tree.units[k + 1])
+                    take_sibling("m", *tree.m_units[k + 1])
                 weight_load((k + 1) % 2, ref["all_m"].at[k + 1]).start()
 
             pl.when(step == k)(load_next)
@@ -685,15 +744,15 @@
     def out_rows(name, j):
         return ref[name].at[columns(j, n)]
 
+    for i in range(s_.tiles):
+        rows = pl.ds(i * tile, tile)
+        ref["n2_t"][:, rows] = ref["nrm"][rows, :].T
+    act(mlp_points + 1)
     for r in range(1, s_.n_hid):
         j = block_of(r)
         send("lo", r, ref["n2"].at[:, columns(j, kh)], out_rows("layer_out", h), peer(r))
     own_lo = local(0, ref["n2"].at[:, columns(h, kh)], out_rows("layer_out", h))
     own_lo.start()
-    for i in range(s_.tiles):
-        rows = pl.ds(i * tile, tile)
-        ref["n2_t"][:, rows] = ref["nrm"][rows, :].T
-    act(mlp_points + 1)
     for k in range(n_units - 2, n_units):
         stage_free("m", k, 2 + k % 2)
 
@@ -783,17 +842,19 @@
         return 0
 
     lax.fori_loop(0, s_.tiles, back_one, 0)
-    for k, (r, f) in enumerate(tree.units):
+    for k, (r, f) in enumerate(tree.m_units):
         for i in range(s_.fs // kh):
             ref["sums"][pl.ds(8 + 2 * f + i, 1), columns(block_of(r), kh)] = ref["hidden_sum"][
                 k, :, pl.ds(i * kh, kh)
             ]
     for r in range(1, s_.n_hid):
         send("sum1", r, ref["sums"].at[:, columns(block_of(r), kh)], ref["sum1"].at[r], peer(r))
-    for r in range(1, s_.n_hid):
-        send("gt", r, ref["ct"].at[:, columns(block_of(r), kh)], out_rows("grad_rows", h), peer(r))
     own_gt = local(1, ref["ct"].at[:, columns(h, kh)], out_rows("grad_rows", h))
     own_gt.start()
+
+    def send_rows():
+        for r in range(1, s_.n_hid):
+            send("gt", r, ref["ct"].at[:, columns(block_of(r), kh)], out_rows("grad_rows", h), peer(r))
 
     total = ref["sums"][:, columns(h, kh)]
     for r in range(1, s_.n_hid):
@@ -801,8 +862,14 @@
         total = total + ref["sum1"][r]
     ref["sum2"][0] = total
     send("sum2", 0, ref["sum2"].at[0], ref["sum2"].at[1], sibling)
+    rows_sent = False
     for point in range(last_point, plan.end):
+        if not rows_sent and any(verb == "fetch" and unit[:2] == ("a", 0) for verb, unit in plan.at.get(point, ())):
+            send_rows()
+            rows_sent = True
         act(point)
+    if not rows_sent:
+        send_rows()
     arrived("sum2", 0, ref["sum2"].at[1])
     ref["sum3"][0] = ref["sum2"][0] + ref["sum2"][1]
     for step in range(1, s_.z):
@@ -813,7 +880,10 @@
     finals = [("m", 0), ("m", 1), ("a", 0), ("a", 1)]
 
     def final_load(k, kind, f):
-        return local(30 + k, ref["z_g" + kind].at[f], buffer("acc", kind, k))
+        slots = ref["z_g" + kind].at[f]
+        if kind == "a":
+            return local(30 + k, slots, ref["acc"].at[k, pl.ds(0, s_.z), pl.ds(0, s_.half)])
+        return local(30 + k, slots, ref["acc"].at[k])
 
     def final_store(k, kind, f):
         if kind == "a":
@@ -825,11 +895,14 @@
         k = number % 2
         for step in range(1, s_.z):
             arrived("zg" + kind, f * s_.z + step, z_slot(kind, f, step))
+        if kind == "m":
+            for i, r in enumerate(tree.far):
+                arrived("fold", tree.m_pos[r, f], z_slot(kind, f, s_.z + i))
         load = final_load(k, kind, f)
         load.start()
         load.wait()
         total = ref["acc"][k, 0].astype(F32) if kind == "m" else ref["acc"][k, 0, pl.ds(0, s_.half)].astype(F32)
-        for step in range(1, s_.z):
+        for step in range(1, s_.z + (len(tree.far) if kind == "m" else 0)):
             more = ref["acc"][k, step] if kind == "m" else ref["acc"][k, step, pl.ds(0, s_.half)]
             total = total + more.astype(F32)
         if number >= 2:
@@ -866,12 +939,17 @@
     z_left("za", 0, ref["a_own"])
     for f in (0, 1):
         z_left("zm", f, ref["m_own"].at[f])
-    for kind in ("a", "m"):
-        for r, f in tree.units:
-            source = part[kind](r, f, c)
-            left(kind + "c", tree.pos[r, f], source)
-            for child, _ in tree.children(r, f):
-                left(kind + "x", tree.pos[child, f], source)
+    for r, f in tree.units:
+        left("ac", tree.pos[r, f], a_part(r, f, c))
+        if r:
+            left("ax", tree.pos[r, f], a_part(r, f, c))
+    for r, f in tree.m_units:
+        left("mc", tree.m_pos[r, f], m_part(r, f, c))
+    for r, f in tree.m_near:
+        left("mx", tree.m_pos[r, f], m_part(r, f, c))
+    for r, f in far_units:
+        left("fs", tree.m_pos[r, f], m_block(r, f))
+        z_left("zf", tree.m_pos[r, f], m_block(r, f))
     for k in range(max(0, s_.n_hid - 2), s_.n_hid):
         stage_free("a", s_.n_hid - 1 - k, 2 + k % 2)
 
@@ -897,7 +975,7 @@
         "wa": ((s_.n_hid, s_.z, 2, s_.tb, s_.wide), BF16),
         "hid": ((s_.n, s_.fs), BF16),
         "gb": ((s_.n, s_.fs), BF16),
-        "acc": ((2, s_.z, s_.tb, s_.wide), BF16),
+        "acc": ((2, s_.z + len(tree.far), s_.tb, s_.wide), BF16),
         "tmp": ((2, s_.z, s_.tb, s_.wide), BF16),
         "more": ((s_.z, s_.tb, s_.wide), BF16),
         "final": ((2, s_.tb, s_.wide), F32),
@@ -922,6 +1000,10 @@
         "sm": units,
         "ga": units,
         "gm": units,
+        "fs": units,
+        "zf": units * s_.z,
+        "zfar": units * s_.z,
+        "fold": units,
         "zga": 2 * s_.z,
         "zgm": 2 * s_.z,
         "lo": s_.n_hid,
@@ -940,25 +1022,45 @@
     return out
 
 
-def finish_kernel(grad_ref, tokens_ref, middle_ref, coarse_ref):
+def finish_kernel(kh, fs, grad_ref, a_ref, m_ref, tokens_ref, middle_ref, coarse_ref, output_ref, up_ref, down_ref):
     grad = grad_ref[...]
     rows = grad.shape[0]
+    part = min(512, rows)
+    by_4, by_16 = group_matrix(part, 4), group_matrix(part, 16)
     tokens_ref[...] = grad.astype(F32)
-    middle_ref[...] = dot(group_matrix(rows, 4), grad)
-    coarse_ref[...] = dot(group_matrix(rows, 16), grad)
-
-
-def finish(grad):
+    for i in range(rows // part):
+        piece = grad[i * part : i * part + part]
+        middle_ref[pl.ds(i * part // 4, part // 4), :] = dot(by_4, piece)
+        coarse_ref[pl.ds(i * part // 16, part // 16), :] = dot(by_16, piece)
+
+    @pl.when(pl.program_id(0) == 0)
+    def _():
+        output_ref[...] = a_ref[:, pl.ds(3 * kh, kh)].T
+        for f in (0, 1):
+            up_ref[:, pl.ds(f * fs, fs)] = m_ref[f, :, pl.ds(0, fs)]
+            down_ref[pl.ds(f * fs, fs), :] = m_ref[f, :, pl.ds(fs, fs)].T
+
+
+def finish(size, grad, grad_a, grad_m):
     positions, features = grad.shape
-    rows = 256
+    rows = min(1024, positions)
+    tb, fs = size.tb, size.fs
+    whole = [((features, tb), F32), ((tb, 2 * fs), F32), ((2 * fs, tb), F32)]
     return pl.pallas_call(
-        finish_kernel,
+        functools.partial(finish_kernel, features, fs),
         grid=(positions // rows,),
-        in_specs=[pl.BlockSpec((rows, features), lambda i: (i, 0))],
-        out_specs=[pl.BlockSpec((rows // t, features), lambda i: (i, 0)) for t in (1, 4, 16)],
-        out_shape=[jax.ShapeDtypeStruct((positions // t, features), F32) for t in (1, 4, 16)],
+        in_specs=[
+            pl.BlockSpec((rows, features), lambda i: (i, 0)),
+            pl.BlockSpec(grad_a.shape, lambda i: (0, 0)),
+            pl.BlockSpec(grad_m.shape, lambda i: (0, 0, 0)),
+        ],
+        out_specs=[pl.BlockSpec((rows // t, features), lambda i: (i, 0)) for t in (1, 4, 16)]
+        + [pl.BlockSpec(shape, lambda i: (0, 0)) for shape, _ in whole],
+        out_shape=[jax.ShapeDtypeStruct((positions // t, features), F32) for t in (1, 4, 16)]
+        + [jax.ShapeDtypeStruct(*x) for x in whole],
+        compiler_params=pltpu.CompilerParams(vmem_limit_bytes=32 * 2**20),
         name="token_gradients",
-    )(grad)
+    )(grad, grad_a, grad_m)
 
 
 def shards(
@@ -1018,7 +1120,8 @@
         "sib_gm": ((units, z, tb, wide), BF16),
         "got_gm": ((units, z, tb, wide), BF16),
         "z_ga": ((2, z, size.half, wide), BF16),
-        "z_gm": ((2, z, tb, wide), BF16),
+        "z_gm": ((2, z + len(tree.far), tb, wide), BF16),
+        "z_far": ((units, z, tb, wide), BF16),
     }
     hbm = pl.BlockSpec(memory_space=pltpu.HBM)
     results = pl.pallas_call(
@@ -1034,7 +1137,9 @@
         name="layer",
     )(tokens, middle_cond, coarse_cond, cotangent, a_own, m_own, params)
     layer_out, grad_rows, grad_a, grad_m, small = results[:5]
-    grad_tokens, grad_middle, grad_coarse = finish(grad_rows)
+    grad_tokens, grad_middle, grad_coarse, grad_output, grad_up, grad_down = finish(
+        size, grad_rows, grad_a, grad_m
+    )
     tok = lax.axis_index("tok")
     share = features // n_tok
     mine = lax.dynamic_slice_in_dim(small[:8], tok * share, share, 1)
@@ -1042,8 +1147,6 @@
     grad_hidden_bias = lax.dynamic_slice_in_dim(
         small[8 : 8 + ff // d].reshape(-1), tok * hidden_share, hidden_share, 0
     )
-    grad_up = jnp.concatenate([grad_m[0, :, :fs], grad_m[1, :, :fs]], axis=1)
-    grad_down = jnp.concatenate([grad_m[0, :, fs:].T, grad_m[1, :, fs:].T], axis=0)
     return (
         layer_out,
         grad_tokens,
@@ -1054,7 +1157,7 @@
         grad_a[:, : 3 * features].reshape(tb, 3, features),
         mine[4],
         mine[5],
-        grad_a[:, 3 * features :].T,
+        grad_output,
         mine[6],
         mine[2],
         mine[3],

time: 461 us -> 416 us (0.902)
  Pallas kernels: 442 us -> 397 us
    pallas_call x1, Pallas kernels: 432 us -> 394 us  [shards(): pl.pallas_call(functools.partial(layer_kernel, size, tree), out_shape=[ja...]
    pallas_call x1, Pallas kernels: 10.3 us -> 3.78 us  [finish(): pl.pallas_call(functools.partial(finish_kernel, features, fs), grid=(posi...]
where the time goes in v3:
time: 416 us; the launch traced here: 415 us
  Pallas kernels  397 us (95%)
  local copies, waits for them, and re-layouts  14.8 us (4%)
    pallas_call x1, Pallas kernels, shards(): pl.pallas_call(functools.partial(layer_kernel, size, tree), out_shape=[ja...  394 us

profile of v3, /device:TPU:8, one launch (start us, length us, event | category | flops | bytes accessed | tf_op | source)
XLA Modules:
  0.0 414.7 jit_solution(16524133382325682121)
XLA Ops:
  0.8 1.1 fusion.1
  1.8 0.1 copy.46
  1.9 0.1 copy.47
  2.1 1.0 fusion
  3.1 0.8 pad_maximum_fusion.refs_5_
  4.0 1.1 copy.39
  5.1 0.2 copy.41
  5.2 0.1 copy.40
  5.3 0.7 pad_maximum_fusion.1.refs_4_
  6.2 1.2 concatenate.15.refs_6_
  7.4 393.6 %layer.1 = (bf16[4096,256]{1,0:T(8,128)(2,1)}, bf16[4096,256]{1,0:T(8,128)(2,1)}, f32[128,1024]{1,0:T(8,128)}, f32[2,128,1024]{2,1,0:T(8,128)}, f32[16,256]{1,0:...) custom-call(bf16[4096,256]{1,0:T(8,128)(2,1)} %refs_0_.1, ...), custom_call_target="tpu_custom_call" | custom-call | flops 80000000000 | bytes 200000000 | tf_op jit(solution)/shard_map/layer/pallas_call | solution.py:1127
  401.0 1.6 copy-done
  402.6 1.0 copy-done.1
  403.6 1.2 copy-done.2
  404.9 3.8 token_gradients.1
  408.6 0.7 slice.49
  409.3 0.1 constant_dynamic-slice_fusion
  409.4 0.5 slice_bitcast_fusion.1
  409.9 0.7 slice_bitcast_fusion
  410.7 0.6 dynamic_slice.7
  411.2 1.0 slice.52
  412.3 0.2 copy.44
  412.4 0.9 copy.45
  413.4 1.3 copy.50
  (29 shorter events, 0.1 us)
Async XLA Ops:
  0.7 4.5 %copy-start.4 = (bf16[256,128]{1,0:T(8,128)(2,1)S(1)}, bf16[256,128]{1,0:T(8,128)(2,1)}, u32[]{:S(2)}) copy-start(bf16[256,128]{1,0:T(8,128)(2,1)} %param.25) | copy-start | bytes 196612
  0.7 5.4 %copy-start.5 = (f32[1024]{0:T(1024)S(1)}, f32[1024]{0:T(1024)}, u32[]{:S(2)}) copy-start(f32[1024]{0:T(1024)} %param.30) | copy-start | bytes 12292
  0.7 5.4 %copy-start.10 = (f32[256]{0:T(256)S(1)}, f32[256]{0:T(256)}, u32[]{:S(2)}) copy-start(f32[256]{0:T(256)} %param.23) | copy-start | bytes 3076
  0.7 5.4 %copy-start.11 = (f32[256]{0:T(256)S(1)}, f32[256]{0:T(256)}, u32[]{:S(2)}) copy-start(f32[256]{0:T(256)} %param.24) | copy-start | bytes 3076
  0.7 5.4 %copy-start.12 = (f32[256]{0:T(256)S(1)}, f32[256]{0:T(256)}, u32[]{:S(2)}) copy-start(f32[256]{0:T(256)} %param.26) | copy-start | bytes 3076
  0.7 5.4 %copy-start.13 = (f32[256]{0:T(256)S(1)}, f32[256]{0:T(256)}, u32[]{:S(2)}) copy-start(f32[256]{0:T(256)} %param.32) | copy-start | bytes 3076
  0.7 5.4 %copy-start.6 = (f32[256]{0:T(256)S(1)}, f32[256]{0:T(256)}, u32[]{:S(2)}) copy-start(f32[256]{0:T(256)} %param.20) | copy-start | bytes 3076
  0.7 5.4 %copy-start.7 = (f32[256]{0:T(256)S(1)}, f32[256]{0:T(256)}, u32[]{:S(2)}) copy-start(f32[256]{0:T(256)} %param.21) | copy-start | bytes 3076
  0.7 5.4 %copy-start.8 = (f32[256]{0:T(256)S(1)}, f32[256]{0:T(256)}, u32[]{:S(2)}) copy-start(f32[256]{0:T(256)} %param.27) | copy-start | bytes 3076
  0.8 5.4 %copy-start.9 = (f32[256]{0:T(256)S(1)}, f32[256]{0:T(256)}, u32[]{:S(2)}) copy-start(f32[256]{0:T(256)} %param.28) | copy-start | bytes 3076
  401.0 1.6 copy-start
  402.6 1.0 copy-start.1
  403.6 1.2 copy-start.2
  404.8 8.5 %copy-start.3 = (bf16[4096,256]{1,0:T(8,128)(2,1)S(1)}, bf16[4096,256]{1,0:T(8,128)(2,1)}, u32[]{:S(2)}) copy-start(bf16[4096,256]{1,0:T(8,128)(2,1)} %get-tuple-element.104) | copy-start | bytes 6291460

commit v4 on v3

--- a/solution.py
+++ b/solution.py
@@ -15,6 +15,7 @@
 BF16 = jnp.bfloat16
 F32 = jnp.float32
 SMALL_ROWS = 16
+SUM_BUFFERS = 6
 
 
 class Tree:
@@ -52,7 +53,7 @@
         self.first = set()
         sent = {}
         seen = set()
-        holders = [None, None]
+        holders = [None] * SUM_BUFFERS
         waiting = sorted(done, key=lambda u: done[u])
         held = None
         point = 0
@@ -69,7 +70,7 @@
                     continue
                 actions.append(("fetch", unit))
                 held = unit
-                self.turn[unit] = k = len(self.turn) % 2
+                self.turn[unit] = k = len(self.turn) % SUM_BUFFERS
                 self.before[unit] = holders[k]
                 holders[k] = unit
                 if unit[:2] not in seen:
@@ -268,8 +269,6 @@
         return ref["all_m"].at[tree.m_pos[r, f], z, c]
 
     far_units = [(r, f) for r in tree.far for f in (0, 1)]
-    for r, f in far_units:
-        send("fs", tree.m_pos[r, f], ref["m_own"].at[f], m_block(r, f), peer(r))
 
     kh, n, tile = s_.kh, s_.n, s_.tile
     rows_m, rows_c = n // 4, n // 16
@@ -312,9 +311,6 @@
 
     for f in (0, 1):
         z_send("zm", f, ref["m_own"].at[f], m_block(0, f))
-    for r, f in far_units:
-        arrived("fs", tree.m_pos[r, f], m_block(r, f))
-        z_send("zf", tree.m_pos[r, f], m_block(r, f), m_block(r, f))
 
     def to_sibling(kind, r, f):
         k = tree.pos[r, f] if kind == "a" else tree.m_pos[r, f]
@@ -344,6 +340,8 @@
         send("ax", tree.pos[r, f], a_part(0, f, c), a_part(r, f, c), peer(r))
     for f in (0, 1):
         to_sibling("a", 0, f)
+    for r, f in far_units:
+        send("fs", tree.m_pos[r, f], ref["m_own"].at[f], m_block(r, f), peer(r))
 
     own_params.wait()
     for r in range(1, s_.n_hid):
@@ -399,6 +397,9 @@
             if r == 1:
                 for u, f in a_near:
                     take_a(u, f)
+                for u, f in far_units:
+                    arrived("fs", tree.m_pos[u, f], m_block(u, f))
+                    z_send("zf", tree.m_pos[u, f], m_block(u, f), m_block(u, f))
                 own_ct.start()
                 for k in range(1, s_.n_hid):
                     send("ct", k, ref["cotangent"].at[columns(block_of(k), n)], cot_rows(h), peer(k))
@@ -557,11 +558,11 @@
     def fetches(unit, k):
         kind, r, f = unit
         if kind == "fold":
-            return [(30 + 3 * k, ref["z_far"].at[tree.m_pos[r, f]], buffer("acc", kind, k))]
-        out = [(30 + 3 * k, own_grad(*unit), buffer("acc", kind, k))]
-        out.append((31 + 3 * k, sib_grad(*unit), buffer("tmp", kind, k)))
+            return [(30, ref["z_far"].at[tree.m_pos[r, f]], buffer("acc", kind, k))]
+        out = [(30, own_grad(*unit), buffer("acc", kind, k))]
+        out.append((31, sib_grad(*unit), buffer("tmp", kind)))
         if kids[unit]:
-            out.append((32 + 3 * k, got_grad(*kids[unit][0]), buffer("more", kind)))
+            out.append((32, got_grad(*kids[unit][0]), buffer("more", kind)))
         return out
 
     def fetch(unit):
@@ -586,7 +587,7 @@
         k = plan.turn[unit]
         for item in fetches(unit, k):
             local(*item).wait()
-        acc, tmp, more = buffer("acc", kind, k), buffer("tmp", kind, k), buffer("more", kind)
+        acc, tmp, more = buffer("acc", kind, k), buffer("tmp", kind), buffer("more", kind)
         if kind == "fold":
             total = acc[0].astype(F32)
             for zz in range(1, s_.z):
@@ -874,43 +875,45 @@
     ref["sum3"][0] = ref["sum2"][0] + ref["sum2"][1]
     for step in range(1, s_.z):
         send("sum3", step, ref["sum3"].at[0], ref["sum3"].at[step], z_peer(step))
-    for k in (0, 1):
+    for k in range(SUM_BUFFERS):
         free_buffer(k, plan.holders[k])
 
     finals = [("m", 0), ("m", 1), ("a", 0), ("a", 1)]
 
-    def final_load(k, kind, f):
+    def final_loads(k, kind, f):
         slots = ref["z_g" + kind].at[f]
         if kind == "a":
-            return local(30 + k, slots, ref["acc"].at[k, pl.ds(0, s_.z), pl.ds(0, s_.half)])
-        return local(30 + k, slots, ref["acc"].at[k])
+            return [local(30 + k, slots, buffer("acc", kind, k))]
+        rest = ref["tmp" if f == 0 else "more"].at[pl.ds(0, len(tree.far))]
+        out = [local(30 + k, slots.at[pl.ds(0, s_.z)], buffer("acc", kind, k))]
+        if tree.far:
+            out.append(local(41 + k, slots.at[pl.ds(s_.z, len(tree.far))], rest))
+        return out
 
     def final_store(k, kind, f):
         if kind == "a":
-            source = ref["final"].at[k, pl.ds(0, s_.half)]
+            source = ref["facc"].at[pl.ds(k * s_.tb, s_.half), pl.ds(0, s_.wide)]
             return local(34 + k, source, ref["grad_a"].at[pl.ds(f * s_.half, s_.half)])
-        return local(34 + k, ref["final"].at[k], ref["grad_m"].at[f])
-
-    for number, (kind, f) in enumerate(finals):
-        k = number % 2
+        return local(34 + k, ref["facc"].at[pl.ds(k * s_.tb, s_.tb), pl.ds(0, s_.wide)], ref["grad_m"].at[f])
+
+    for k, (kind, f) in enumerate(finals):
         for step in range(1, s_.z):
             arrived("zg" + kind, f * s_.z + step, z_slot(kind, f, step))
         if kind == "m":
             for i, r in enumerate(tree.far):
                 arrived("fold", tree.m_pos[r, f], z_slot(kind, f, s_.z + i))
-        load = final_load(k, kind, f)
-        load.start()
-        load.wait()
-        total = ref["acc"][k, 0].astype(F32) if kind == "m" else ref["acc"][k, 0, pl.ds(0, s_.half)].astype(F32)
-        for step in range(1, s_.z + (len(tree.far) if kind == "m" else 0)):
-            more = ref["acc"][k, step] if kind == "m" else ref["acc"][k, step, pl.ds(0, s_.half)]
-            total = total + more.astype(F32)
-        if number >= 2:
-            final_store(k, *finals[number - 2]).wait()
-        if kind == "a":
-            ref["final"][k, pl.ds(0, s_.half)] = total
-        else:
-            ref["final"][k] = total
+        for load in final_loads(k, kind, f):
+            load.start()
+        for load in final_loads(k, kind, f):
+            load.wait()
+        rows = pl.ds(0, s_.half if kind == "a" else s_.tb)
+        total = ref["acc"][k, 0, rows].astype(F32)
+        for step in range(1, s_.z):
+            total = total + ref["acc"][k, step, rows].astype(F32)
+        if kind == "m":
+            for i in range(len(tree.far)):
+                total = total + ref["tmp" if f == 0 else "more"][i].astype(F32)
+        ref["facc"][pl.ds(k * s_.tb, rows.size), pl.ds(0, s_.wide)] = total
         final_store(k, kind, f).start()
     total = ref["sum3"][0]
     for step in range(1, s_.z):
@@ -921,8 +924,8 @@
     small.start()
 
     small.wait()
-    for number in (2, 3):
-        final_store(number % 2, *finals[number]).wait()
+    for k, (kind, f) in enumerate(finals):
+        final_store(k, kind, f).wait()
     own_lo.wait()
     own_gt.wait()
     for r in range(1, s_.n_hid):
@@ -975,10 +978,9 @@
         "wa": ((s_.n_hid, s_.z, 2, s_.tb, s_.wide), BF16),
         "hid": ((s_.n, s_.fs), BF16),
         "gb": ((s_.n, s_.fs), BF16),
-        "acc": ((2, s_.z + len(tree.far), s_.tb, s_.wide), BF16),
-        "tmp": ((2, s_.z, s_.tb, s_.wide), BF16),
+        "acc": ((SUM_BUFFERS, s_.z, s_.tb, s_.wide), BF16),
+        "tmp": ((s_.z, s_.tb, s_.wide), BF16),
         "more": ((s_.z, s_.tb, s_.wide), BF16),
-        "final": ((2, s_.tb, s_.wide), F32),
         "hidden_bias": ((units, 1, s_.fs), F32),
         "hidden_sum": ((units, 1, s_.fs), F32),
         "sums": ((SMALL_ROWS, s_.d), F32),

time: 416 us -> 356 us (0.86)
  Pallas kernels: 397 us -> 338 us
    pallas_call x1, Pallas kernels: 394 us -> 334 us  [shards(): pl.pallas_call(functools.partial(layer_kernel, size, tree), out_shape=[ja...]
where the time goes in v4:
time: 356 us; the launch traced here: 355 us
  Pallas kernels  338 us (95%)
  local copies, waits for them, and re-layouts  14.8 us (4%)
    pallas_call x1, Pallas kernels, shards(): pl.pallas_call(functools.partial(layer_kernel, size, tree), out_shape=[ja...  334 us
    unnamed x36, local copies, waits for them, and re-layouts  8.26 us

profile of v4, /device:TPU:8, one launch (start us, length us, event | category | flops | bytes accessed | tf_op | source)
XLA Modules:
  0.0 355.2 jit_solution(16014322888819990997)
XLA Ops:
  0.8 1.1 fusion.1
  1.8 0.1 copy.46
  1.9 0.1 copy.47
  2.1 1.0 fusion
  3.1 0.8 pad_maximum_fusion.refs_5_
  4.0 1.1 copy.39
  5.1 0.2 copy.41
  5.2 0.1 copy.40
  5.3 0.7 pad_maximum_fusion.1.refs_4_
  6.2 1.2 concatenate.15.refs_6_
  7.4 334.1 %layer.1 = (bf16[4096,256]{1,0:T(8,128)(2,1)}, bf16[4096,256]{1,0:T(8,128)(2,1)}, f32[128,1024]{1,0:T(8,128)}, f32[2,128,1024]{2,1,0:T(8,128)}, f32[16,256]{1,0:...) custom-call(bf16[4096,256]{1,0:T(8,128)(2,1)} %refs_0_.1, ...), custom_call_target="tpu_custom_call" | custom-call | flops 80000000000 | bytes 200000000 | tf_op jit(solution)/shard_map/layer/pallas_call | solution.py:1129
  341.6 1.6 copy-done
  343.1 1.0 copy-done.1
  344.2 1.2 copy-done.2
  345.4 3.8 %token_gradients.1 = (f32[4096,256]{1,0:T(8,128)}, f32[1024,256]{1,0:T(8,128)}, f32[256,256]{1,0:T(8,128)}, f32[256,128]{1,0:T(8,128)}, f32[128,1024]{1,0:T(8,128)}, /*index=5*/f32[1024,128]{1,0:T(8,128)}) custom-call(bf16[4096,256]{1,0:T(8,128)(2,1)S(1)} %copy-done, f32[128,1024]{1,0:T(8,128)S(1)} %copy-done.1, f32[2,128,1024]{2,1,0:T(8,128)S(1)} %copy-done.2), custom_call_target="tpu_custom_call" | custom-call | tf_op jit(solution)/shard_map/token_gradients/pallas_call | solution.py:1051
  349.2 0.7 slice.49
  349.9 0.1 constant_dynamic-slice_fusion
  350.0 0.5 slice_bitcast_fusion.1
  350.5 0.7 slice_bitcast_fusion
  351.2 0.6 dynamic_slice.7
  351.8 1.0 slice.52
  352.8 0.2 copy.44
  353.0 0.9 copy.45
  353.9 1.3 copy.50
  (29 shorter events, 0.1 us)
Async XLA Ops:
  0.7 4.5 %copy-start.4 = (bf16[256,128]{1,0:T(8,128)(2,1)S(1)}, bf16[256,128]{1,0:T(8,128)(2,1)}, u32[]{:S(2)}) copy-start(bf16[256,128]{1,0:T(8,128)(2,1)} %param.25) | copy-start | bytes 196612
  0.7 5.4 %copy-start.5 = (f32[1024]{0:T(1024)S(1)}, f32[1024]{0:T(1024)}, u32[]{:S(2)}) copy-start(f32[1024]{0:T(1024)} %param.30) | copy-start | bytes 12292
  0.7 5.4 %copy-start.10 = (f32[256]{0:T(256)S(1)}, f32[256]{0:T(256)}, u32[]{:S(2)}) copy-start(f32[256]{0:T(256)} %param.23) | copy-start | bytes 3076
  0.7 5.4 %copy-start.11 = (f32[256]{0:T(256)S(1)}, f32[256]{0:T(256)}, u32[]{:S(2)}) copy-start(f32[256]{0:T(256)} %param.24) | copy-start | bytes 3076
  0.7 5.4 %copy-start.12 = (f32[256]{0:T(256)S(1)}, f32[256]{0:T(256)}, u32[]{:S(2)}) copy-start(f32[256]{0:T(256)} %param.26) | copy-start | bytes 3076
  0.7 5.4 %copy-start.13 = (f32[256]{0:T(256)S(1)}, f32[256]{0:T(256)}, u32[]{:S(2)}) copy-start(f32[256]{0:T(256)} %param.32) | copy-start | bytes 3076
  0.7 5.4 %copy-start.6 = (f32[256]{0:T(256)S(1)}, f32[256]{0:T(256)}, u32[]{:S(2)}) copy-start(f32[256]{0:T(256)} %param.20) | copy-start | bytes 3076
  0.7 5.4 %copy-start.7 = (f32[256]{0:T(256)S(1)}, f32[256]{0:T(256)}, u32[]{:S(2)}) copy-start(f32[256]{0:T(256)} %param.21) | copy-start | bytes 3076
  0.7 5.4 %copy-start.8 = (f32[256]{0:T(256)S(1)}, f32[256]{0:T(256)}, u32[]{:S(2)}) copy-start(f32[256]{0:T(256)} %param.27) | copy-start | bytes 3076
  0.8 5.4 %copy-start.9 = (f32[256]{0:T(256)S(1)}, f32[256]{0:T(256)}, u32[]{:S(2)}) copy-start(f32[256]{0:T(256)} %param.28) | copy-start | bytes 3076
  341.5 1.6 copy-start
  343.1 1.0 copy-start.1
  344.2 1.2 copy-start.2
  345.4 8.5 %copy-start.3 = (bf16[4096,256]{1,0:T(8,128)(2,1)S(1)}, bf16[4096,256]{1,0:T(8,128)(2,1)}, u32[]{:S(2)}) copy-start(bf16[4096,256]{1,0:T(8,128)(2,1)} %get-tuple-element.104) | copy-start | bytes 6291460

commit v5 on v4

--- a/solution.py
+++ b/solution.py
@@ -15,7 +15,7 @@
 BF16 = jnp.bfloat16
 F32 = jnp.float32
 SMALL_ROWS = 16
-SUM_BUFFERS = 6
+SUM_BUFFERS = 4
 
 
 class Tree:
@@ -30,7 +30,9 @@
         first = [(1 << b, b % 2) for b in range(self.bits)]
         second = [(1 << b, 1 - b % 2) for b in range(self.bits)]
         self.m_near = first + second
-        self.m_units = [(0, 0), (0, 1)] + first + [(r, f) for r in self.far for f in (0, 1)] + second
+        rest = [(r, f) for r in self.far for f in (0, 1)]
+        mixed = [u for k in range(max(len(second), len(rest))) for u in second[k : k + 1] + rest[k : k + 1]]
+        self.m_units = [(0, 0), (0, 1)] + first + mixed
         self.m_pos = {u: k for k, u in enumerate(self.m_units)}
 
     def children(self, r, f):
@@ -53,7 +55,8 @@
         self.first = set()
         sent = {}
         seen = set()
-        holders = [None] * SUM_BUFFERS
+        holders = {True: [None] * SUM_BUFFERS, False: [None] * SUM_BUFFERS}
+        turns = {True: 0, False: 0}
         waiting = sorted(done, key=lambda u: done[u])
         held = None
         point = 0
@@ -70,9 +73,11 @@
                     continue
                 actions.append(("fetch", unit))
                 held = unit
-                self.turn[unit] = k = len(self.turn) % SUM_BUFFERS
-                self.before[unit] = holders[k]
-                holders[k] = unit
+                pool = unit[0] == "a"
+                self.turn[unit] = k = turns[pool] % SUM_BUFFERS
+                turns[pool] += 1
+                self.before[unit] = holders[pool][k]
+                holders[pool][k] = unit
                 if unit[:2] not in seen:
                     self.first.add(unit)
                 seen.add(unit[:2])
@@ -82,7 +87,7 @@
                 self.at[point] = actions
             point += 1
         self.end = point
-        self.holders = holders
+        self.holders = holders[True] + holders[False]
 
 
 def dot(a, b):
@@ -258,12 +263,12 @@
     own_params = local(0, ref["params"], ref["params_all"].at[:, columns(h, s_.kh)])
     own_params.start()
     z_send("za", 0, ref["a_own"], ref["all_a"].at[0, z, c])
-    own_a = local(1, ref["a_own"], ref["all_a"].at[0, z, c])
-    own_a.start()
-    own_m = []
-    for f in (0, 1):
-        own_m.append(local(2 + f, ref["m_own"].at[f], ref["all_m"].at[tree.m_pos[0, f], z, c]))
-        own_m[f].start()
+    own_blocks = [(ref["a_own"], ref["all_a"].at[0, z, c])]
+    own_blocks += [(ref["m_own"].at[f], ref["all_m"].at[tree.m_pos[0, f], z, c]) for f in (0, 1)]
+    own_in = [local(1 + k, source, ref["acc"].at[k, 0]) for k, (source, _) in enumerate(own_blocks)]
+    own_out = [local(1 + k, ref["acc"].at[k, 0], to) for k, (_, to) in enumerate(own_blocks)]
+    for copy in own_in:
+        copy.start()
 
     def m_block(r, f):
         return ref["all_m"].at[tree.m_pos[r, f], z, c]
@@ -309,8 +314,9 @@
                 copy.start()
                 own_xs.append(copy)
 
-    for f in (0, 1):
-        z_send("zm", f, ref["m_own"].at[f], m_block(0, f))
+    for load, store in zip(own_in, own_out, strict=True):
+        load.wait()
+        store.start()
 
     def to_sibling(kind, r, f):
         k = tree.pos[r, f] if kind == "a" else tree.m_pos[r, f]
@@ -334,14 +340,15 @@
         arrived(kind + "c", k, part[kind](r, f, 1 - c))
 
     a_near = sorted([u for u in tree.units if u[0] in tree.near], key=lambda u: -len(tree.children(*u)))
-    own_a.wait()
+    for store in own_out:
+        store.wait()
     z_arrived("za", 0, ref["all_a"].at[0, z, c])
+    for f in (0, 1):
+        z_send("zm", f, ref["m_own"].at[f], m_block(0, f))
     for r, f in a_near:
         send("ax", tree.pos[r, f], a_part(0, f, c), a_part(r, f, c), peer(r))
     for f in (0, 1):
         to_sibling("a", 0, f)
-    for r, f in far_units:
-        send("fs", tree.m_pos[r, f], ref["m_own"].at[f], m_block(r, f), peer(r))
 
     own_params.wait()
     for r in range(1, s_.n_hid):
@@ -397,23 +404,12 @@
             if r == 1:
                 for u, f in a_near:
                     take_a(u, f)
-                for u, f in far_units:
-                    arrived("fs", tree.m_pos[u, f], m_block(u, f))
-                    z_send("zf", tree.m_pos[u, f], m_block(u, f), m_block(u, f))
                 own_ct.start()
                 for k in range(1, s_.n_hid):
                     send("ct", k, ref["cotangent"].at[columns(block_of(k), n)], cot_rows(h), peer(k))
         else:
             for f in (0, 1):
                 take_a(r, f)
-        if r == s_.n_hid - 1:
-            for f in (0, 1):
-                own_m[f].wait()
-                z_arrived("zm", f, m_block(0, f))
-            for u, f in tree.m_near:
-                send("mx", tree.m_pos[u, f], m_part(0, f, c), m_part(u, f, c), peer(u))
-            for f in (0, 1):
-                to_sibling("m", 0, f)
         for f in (0, 1):
             take_sibling("a", r, f)
         load = weight_load(r, ref["all_a"].at[r])
@@ -465,17 +461,28 @@
                 ref["att"][r, rows, pl.ds(p * PAIR, PAIR)] = out.astype(BF16)
             return 0
 
-        lax.fori_loop(0, s_.blocks, attend, 0)
+        def attend_two(i, _):
+            attend(2 * i, 0)
+            return attend(2 * i + 1, 0)
+
+        lax.fori_loop(0, s_.blocks // 2, attend_two, 0)
 
     lax.fori_loop(0, s_.n_hid, lambda r, _: (attend_chunk(r), 0)[1], 0)
+
+    for f in (0, 1):
+        z_arrived("zm", f, m_block(0, f))
+    for f in (0, 1):
+        to_sibling("m", 0, f)
 
     def mix(i, _):
         rows = pl.ds(pl.multiple_of(i * tile, tile), tile)
         total = ref["xs"][rows, :].astype(F32) + gain_row(6)
         for r in range(s_.n_hid):
             total = total + dot_t(ref["att"][r, rows, :], matrix(r, 3 * kh, kh))
-        ref["res"][rows, :] = total
-        scaled, _inverse = scaled_rows(total)
+        ref["facc"][rows, :] = total + gain_row(7)
+        scaled, inverse = scaled_rows(total)
+        ref["scaled_two"][rows, :] = scaled.astype(BF16)
+        ref["inverse_two"][rows, :] = inverse
         normed = (scaled * gain_row(2) + gain_row(3)).astype(BF16)
         ref["n2"][rows, :] = normed
         return 0
@@ -485,13 +492,14 @@
     own_ct.wait()
     for k in range(1, s_.n_hid):
         arrived("ct", k, cot_rows(h))
+    for r, f in far_units:
+        send("fs", tree.m_pos[r, f], ref["m_own"].at[f], m_block(r, f), peer(r))
     for i in range(s_.tiles):
         rows = pl.ds(i * tile, tile)
         ref["n2_t"][:, rows] = ref["n2"][rows, :].T
         upstream = ref["ct"][rows, :]
-        ref["ct_t"][:, rows] = upstream.T
+        ref["ct_t"][:, :, :, rows] = upstream.T.reshape(s_.z, 2, s_.tb, tile)
         add_sum(7, upstream.astype(F32))
-        ref["facc"][rows, :] = jnp.zeros((tile, s_.d), F32)
         ref["gacc"][rows, :] = jnp.zeros((tile, s_.d), F32)
 
     mlp_points = 2 * n_units
@@ -501,6 +509,8 @@
     for k, (r, f) in enumerate(tree.m_units):
         done["m", r, f] = 2 * k + 1
         kids["m", r, f] = [("m", u, f) for u in tree.near] if r == 0 else []
+        if r == 0:
+            done["m", r, f] = mlp_points - 1
     for r, f in far_units:
         done["fold", r, f] = 0
         kids["fold", r, f] = [("m", r, f)]
@@ -508,7 +518,7 @@
         for f in (0, 1):
             done["a", r, f] = chunk_points + 4 * (s_.n_hid - 1 - r) + 3
             kids["a", r, f] = [("a", child, f) for child, _ in tree.children(r, f)]
-    plan = Schedule(done, kids, {"m": 6, "a": 4, "fold": 9}, last_point)
+    plan = Schedule(done, kids, {"m": 11, "a": 4, "fold": 9}, last_point)
 
     def place(kind, r, f):
         return tree.pos[r, f] if kind == "a" else tree.m_pos[r, f]
@@ -526,9 +536,18 @@
     def got_grad(kind, r, f):
         return ref["got_g" + kind].at[place(kind, r, f)]
 
-    def buffer(name, kind, k=None):
-        whole = ref[name] if k is None else ref[name].at[k]
-        return whole.at[pl.ds(0, s_.z), pl.ds(0, s_.half if kind == "a" else s_.tb)]
+    def part_of(whole, kind):
+        return whole.at[:, pl.ds(0, s_.half if kind == "a" else s_.tb)]
+
+    def spare(first, rows):
+        return ref["ct_t"].at[:, first, rows, pl.ds(0, s_.wide)]
+
+    def sum_buffer(unit):
+        k = plan.turn[unit]
+        if unit[0] != "a":
+            return ref["acc"].at[k]
+        rows = pl.ds(k % 2 * s_.half, s_.half)
+        return ref["acc"].at[SUM_BUFFERS, :, rows] if k < 2 else spare(1, rows)
 
     def z_slot(kind, f, step):
         return ref["z_g" + kind].at[f, step]
@@ -541,11 +560,11 @@
     def scatters(kind, r):
         return r == 0 or (kind == "m" and r in tree.far)
 
-    def free_buffer(k, holder):
+    def free_buffer(holder):
         if holder is None:
             return
         kind, r, f = holder
-        source = buffer("acc", kind, k)
+        source = sum_buffer(holder)
         if kind == "fold":
             left("fold", tree.m_pos[r, f], source.at[0])
         elif scatters(kind, r):
@@ -555,20 +574,19 @@
         else:
             left("g" + kind, place(kind, r, f), source)
 
-    def fetches(unit, k):
+    def fetches(unit):
         kind, r, f = unit
         if kind == "fold":
-            return [(30, ref["z_far"].at[tree.m_pos[r, f]], buffer("acc", kind, k))]
-        out = [(30, own_grad(*unit), buffer("acc", kind, k))]
-        out.append((31, sib_grad(*unit), buffer("tmp", kind)))
+            return [(30, ref["z_far"].at[tree.m_pos[r, f]], sum_buffer(unit))]
+        out = [(30, own_grad(*unit), sum_buffer(unit))]
+        out.append((31, sib_grad(*unit), part_of(ref["tmp"], kind)))
         if kids[unit]:
-            out.append((32, got_grad(*kids[unit][0]), buffer("more", kind)))
+            out.append((32, got_grad(*kids[unit][0]), part_of(spare(0, pl.ds(0, s_.tb)), kind)))
         return out
 
     def fetch(unit):
         kind, r, f = unit
-        k = plan.turn[unit]
-        free_buffer(k, plan.before[unit])
+        free_buffer(plan.before[unit])
         if kind == "fold":
             for step in range(1, s_.z):
                 name, first, slots = scattered("m", r, f)
@@ -579,15 +597,14 @@
         if kind != "fold":
             for kid in kids[unit][:1]:
                 arrived("g" + kind, place(*kid), got_grad(*kid))
-        for item in fetches(unit, k):
+        for item in fetches(unit):
             local(*item).start()
 
     def finish(unit):
         kind, r, f = unit
-        k = plan.turn[unit]
-        for item in fetches(unit, k):
+        for item in fetches(unit):
             local(*item).wait()
-        acc, tmp, more = buffer("acc", kind, k), buffer("tmp", kind), buffer("more", kind)
+        acc, tmp, more = sum_buffer(unit), part_of(ref["tmp"], kind), part_of(spare(0, pl.ds(0, s_.tb)), kind)
         if kind == "fold":
             total = acc[0].astype(F32)
             for zz in range(1, s_.z):
@@ -658,6 +675,7 @@
     for k in (0, 1):
         take_sibling("m", *tree.m_units[k])
     weight_load(0, ref["all_m"].at[0]).start()
+    big = min(256, n)
     gelu_scale = (2.0 / jnp.pi) ** 0.5
 
     def feed(step, _):
@@ -665,7 +683,7 @@
         weight_load(slot, ref["all_m"].at[step]).wait()
 
         def rows_of(i, _):
-            rows = pl.ds(pl.multiple_of(i * tile, tile), tile)
+            rows = pl.ds(pl.multiple_of(i * big, big), big)
             up, down = matrix(slot, 0, fs), matrix(slot, fs, fs)
             before = dot(ref["n2"][rows, :], up) + ref["hidden_bias"][step]
             square = before * before
@@ -683,7 +701,16 @@
             ref["hidden_sum"][step] = ref["hidden_sum"][step] + row_sum(grad_before.astype(F32))
             return 0
 
-        lax.fori_loop(0, s_.tiles, rows_of, 0)
+        lax.fori_loop(0, n // big, rows_of, 0)
+
+        @pl.when(step == 0)
+        def _():
+            for r, f in far_units:
+                arrived("fs", tree.m_pos[r, f], m_block(r, f))
+                z_send("zf", tree.m_pos[r, f], m_block(r, f), m_block(r, f))
+            for r, f in tree.m_near:
+                send("mx", tree.m_pos[r, f], m_part(0, f, c), m_part(r, f, c), peer(r))
+
         for k in range(1, n_units - 1):
             pl.when(step == k)(functools.partial(take_m, *tree.m_units[k + 1]))
 
@@ -701,7 +728,7 @@
         def grads(zz, _):
             rows = pl.ds(pl.multiple_of(zz * (2 * s_.tb), 2 * s_.tb), 2 * s_.tb)
             put_rows(stage, zz, 0, dot(ref["n2_t"][rows, :], ref["gb"][...]).astype(BF16))
-            put_rows(stage, zz, fs, dot(ref["ct_t"][rows, :], ref["hid"][...]).astype(BF16))
+            put_rows(stage, zz, fs, dot(ref["ct_t"][zz].reshape(2 * s_.tb, n), ref["hid"][...]).astype(BF16))
             return 0
 
         lax.fori_loop(0, s_.z // 2, grads, 0)
@@ -726,9 +753,8 @@
 
     def back_two(i, _):
         rows = pl.ds(pl.multiple_of(i * tile, tile), tile)
-        residual = ref["res"][rows, :]
-        ref["n2"][rows, :] = (residual + (ref["facc"][rows, :] + gain_row(7))).astype(BF16)
-        scaled, inverse = scaled_rows(residual)
+        ref["n2"][rows, :] = ref["facc"][rows, :].astype(BF16)
+        scaled, inverse = ref["scaled_two"][rows, :].astype(F32), ref["inverse_two"][rows, :]
         grad = ref["gacc"][rows, :]
         add_sum(2, grad * scaled)
         add_sum(3, grad)
@@ -797,7 +823,11 @@
                     ref["pj"][r, rows, pl.ds(k * kh + p * PAIR, PAIR)] = values.astype(BF16)
             return 0
 
-        lax.fori_loop(0, s_.blocks, pull_attention, 0)
+        def pull_two(i, _):
+            pull_attention(2 * i, 0)
+            return pull_attention(2 * i + 1, 0)
+
+        lax.fori_loop(0, s_.blocks // 2, pull_two, 0)
         loop_point(step, chunk_points, 4, 1, s_.n_hid)
 
         @pl.when(step >= 2)
@@ -825,24 +855,43 @@
                 ref["sums"][pl.ds(k, 1), cols] = ref["sums"][pl.ds(k, 1), cols] + part_sum
             return 0
 
-        lax.fori_loop(0, s_.tiles, pull_rows, 0)
+        @pl.when(step + 2 < s_.n_hid)
+        def _():
+            lax.fori_loop(0, s_.tiles, pull_rows, 0)
+
         loop_point(step, chunk_points, 4, 3, s_.n_hid)
         return 0
 
     lax.fori_loop(0, s_.n_hid, back_chunk, 0)
     stage_kept("a", 0, 2 + (s_.n_hid - 1) % 2)
-
-    def back_one(i, _):
-        rows = pl.ds(pl.multiple_of(i * tile, tile), tile)
+    last_two = [(r, (s_.n_hid - 1 - r) % 2) for r in (1, 0)]
+
+    def back_one(i):
+        rows = pl.ds(i * tile, tile)
         scaled, inverse = scaled_rows(ref["xs"][rows, :].astype(F32))
         grad = ref["gacc"][rows, :]
+        for r, slot in last_two:
+            grad = grad + dot_t(ref["pj"][r, rows, :], matrix(slot, 0, 3 * kh))
+            for k, first in ((4, 0), (5, 2 * kh)):
+                cols = columns(block_of(r), kh)
+                part_sum = row_sum(ref["pj"][r, rows, pl.ds(first, kh)].astype(F32))
+                ref["sums"][pl.ds(k, 1), cols] = ref["sums"][pl.ds(k, 1), cols] + part_sum
         add_sum(0, grad * scaled)
         add_sum(1, grad)
         total = ref["facc"][rows, :] + norm_pull(grad, gain_row(0), scaled, inverse)
         ref["ct"][rows, :] = total.astype(BF16)
-        return 0
-
-    lax.fori_loop(0, s_.tiles, back_one, 0)
+
+    def row_copy(i, r):
+        source = ref["ct"].at[pl.ds(i * tile, tile), columns(block_of(r), kh)]
+        return source, ref["grad_rows"].at[pl.ds(pl.multiple_of(h * n + i * tile, tile), tile)]
+
+    def send_rows(i):
+        for r in range(1, s_.n_hid):
+            send("gt", i * s_.n_hid + r, *row_copy(i, r), peer(r))
+        local(41 + i, *row_copy(i, 0)).start()
+
+    for i in range(s_.tiles):
+        back_one(i)
     for k, (r, f) in enumerate(tree.m_units):
         for i in range(s_.fs // kh):
             ref["sums"][pl.ds(8 + 2 * f + i, 1), columns(block_of(r), kh)] = ref["hidden_sum"][
@@ -850,44 +899,19 @@
             ]
     for r in range(1, s_.n_hid):
         send("sum1", r, ref["sums"].at[:, columns(block_of(r), kh)], ref["sum1"].at[r], peer(r))
-    own_gt = local(1, ref["ct"].at[:, columns(h, kh)], out_rows("grad_rows", h))
-    own_gt.start()
-
-    def send_rows():
-        for r in range(1, s_.n_hid):
-            send("gt", r, ref["ct"].at[:, columns(block_of(r), kh)], out_rows("grad_rows", h), peer(r))
-
-    total = ref["sums"][:, columns(h, kh)]
-    for r in range(1, s_.n_hid):
-        arrived("sum1", r, ref["sum1"].at[r])
-        total = total + ref["sum1"][r]
-    ref["sum2"][0] = total
-    send("sum2", 0, ref["sum2"].at[0], ref["sum2"].at[1], sibling)
-    rows_sent = False
-    for point in range(last_point, plan.end):
-        if not rows_sent and any(verb == "fetch" and unit[:2] == ("a", 0) for verb, unit in plan.at.get(point, ())):
-            send_rows()
-            rows_sent = True
-        act(point)
-    if not rows_sent:
-        send_rows()
-    arrived("sum2", 0, ref["sum2"].at[1])
-    ref["sum3"][0] = ref["sum2"][0] + ref["sum2"][1]
-    for step in range(1, s_.z):
-        send("sum3", step, ref["sum3"].at[0], ref["sum3"].at[step], z_peer(step))
-    for k in range(SUM_BUFFERS):
-        free_buffer(k, plan.holders[k])
+    for i in range(s_.tiles):
+        send_rows(i)
 
     finals = [("m", 0), ("m", 1), ("a", 0), ("a", 1)]
 
     def final_loads(k, kind, f):
         slots = ref["z_g" + kind].at[f]
+        room = ref["wa"].at[k % 2]
         if kind == "a":
-            return [local(30 + k, slots, buffer("acc", kind, k))]
-        rest = ref["tmp" if f == 0 else "more"].at[pl.ds(0, len(tree.far))]
-        out = [local(30 + k, slots.at[pl.ds(0, s_.z)], buffer("acc", kind, k))]
+            return [local(30, slots, room.at[:, 0, pl.ds(0, s_.half)])]
+        out = [local(30, slots.at[pl.ds(0, s_.z)], room.at[:, 0])]
         if tree.far:
-            out.append(local(41 + k, slots.at[pl.ds(s_.z, len(tree.far))], rest))
+            out.append(local(31, slots.at[pl.ds(s_.z, len(tree.far))], room.at[pl.ds(0, len(tree.far)), 1]))
         return out
 
     def final_store(k, kind, f):
@@ -896,7 +920,8 @@
             return local(34 + k, source, ref["grad_a"].at[pl.ds(f * s_.half, s_.half)])
         return local(34 + k, ref["facc"].at[pl.ds(k * s_.tb, s_.tb), pl.ds(0, s_.wide)], ref["grad_m"].at[f])
 
-    for k, (kind, f) in enumerate(finals):
+    def final(k):
+        kind, f = finals[k]
         for step in range(1, s_.z):
             arrived("zg" + kind, f * s_.z + step, z_slot(kind, f, step))
         if kind == "m":
@@ -907,14 +932,44 @@
         for load in final_loads(k, kind, f):
             load.wait()
         rows = pl.ds(0, s_.half if kind == "a" else s_.tb)
-        total = ref["acc"][k, 0, rows].astype(F32)
+        total = ref["wa"][k % 2, 0, 0, rows].astype(F32)
         for step in range(1, s_.z):
-            total = total + ref["acc"][k, step, rows].astype(F32)
+            total = total + ref["wa"][k % 2, step, 0, rows].astype(F32)
         if kind == "m":
             for i in range(len(tree.far)):
-                total = total + ref["tmp" if f == 0 else "more"][i].astype(F32)
+                total = total + ref["wa"][k % 2, i, 1].astype(F32)
         ref["facc"][pl.ds(k * s_.tb, rows.size), pl.ds(0, s_.wide)] = total
         final_store(k, kind, f).start()
+
+    def first_finals():
+        final(0)
+        final(1)
+
+    def first_sums():
+        total = ref["sums"][:, columns(h, kh)]
+        for r in range(1, s_.n_hid):
+            arrived("sum1", r, ref["sum1"].at[r])
+            total = total + ref["sum1"][r]
+        ref["sum2"][0] = total
+        send("sum2", 0, ref["sum2"].at[0], ref["sum2"].at[1], sibling)
+
+    feed_done = False
+    for point in range(last_point, plan.end):
+        units = [unit for verb, unit in plan.at.get(point, ()) if verb == "fetch"]
+        if not feed_done and units and units[0][:2] == ("a", 0):
+            first_finals()
+            feed_done = True
+        act(point)
+    if not feed_done:
+        first_finals()
+
+    first_sums()
+    arrived("sum2", 0, ref["sum2"].at[1])
+    ref["sum3"][0] = ref["sum2"][0] + ref["sum2"][1]
+    for step in range(1, s_.z):
+        send("sum3", step, ref["sum3"].at[0], ref["sum3"].at[step], z_peer(step))
+    final(2)
+    final(3)
     total = ref["sum3"][0]
     for step in range(1, s_.z):
         arrived("sum3", step, ref["sum3"].at[step])
@@ -927,14 +982,19 @@
     for k, (kind, f) in enumerate(finals):
         final_store(k, kind, f).wait()
     own_lo.wait()
-    own_gt.wait()
+    for holder in plan.holders:
+        free_buffer(holder)
+    for i in range(s_.tiles):
+        local(41 + i, *row_copy(i, 0)).wait()
+        for r in range(1, s_.n_hid):
+            source, to = row_copy(i, r)
+            arrived("gt", i * s_.n_hid + r, to)
+            left("gt", i * s_.n_hid + r, source)
     for r in range(1, s_.n_hid):
         arrived("lo", r, out_rows("layer_out", h))
-        arrived("gt", r, out_rows("grad_rows", h))
         left("params", r, ref["params"])
         left("ct", r, cot_rows(h))
         left("lo", r, cot_rows(h))
-        left("gt", r, cot_rows(h))
         left("sum1", r, ref["sum1"].at[r])
     left("sum2", 0, ref["sum2"].at[0])
     for step in range(1, s_.z):
@@ -968,19 +1028,19 @@
         "nrm_t": ((s_.d, s_.n), BF16),
         "n2": ((s_.n, s_.d), BF16),
         "n2_t": ((s_.d, s_.n), BF16),
-        "ct_t": ((s_.d, s_.n), BF16),
+        "ct_t": ((s_.z, 2, s_.tb, s_.n), BF16),
         "pj": ((s_.n_hid, s_.n, 3 * s_.kh), BF16),
         "probs": ((s_.n_hid, s_.pairs, s_.n, 2 * BLOCK), BF16),
         "att": ((s_.n_hid, s_.n, s_.kh), BF16),
-        "res": ((s_.n, s_.d), F32),
+        "scaled_two": ((s_.n, s_.d), BF16),
+        "inverse_two": ((s_.n, 1), F32),
         "facc": ((s_.n, s_.d), F32),
         "gacc": ((s_.n, s_.d), F32),
         "wa": ((s_.n_hid, s_.z, 2, s_.tb, s_.wide), BF16),
         "hid": ((s_.n, s_.fs), BF16),
         "gb": ((s_.n, s_.fs), BF16),
-        "acc": ((SUM_BUFFERS, s_.z, s_.tb, s_.wide), BF16),
+        "acc": ((SUM_BUFFERS + 1, s_.z, s_.tb, s_.wide), BF16),
         "tmp": ((s_.z, s_.tb, s_.wide), BF16),
-        "more": ((s_.z, s_.tb, s_.wide), BF16),
         "hidden_bias": ((units, 1, s_.fs), F32),
         "hidden_sum": ((units, 1, s_.fs), F32),
         "sums": ((SMALL_ROWS, s_.d), F32),
@@ -1009,7 +1069,7 @@
         "zga": 2 * s_.z,
         "zgm": 2 * s_.z,
         "lo": s_.n_hid,
-        "gt": s_.n_hid,
+        "gt": s_.tiles * s_.n_hid,
         "sum1": s_.n_hid,
         "sum2": 1,
         "sum3": s_.z,
@@ -1133,7 +1193,7 @@
         out_specs=[hbm] * len(OUTPUTS),
         scratch_shapes=list(scratch(size, tree).values()),
         compiler_params=pltpu.CompilerParams(
-            collective_id=0, has_side_effects=True, vmem_limit_bytes=62 * 2**20
+            collective_id=0, has_side_effects=True, vmem_limit_bytes=63 * 2**20
         ),
         cost_estimate=pl.CostEstimate(flops=80 * 10**9, bytes_accessed=2 * 10**8, transcendentals=10**7),
         name="layer",

time: 356 us -> 336 us (0.944)
  Pallas kernels: 338 us -> 316 us
    pallas_call x1, Pallas kernels: 334 us -> 313 us  [shards(): pl.pallas_call(functools.partial(layer_kernel, size, tree), out_shape=[ja...]
where the time goes in v5:
time: 336 us; the launch traced here: 334 us
  Pallas kernels  316 us (94%)
  local copies, waits for them, and re-layouts  14.8 us (4%)
    pallas_call x1, Pallas kernels, shards(): pl.pallas_call(functools.partial(layer_kernel, size, tree), out_shape=[ja...  313 us
    unnamed x36, local copies, waits for them, and re-layouts  8.26 us

profile of v5, /device:TPU:8, one launch (start us, length us, event | category | flops | bytes accessed | tf_op | source)
XLA Modules:
  0.0 333.8 jit_solution(16286984712087692354)
XLA Ops:
  0.8 1.1 fusion.1
  1.8 0.1 copy.46
  1.9 0.1 copy.47
  2.1 1.0 fusion
  3.1 0.8 pad_maximum_fusion.refs_5_
  4.0 1.1 copy.39
  5.1 0.2 copy.41
  5.2 0.1 copy.40
  5.3 0.7 pad_maximum_fusion.1.refs_4_
  6.2 1.2 concatenate.15.refs_6_
  7.4 312.7 %layer.1 = (bf16[4096,256]{1,0:T(8,128)(2,1)}, bf16[4096,256]{1,0:T(8,128)(2,1)}, f32[128,1024]{1,0:T(8,128)}, f32[2,128,1024]{2,1,0:T(8,128)}, f32[16,256]{1,0:...) custom-call(bf16[4096,256]{1,0:T(8,128)(2,1)} %refs_0_.1, ...), custom_call_target="tpu_custom_call" | custom-call | flops 80000000000 | bytes 200000000 | tf_op jit(solution)/shard_map/layer/pallas_call | solution.py:1189
  320.1 1.6 copy-done
  321.7 1.0 copy-done.1
  322.7 1.2 copy-done.2
  323.9 3.8 %token_gradients.1 = (f32[4096,256]{1,0:T(8,128)}, f32[1024,256]{1,0:T(8,128)}, f32[256,256]{1,0:T(8,128)}, f32[256,128]{1,0:T(8,128)}, f32[128,1024]{1,0:T(8,128)}, /*index=5*/f32[1024,128]{1,0:T(8,128)}) custom-call(bf16[4096,256]{1,0:T(8,128)(2,1)S(1)} %copy-done, f32[128,1024]{1,0:T(8,128)S(1)} %copy-done.1, f32[2,128,1024]{2,1,0:T(8,128)S(1)} %copy-done.2), custom_call_target="tpu_custom_call" | custom-call | tf_op jit(solution)/shard_map/token_gradients/pallas_call | solution.py:1111
  327.7 0.7 slice.49
  328.4 0.1 constant_dynamic-slice_fusion
  328.5 0.5 slice_bitcast_fusion.1
  329.0 0.7 slice_bitcast_fusion
  329.7 0.6 dynamic_slice.7
  330.3 1.0 slice.52
  331.3 0.2 copy.44
  331.5 0.9 copy.45
  332.4 1.3 copy.50
  (29 shorter events, 0.1 us)
Async XLA Ops:
  0.7 4.5 %copy-start.4 = (bf16[256,128]{1,0:T(8,128)(2,1)S(1)}, bf16[256,128]{1,0:T(8,128)(2,1)}, u32[]{:S(2)}) copy-start(bf16[256,128]{1,0:T(8,128)(2,1)} %param.25) | copy-start | bytes 196612
  0.7 5.4 %copy-start.5 = (f32[1024]{0:T(1024)S(1)}, f32[1024]{0:T(1024)}, u32[]{:S(2)}) copy-start(f32[1024]{0:T(1024)} %param.30) | copy-start | bytes 12292
  0.7 5.4 %copy-start.10 = (f32[256]{0:T(256)S(1)}, f32[256]{0:T(256)}, u32[]{:S(2)}) copy-start(f32[256]{0:T(256)} %param.23) | copy-start | bytes 3076
  0.7 5.4 %copy-start.11 = (f32[256]{0:T(256)S(1)}, f32[256]{0:T(256)}, u32[]{:S(2)}) copy-start(f32[256]{0:T(256)} %param.24) | copy-start | bytes 3076
  0.7 5.4 %copy-start.12 = (f32[256]{0:T(256)S(1)}, f32[256]{0:T(256)}, u32[]{:S(2)}) copy-start(f32[256]{0:T(256)} %param.26) | copy-start | bytes 3076
  0.7 5.4 %copy-start.13 = (f32[256]{0:T(256)S(1)}, f32[256]{0:T(256)}, u32[]{:S(2)}) copy-start(f32[256]{0:T(256)} %param.32) | copy-start | bytes 3076
  0.7 5.4 %copy-start.6 = (f32[256]{0:T(256)S(1)}, f32[256]{0:T(256)}, u32[]{:S(2)}) copy-start(f32[256]{0:T(256)} %param.20) | copy-start | bytes 3076
  0.7 5.4 %copy-start.7 = (f32[256]{0:T(256)S(1)}, f32[256]{0:T(256)}, u32[]{:S(2)}) copy-start(f32[256]{0:T(256)} %param.21) | copy-start | bytes 3076
  0.7 5.4 %copy-start.8 = (f32[256]{0:T(256)S(1)}, f32[256]{0:T(256)}, u32[]{:S(2)}) copy-start(f32[256]{0:T(256)} %param.27) | copy-start | bytes 3076
  0.8 5.4 %copy-start.9 = (f32[256]{0:T(256)S(1)}, f32[256]{0:T(256)}, u32[]{:S(2)}) copy-start(f32[256]{0:T(256)} %param.28) | copy-start | bytes 3076
  320.1 1.6 copy-start
  321.7 1.0 copy-start.1
  322.7 1.2 copy-start.2
  323.9 8.5 %copy-start.3 = (bf16[4096,256]{1,0:T(8,128)(2,1)S(1)}, bf16[4096,256]{1,0:T(8,128)(2,1)}, u32[]{:S(2)}) copy-start(bf16[4096,256]{1,0:T(8,128)(2,1)} %get-tuple-element.104) | copy-start | bytes 6291460

commit v6 on v5

--- a/solution.py
+++ b/solution.py
@@ -31,8 +31,7 @@
         second = [(1 << b, 1 - b % 2) for b in range(self.bits)]
         self.m_near = first + second
         rest = [(r, f) for r in self.far for f in (0, 1)]
-        mixed = [u for k in range(max(len(second), len(rest))) for u in second[k : k + 1] + rest[k : k + 1]]
-        self.m_units = [(0, 0), (0, 1)] + first + mixed
+        self.m_units = [(0, 0), (0, 1)] + first + rest[:1] + second + rest[1:]
         self.m_pos = {u: k for k, u in enumerate(self.m_units)}
 
     def children(self, r, f):
@@ -57,7 +56,7 @@
         seen = set()
         holders = {True: [None] * SUM_BUFFERS, False: [None] * SUM_BUFFERS}
         turns = {True: 0, False: 0}
-        waiting = sorted(done, key=lambda u: done[u])
+        waiting = sorted(done, key=lambda u: (done[u], len(kids[u])))
         held = None
         point = 0
         while waiting or held is not None:
@@ -145,7 +144,7 @@
     return jnp.where(low, both[:BLOCK], both[BLOCK:])
 
 
-INPUTS = ("tokens", "middle", "coarse", "cotangent", "a_own", "m_own", "params")
+INPUTS = ("tokens", "middle", "coarse", "cotangent", "attend_w", "output_w", "up_w", "down_w", "params")
 OUTPUTS = (
     "layer_out",
     "grad_rows",
@@ -262,20 +261,20 @@
         send("params", r, ref["params"], here, peer(r))
     own_params = local(0, ref["params"], ref["params_all"].at[:, columns(h, s_.kh)])
     own_params.start()
-    z_send("za", 0, ref["a_own"], ref["all_a"].at[0, z, c])
-    own_blocks = [(ref["a_own"], ref["all_a"].at[0, z, c])]
-    own_blocks += [(ref["m_own"].at[f], ref["all_m"].at[tree.m_pos[0, f], z, c]) for f in (0, 1)]
-    own_in = [local(1 + k, source, ref["acc"].at[k, 0]) for k, (source, _) in enumerate(own_blocks)]
-    own_out = [local(1 + k, ref["acc"].at[k, 0], to) for k, (_, to) in enumerate(own_blocks)]
-    for copy in own_in:
+    kh, n, tile, fs = s_.kh, s_.n, s_.tile, s_.fs
+    own_block = [ref["acc"].at[k, 0] for k in range(3)]
+    own_loads = [local(1 + k, ref["attend_w"].at[k], own_block[0].at[:, pl.ds(k * kh, kh)]) for k in range(3)]
+    own_loads.append(local(40, ref["output_w"], ref["out_in"]))
+    for f in (0, 1):
+        own_loads.append(local(41 + f, ref["up_w"].at[:, pl.ds(f * fs, fs)], own_block[1 + f].at[:, pl.ds(0, fs)]))
+    own_loads.append(local(43, ref["down_w"], ref["down_in"]))
+    for copy in own_loads:
         copy.start()
-
     def m_block(r, f):
         return ref["all_m"].at[tree.m_pos[r, f], z, c]
 
     far_units = [(r, f) for r in tree.far for f in (0, 1)]
 
-    kh, n, tile = s_.kh, s_.n, s_.tile
     rows_m, rows_c = n // 4, n // 16
     loads = {}
     order = list(range(1, s_.n_hid)) + [0]
@@ -289,6 +288,18 @@
         loads[r] = [local(4 + 3 * r + k, *pair) for k, pair in enumerate(sources)]
         for copy in loads[r]:
             copy.start()
+    for copy in own_loads:
+        copy.wait()
+    ref["acc"][0, 0, :, pl.ds(3 * kh, kh)] = ref["out_in"][...].T
+    z_send("za", 0, own_block[0], ref["all_a"].at[0, z, c])
+    for f in (0, 1):
+        ref["acc"][1 + f, 0, :, pl.ds(fs, fs)] = ref["down_in"][pl.ds(f * fs, fs), :].T
+    for r, f in far_units:
+        send("fs", tree.m_pos[r, f], own_block[1 + f], m_block(r, f), peer(r))
+    own_places = [ref["all_a"].at[0, z, c], m_block(0, 0), m_block(0, 1)]
+    own_out = [local(1 + k, own_block[k], place) for k, place in enumerate(own_places)]
+    for store in own_out:
+        store.start()
     repeat_4, repeat_16 = repeat_matrix(tile, 4), repeat_matrix(tile, 16)
 
     def xs_rows(i, j):
@@ -314,9 +325,6 @@
                 copy.start()
                 own_xs.append(copy)
 
-    for load, store in zip(own_in, own_out, strict=True):
-        load.wait()
-        store.start()
 
     def to_sibling(kind, r, f):
         k = tree.pos[r, f] if kind == "a" else tree.m_pos[r, f]
@@ -344,7 +352,10 @@
         store.wait()
     z_arrived("za", 0, ref["all_a"].at[0, z, c])
     for f in (0, 1):
-        z_send("zm", f, ref["m_own"].at[f], m_block(0, f))
+        z_send("zm", f, own_block[1 + f], m_block(0, f))
+    for r, f in far_units:
+        arrived("fs", tree.m_pos[r, f], m_block(r, f))
+        z_send("zf", tree.m_pos[r, f], m_block(r, f), m_block(r, f))
     for r, f in a_near:
         send("ax", tree.pos[r, f], a_part(0, f, c), a_part(r, f, c), peer(r))
     for f in (0, 1):
@@ -473,6 +484,11 @@
         z_arrived("zm", f, m_block(0, f))
     for f in (0, 1):
         to_sibling("m", 0, f)
+    z_left("za", 0, own_block[0])
+    for f in (0, 1):
+        z_left("zm", f, own_block[1 + f])
+    for r, f in far_units:
+        left("fs", tree.m_pos[r, f], own_block[1 + f])
 
     def mix(i, _):
         rows = pl.ds(pl.multiple_of(i * tile, tile), tile)
@@ -492,8 +508,8 @@
     own_ct.wait()
     for k in range(1, s_.n_hid):
         arrived("ct", k, cot_rows(h))
-    for r, f in far_units:
-        send("fs", tree.m_pos[r, f], ref["m_own"].at[f], m_block(r, f), peer(r))
+    for r, f in tree.m_near:
+        send("mx", tree.m_pos[r, f], m_part(0, f, c), m_part(r, f, c), peer(r))
     for i in range(s_.tiles):
         rows = pl.ds(i * tile, tile)
         ref["n2_t"][:, rows] = ref["n2"][rows, :].T
@@ -671,7 +687,6 @@
     def stage_free(kind, index, slot):
         stage_copies(kind, index, slot)[1].wait_send()
 
-    fs = s_.fs
     for k in (0, 1):
         take_sibling("m", *tree.m_units[k])
     weight_load(0, ref["all_m"].at[0]).start()
@@ -703,16 +718,13 @@
 
         lax.fori_loop(0, n // big, rows_of, 0)
 
-        @pl.when(step == 0)
-        def _():
-            for r, f in far_units:
-                arrived("fs", tree.m_pos[r, f], m_block(r, f))
-                z_send("zf", tree.m_pos[r, f], m_block(r, f), m_block(r, f))
-            for r, f in tree.m_near:
-                send("mx", tree.m_pos[r, f], m_part(0, f, c), m_part(r, f, c), peer(r))
-
-        for k in range(1, n_units - 1):
-            pl.when(step == k)(functools.partial(take_m, *tree.m_units[k + 1]))
+        for k in range(1, n_units - 1, 2):
+
+            @pl.when(step == k)
+            def _(k=k):
+                for unit in tree.m_units[k + 1 : k + 3]:
+                    take_m(*unit)
+
 
         @pl.when(step >= 1)
         def _():
@@ -952,6 +964,10 @@
             total = total + ref["sum1"][r]
         ref["sum2"][0] = total
         send("sum2", 0, ref["sum2"].at[0], ref["sum2"].at[1], sibling)
+        arrived("sum2", 0, ref["sum2"].at[1])
+        ref["sum3"][0] = ref["sum2"][0] + ref["sum2"][1]
+        for step in range(1, s_.z):
+            send("sum3", step, ref["sum3"].at[0], ref["sum3"].at[step], z_peer(step))
 
     feed_done = False
     for point in range(last_point, plan.end):
@@ -960,14 +976,11 @@
             first_finals()
             feed_done = True
         act(point)
+        if ("a", 0, 1) in units:
+            first_sums()
     if not feed_done:
         first_finals()
 
-    first_sums()
-    arrived("sum2", 0, ref["sum2"].at[1])
-    ref["sum3"][0] = ref["sum2"][0] + ref["sum2"][1]
-    for step in range(1, s_.z):
-        send("sum3", step, ref["sum3"].at[0], ref["sum3"].at[step], z_peer(step))
     final(2)
     final(3)
     total = ref["sum3"][0]
@@ -999,9 +1012,6 @@
     left("sum2", 0, ref["sum2"].at[0])
     for step in range(1, s_.z):
         left("sum3", step, ref["sum3"].at[0])
-    z_left("za", 0, ref["a_own"])
-    for f in (0, 1):
-        z_left("zm", f, ref["m_own"].at[f])
     for r, f in tree.units:
         left("ac", tree.pos[r, f], a_part(r, f, c))
         if r:
@@ -1011,7 +1021,6 @@
     for r, f in tree.m_near:
         left("mx", tree.m_pos[r, f], m_part(r, f, c))
     for r, f in far_units:
-        left("fs", tree.m_pos[r, f], m_block(r, f))
         z_left("zf", tree.m_pos[r, f], m_block(r, f))
     for k in range(max(0, s_.n_hid - 2), s_.n_hid):
         stage_free("a", s_.n_hid - 1 - k, 2 + k % 2)
@@ -1037,6 +1046,8 @@
         "facc": ((s_.n, s_.d), F32),
         "gacc": ((s_.n, s_.d), F32),
         "wa": ((s_.n_hid, s_.z, 2, s_.tb, s_.wide), BF16),
+        "out_in": ((s_.kh, s_.tb), BF16),
+        "down_in": ((2 * s_.fs, s_.tb), BF16),
         "hid": ((s_.n, s_.fs), BF16),
         "gb": ((s_.n, s_.fs), BF16),
         "acc": ((SUM_BUFFERS + 1, s_.z, s_.tb, s_.wide), BF16),
@@ -1084,7 +1095,9 @@
     return out
 
 
-def finish_kernel(kh, fs, grad_ref, a_ref, m_ref, tokens_ref, middle_ref, coarse_ref, output_ref, up_ref, down_ref):
+def finish_kernel(
+    kh, fs, grad_ref, a_ref, m_ref, tokens_ref, middle_ref, coarse_ref, output_ref, up_ref, down_ref, attend_ref
+):
     grad = grad_ref[...]
     rows = grad.shape[0]
     part = min(512, rows)
@@ -1098,6 +1111,8 @@
     @pl.when(pl.program_id(0) == 0)
     def _():
         output_ref[...] = a_ref[:, pl.ds(3 * kh, kh)].T
+        for k in range(3):
+            attend_ref[k] = a_ref[:, pl.ds(k * kh, kh)]
         for f in (0, 1):
             up_ref[:, pl.ds(f * fs, fs)] = m_ref[f, :, pl.ds(0, fs)]
             down_ref[pl.ds(f * fs, fs), :] = m_ref[f, :, pl.ds(fs, fs)].T
@@ -1107,7 +1122,7 @@
     positions, features = grad.shape
     rows = min(1024, positions)
     tb, fs = size.tb, size.fs
-    whole = [((features, tb), F32), ((tb, 2 * fs), F32), ((2 * fs, tb), F32)]
+    whole = [((features, tb), F32), ((tb, 2 * fs), F32), ((2 * fs, tb), F32), ((3, tb, features), F32)]
     return pl.pallas_call(
         functools.partial(finish_kernel, features, fs),
         grid=(positions // rows,),
@@ -1117,10 +1132,10 @@
             pl.BlockSpec(grad_m.shape, lambda i: (0, 0, 0)),
         ],
         out_specs=[pl.BlockSpec((rows // t, features), lambda i: (i, 0)) for t in (1, 4, 16)]
-        + [pl.BlockSpec(shape, lambda i: (0, 0)) for shape, _ in whole],
+        + [pl.BlockSpec(shape, lambda i, n=len(shape): (0,) * n) for shape, _ in whole],
         out_shape=[jax.ShapeDtypeStruct((positions // t, features), F32) for t in (1, 4, 16)]
         + [jax.ShapeDtypeStruct(*x) for x in whole],
-        compiler_params=pltpu.CompilerParams(vmem_limit_bytes=32 * 2**20),
+        compiler_params=pltpu.CompilerParams(vmem_limit_bytes=60 * 2**20),
         name="token_gradients",
     )(grad, grad_a, grad_m)
 
@@ -1151,13 +1166,6 @@
     size = Sizes(positions, features, d, ff, n_tok, n_hid)
     tree = Tree(n_hid)
     tb, fs, wide, z = size.tb, size.fs, size.wide, size.z
-    a_own = jnp.concatenate([attend_weight.reshape(tb, 3 * features), output_weight.T], axis=1)
-    m_own = jnp.stack(
-        [
-            jnp.concatenate([up_weight[:, f * fs : f * fs + fs], down_weight[f * fs : f * fs + fs].T], axis=1)
-            for f in (0, 1)
-        ]
-    )
     vectors = (first_gain, first_shift, second_gain, second_shift, query_bias, value_bias, mixer_bias, down_bias)
     params = jnp.concatenate(
         [
@@ -1197,9 +1205,19 @@
         ),
         cost_estimate=pl.CostEstimate(flops=80 * 10**9, bytes_accessed=2 * 10**8, transcendentals=10**7),
         name="layer",
-    )(tokens, middle_cond, coarse_cond, cotangent, a_own, m_own, params)
+    )(
+        tokens,
+        middle_cond,
+        coarse_cond,
+        cotangent,
+        attend_weight.transpose(1, 0, 2),
+        output_weight,
+        up_weight,
+        down_weight,
+        params,
+    )
     layer_out, grad_rows, grad_a, grad_m, small = results[:5]
-    grad_tokens, grad_middle, grad_coarse, grad_output, grad_up, grad_down = finish(
+    grad_tokens, grad_middle, grad_coarse, grad_output, grad_up, grad_down, grad_attend = finish(
         size, grad_rows, grad_a, grad_m
     )
     tok = lax.axis_index("tok")
@@ -1216,7 +1234,7 @@
         grad_coarse,
         mine[0],
         mine[1],
-        grad_a[:, : 3 * features].reshape(tb, 3, features),
+        grad_attend.transpose(1, 0, 2),
         mine[4],
         mine[5],
         grad_output,

time: 336 us -> 328 us (0.976)
  local copies, waits for them, and re-layouts: 14.8 us -> 6.64 us
    unnamed x36 -> x5, local copies, waits for them, and re-layouts: 8.26 us -> 2.03 us
where the time goes in v6:
time: 328 us; the launch traced here: 324 us
  Pallas kernels  317 us (97%)
  local copies, waits for them, and re-layouts  6.64 us (2%)
    pallas_call x1, Pallas kernels, shards(): pl.pallas_call(functools.partial(layer_kernel, size, tree), out_shape=[ja...  311 us

profile of v6, /device:TPU:8, one launch (start us, length us, event | category | flops | bytes accessed | tf_op | source)
XLA Modules:
  0.0 324.4 jit_solution(6019768745129845550)
XLA Ops:
  0.7 0.7 reshape.40
  1.4 2.0 concatenate.3.refs_8_
  3.4 310.7 %layer.1 = (bf16[4096,256]{1,0:T(8,128)(2,1)}, bf16[4096,256]{1,0:T(8,128)(2,1)}, f32[128,1024]{1,0:T(8,128)}, f32[2,128,1024]{2,1,0:T(8,128)}, f32[16,256]{1,0:...) custom-call(bf16[4096,256]{1,0:T(8,128)(2,1)} %refs_0_.1, ...), custom_call_target="tpu_custom_call" | custom-call | flops 80000000000 | bytes 200000000 | tf_op jit(solution)/shard_map/layer/pallas_call | solution.py:1197
  314.1 0.0 copy-start
  314.1 6.3 %token_gradients.1 = (f32[4096,256]{1,0:T(8,128)}, f32[1024,256]{1,0:T(8,128)}, f32[256,256]{1,0:T(8,128)}, f32[256,128]{1,0:T(8,128)}, f32[128,1024]{1,0:T(8,12...) custom-call(bf16[4096,256]{1,0:T(8,128)(2,1)} %get-tuple-element.30.grad_ref, f32[128,1024]{1,0:T(8,128)} %get-tuple-element.31.a_ref, ...), custom_call_target="tpu_custom_call" | custom-call | tf_op jit(solution)/shard_map/token_gradients/pallas_call | solution.py:1126
  320.5 0.7 slice.30
  321.1 0.1 constant_dynamic-slice_fusion
  321.2 0.5 slice_bitcast_fusion.1
  321.8 0.7 slice_bitcast_fusion
  322.5 0.6 dynamic_slice.7
  323.1 0.0 copy-done
  323.1 1.3 copy.36
  (2 shorter events, 0.0 us)
Async XLA Ops:
  314.1 9.0 %copy-start = (bf16[4096,256]{1,0:T(8,128)(2,1)S(1)}, bf16[4096,256]{1,0:T(8,128)(2,1)}, u32[]{:S(2)}) copy-start(bf16[4096,256]{1,0:T(8,128)(2,1)} %get-tuple-element.66) | copy-start | bytes 6291460

commit v7 on v6

--- a/solution.py
+++ b/solution.py
@@ -15,7 +15,8 @@
 BF16 = jnp.bfloat16
 F32 = jnp.float32
 SMALL_ROWS = 16
-SUM_BUFFERS = 4
+WHOLE_BUFFERS = 3
+HALF_BUFFERS = 4
 
 
 class Tree:
@@ -54,7 +55,7 @@
         self.first = set()
         sent = {}
         seen = set()
-        holders = {True: [None] * SUM_BUFFERS, False: [None] * SUM_BUFFERS}
+        holders = {True: [None] * HALF_BUFFERS, False: [None] * WHOLE_BUFFERS}
         turns = {True: 0, False: 0}
         waiting = sorted(done, key=lambda u: (done[u], len(kids[u])))
         held = None
@@ -73,7 +74,7 @@
                 actions.append(("fetch", unit))
                 held = unit
                 pool = unit[0] == "a"
-                self.turn[unit] = k = turns[pool] % SUM_BUFFERS
+                self.turn[unit] = k = turns[pool] % len(holders[pool])
                 turns[pool] += 1
                 self.before[unit] = holders[pool][k]
                 holders[pool][k] = unit
@@ -401,7 +402,7 @@
 
     def put_rows(slot, zz, first, values):
         width = values.shape[1]
-        ref["wa"][slot, zz, :, :, pl.ds(first, width)] = values.reshape(2, s_.tb, width)
+        ref["wa"][slot, pl.ds(zz * 2, 2), :, :, pl.ds(first, width)] = values.reshape(2, 2, s_.tb, width)
 
     def cot_rows(j):
         return ref["ct"].at[:, columns(j, kh)]
@@ -563,7 +564,7 @@
         if unit[0] != "a":
             return ref["acc"].at[k]
         rows = pl.ds(k % 2 * s_.half, s_.half)
-        return ref["acc"].at[SUM_BUFFERS, :, rows] if k < 2 else spare(1, rows)
+        return ref["acc"].at[WHOLE_BUFFERS, :, rows] if k < 2 else spare(1, rows)
 
     def z_slot(kind, f, step):
         return ref["z_g" + kind].at[f, step]
@@ -690,7 +691,7 @@
     for k in (0, 1):
         take_sibling("m", *tree.m_units[k])
     weight_load(0, ref["all_m"].at[0]).start()
-    big = min(256, n)
+    big = min(512, n)
     gelu_scale = (2.0 / jnp.pi) ** 0.5
 
     def feed(step, _):
@@ -738,12 +739,13 @@
             stage_free("m", step - 2, stage)
 
         def grads(zz, _):
-            rows = pl.ds(pl.multiple_of(zz * (2 * s_.tb), 2 * s_.tb), 2 * s_.tb)
+            rows = pl.ds(pl.multiple_of(zz * (4 * s_.tb), 4 * s_.tb), 4 * s_.tb)
             put_rows(stage, zz, 0, dot(ref["n2_t"][rows, :], ref["gb"][...]).astype(BF16))
-            put_rows(stage, zz, fs, dot(ref["ct_t"][zz].reshape(2 * s_.tb, n), ref["hid"][...]).astype(BF16))
+            upstream = ref["ct_t"][pl.ds(zz * 2, 2)].reshape(4 * s_.tb, n)
+            put_rows(stage, zz, fs, dot(upstream, ref["hid"][...]).astype(BF16))
             return 0
 
-        lax.fori_loop(0, s_.z // 2, grads, 0)
+        lax.fori_loop(0, s_.z // 4, grads, 0)
         for k in range(n_units - 1):
 
             def load_next(k=k):
@@ -752,7 +754,7 @@
                 weight_load((k + 1) % 2, ref["all_m"].at[k + 1]).start()
 
             pl.when(step == k)(load_next)
-        lax.fori_loop(s_.z // 2, s_.z, grads, 0)
+        lax.fori_loop(s_.z // 4, s_.z // 2, grads, 0)
         stage_out("m", step, stage)
         loop_point(step, 0, 2, 1, n_units)
         return 0
@@ -788,8 +790,7 @@
         ref["n2_t"][:, rows] = ref["nrm"][rows, :].T
     act(mlp_points + 1)
     for r in range(1, s_.n_hid):
-        j = block_of(r)
-        send("lo", r, ref["n2"].at[:, columns(j, kh)], out_rows("layer_out", h), peer(r))
+        send("lo", r, ref["n2"].at[:, columns(block_of(r), kh)], out_rows("layer_out", h), peer(r))
     own_lo = local(0, ref["n2"].at[:, columns(h, kh)], out_rows("layer_out", h))
     own_lo.start()
     for k in range(n_units - 2, n_units):
@@ -849,12 +850,12 @@
         cols = columns(block_of(r), kh)
 
         def grads(zz, _):
-            rows = pl.ds(pl.multiple_of(zz * (2 * s_.tb), 2 * s_.tb), 2 * s_.tb)
+            rows = pl.ds(pl.multiple_of(zz * (4 * s_.tb), 4 * s_.tb), 4 * s_.tb)
             put_rows(stage, zz, 0, dot(ref["nrm_t"][rows, :], ref["pj"][r]).astype(BF16))
             put_rows(stage, zz, 3 * kh, dot(ref["n2_t"][rows, :], ref["att"][r]).astype(BF16))
             return 0
 
-        lax.fori_loop(0, s_.z, grads, 0)
+        lax.fori_loop(0, s_.z // 2, grads, 0)
         stage_out("a", r, stage)
         loop_point(step, chunk_points, 4, 2, s_.n_hid)
 
@@ -1050,7 +1051,7 @@
         "down_in": ((2 * s_.fs, s_.tb), BF16),
         "hid": ((s_.n, s_.fs), BF16),
         "gb": ((s_.n, s_.fs), BF16),
-        "acc": ((SUM_BUFFERS + 1, s_.z, s_.tb, s_.wide), BF16),
+        "acc": ((WHOLE_BUFFERS + 1, s_.z, s_.tb, s_.wide), BF16),
         "tmp": ((s_.z, s_.tb, s_.wide), BF16),
         "hidden_bias": ((units, 1, s_.fs), F32),
         "hidden_sum": ((units, 1, s_.fs), F32),
@@ -1224,9 +1225,10 @@
     share = features // n_tok
     mine = lax.dynamic_slice_in_dim(small[:8], tok * share, share, 1)
     hidden_share = fs * 2 // n_tok
-    grad_hidden_bias = lax.dynamic_slice_in_dim(
-        small[8 : 8 + ff // d].reshape(-1), tok * hidden_share, hidden_share, 0
-    )
+    first = tok * hidden_share
+    grad_hidden_bias = lax.dynamic_slice(
+        small, (8 + first // features, lax.rem(first, features)), (1, hidden_share)
+    ).reshape(hidden_share)
     return (
         layer_out,
         grad_tokens,

time: 328 us -> 324 us (0.988)
  Pallas kernels: 317 us -> 312 us
    pallas_call x1, Pallas kernels: 311 us -> 306 us  [shards(): pl.pallas_call(functools.partial(layer_kernel, size, tree), out_shape=[ja...]
where the time goes in v7:
time: 324 us; the launch traced here: 320 us
  Pallas kernels  312 us (96%)
  local copies, waits for them, and re-layouts  6.61 us (2%)
    pallas_call x1, Pallas kernels, shards(): pl.pallas_call(functools.partial(layer_kernel, size, tree), out_shape=[ja...  306 us

profile of v7, /device:TPU:8, one launch (start us, length us, event | category | flops | bytes accessed | tf_op | source)
XLA Modules:
  0.0 319.5 jit_solution(332319964990235207)
XLA Ops:
  0.7 0.7 reshape.40
  1.4 2.0 concatenate.3.refs_8_
  3.4 305.9 %layer.1 = (bf16[4096,256]{1,0:T(8,128)(2,1)}, bf16[4096,256]{1,0:T(8,128)(2,1)}, f32[128,1024]{1,0:T(8,128)}, f32[2,128,1024]{2,1,0:T(8,128)}, f32[16,256]{1,0:...) custom-call(bf16[4096,256]{1,0:T(8,128)(2,1)} %refs_0_.1, ...), custom_call_target="tpu_custom_call" | custom-call | flops 80000000000 | bytes 200000000 | tf_op jit(solution)/shard_map/layer/pallas_call | solution.py:1198
  309.3 0.0 copy-start
  309.3 6.3 %token_gradients.1 = (f32[4096,256]{1,0:T(8,128)}, f32[1024,256]{1,0:T(8,128)}, f32[256,256]{1,0:T(8,128)}, f32[256,128]{1,0:T(8,128)}, f32[128,1024]{1,0:T(8,12...) custom-call(bf16[4096,256]{1,0:T(8,128)(2,1)} %get-tuple-element.30.grad_ref, f32[128,1024]{1,0:T(8,128)} %get-tuple-element.31.a_ref, ...), custom_call_target="tpu_custom_call" | custom-call | tf_op jit(solution)/shard_map/token_gradients/pallas_call | solution.py:1127
  315.6 0.7 slice.27
  316.3 0.1 constant_dynamic-slice_fusion
  316.4 0.5 slice_bitcast_fusion
  316.9 1.3 dynamic-slice_bitcast_fusion
  318.2 0.0 copy-done
  318.2 1.3 copy.35
  (1 shorter events, 0.0 us)
Async XLA Ops:
  309.3 8.9 %copy-start = (bf16[4096,256]{1,0:T(8,128)(2,1)S(1)}, bf16[4096,256]{1,0:T(8,128)(2,1)}, u32[]{:S(2)}) copy-start(bf16[4096,256]{1,0:T(8,128)(2,1)} %get-tuple-element.66) | copy-start | bytes 6291460

commit v8 on v7

--- a/solution.py
+++ b/solution.py
@@ -55,9 +55,9 @@
         self.first = set()
         sent = {}
         seen = set()
-        holders = {True: [None] * HALF_BUFFERS, False: [None] * WHOLE_BUFFERS}
-        turns = {True: 0, False: 0}
-        waiting = sorted(done, key=lambda u: (done[u], len(kids[u])))
+        holders = {True: [None] * HALF_BUFFERS, False: [None] * (WHOLE_BUFFERS + 1)}
+        turns = {True: -1, False: -1}
+        waiting = sorted(done, key=lambda u: (u[0] != "a", done[u], len(kids[u])))
         held = None
         point = 0
         while waiting or held is not None:
@@ -74,10 +74,13 @@
                 actions.append(("fetch", unit))
                 held = unit
                 pool = unit[0] == "a"
-                self.turn[unit] = k = turns[pool] % len(holders[pool])
-                turns[pool] += 1
+                size = HALF_BUFFERS if pool else WHOLE_BUFFERS + (turns[True] < 0)
+                self.turn[unit] = k = turns[pool] = (turns[pool] + 1) % size
                 self.before[unit] = holders[pool][k]
                 holders[pool][k] = unit
+                if pool and k == 2 and holders[False][-1]:
+                    self.before[unit] = holders[False][-1]
+                    holders[False][-1] = None
                 if unit[:2] not in seen:
                     self.first.add(unit)
                 seen.add(unit[:2])
@@ -145,7 +148,8 @@
     return jnp.where(low, both[:BLOCK], both[BLOCK:])
 
 
-INPUTS = ("tokens", "middle", "coarse", "cotangent", "attend_w", "output_w", "up_w", "down_w", "params")
+INPUTS = ("tokens", "middle", "coarse", "cotangent", "attend_w", "output_w", "up_w", "down_w")
+VECTORS = 8
 OUTPUTS = (
     "layer_out",
     "grad_rows",
@@ -176,6 +180,7 @@
         self.tb = d // n_tok
         self.half = self.tb // 2
         self.wide = 4 * features
+        self.vector_rows = ff // d
         self.pairs = features // PAIR
         self.tile = min(256, self.n)
         self.tiles = self.n // self.tile
@@ -184,7 +189,8 @@
 
 
 def layer_kernel(size, tree, *refs):
-    names = list(INPUTS) + list(OUTPUTS) + list(scratch(size, tree))
+    vectors = [f"vector_{k}" for k in range(VECTORS + 1)]
+    names = list(INPUTS) + vectors + list(OUTPUTS) + list(scratch(size, tree))
     ref = dict(zip(names, refs, strict=True))
     s_ = size
     n_units = len(tree.units)
@@ -257,11 +263,13 @@
 
     part = {"a": a_part, "m": m_part}
 
-    for r in range(1, s_.n_hid):
-        here = ref["params_all"].at[:, columns(h, s_.kh)]
-        send("params", r, ref["params"], here, peer(r))
-    own_params = local(0, ref["params"], ref["params_all"].at[:, columns(h, s_.kh)])
-    own_params.start()
+    ref["sum2"][0] = jnp.zeros((SMALL_ROWS, s_.kh), F32)
+    vector_loads = [
+        local(44 + k, ref[name], ref["sum2"].at[0, pl.ds(k, s_.vector_rows if k == VECTORS else 1)])
+        for k, name in enumerate(vectors)
+    ]
+    for copy in vector_loads:
+        copy.start()
     kh, n, tile, fs = s_.kh, s_.n, s_.tile, s_.fs
     own_block = [ref["acc"].at[k, 0] for k in range(3)]
     own_loads = [local(1 + k, ref["attend_w"].at[k], own_block[0].at[:, pl.ds(k * kh, kh)]) for k in range(3)]
@@ -271,6 +279,13 @@
     own_loads.append(local(43, ref["down_w"], ref["down_in"]))
     for copy in own_loads:
         copy.start()
+    for copy in vector_loads:
+        copy.wait()
+    own_params = local(0, ref["sum2"].at[0], ref["params_all"].at[:, columns(h, s_.kh)])
+    own_params.start()
+    for r in range(1, s_.n_hid):
+        send("params", r, ref["sum2"].at[0], ref["params_all"].at[:, columns(h, s_.kh)], peer(r))
+
     def m_block(r, f):
         return ref["all_m"].at[tree.m_pos[r, f], z, c]
 
@@ -365,6 +380,7 @@
     own_params.wait()
     for r in range(1, s_.n_hid):
         arrived("params", r, ref["params_all"].at[:, columns(h, kh)])
+        left("params", r, ref["sum2"].at[0])
 
     def gain_row(k):
         return ref["params_all"][pl.ds(k, 1), :]
@@ -519,12 +535,12 @@
         add_sum(7, upstream.astype(F32))
         ref["gacc"][rows, :] = jnp.zeros((tile, s_.d), F32)
 
-    mlp_points = 2 * n_units
+    mlp_points = 3 * n_units
     chunk_points = mlp_points + 2
-    last_point = chunk_points + 4 * s_.n_hid
+    last_point = chunk_points + 5 * s_.n_hid
     done, kids = {}, {}
     for k, (r, f) in enumerate(tree.m_units):
-        done["m", r, f] = 2 * k + 1
+        done["m", r, f] = 3 * k + 2
         kids["m", r, f] = [("m", u, f) for u in tree.near] if r == 0 else []
         if r == 0:
             done["m", r, f] = mlp_points - 1
@@ -533,9 +549,9 @@
         kids["fold", r, f] = [("m", r, f)]
     for r in range(s_.n_hid):
         for f in (0, 1):
-            done["a", r, f] = chunk_points + 4 * (s_.n_hid - 1 - r) + 3
+            done["a", r, f] = chunk_points + 5 * (s_.n_hid - 1 - r) + 4
             kids["a", r, f] = [("a", child, f) for child, _ in tree.children(r, f)]
-    plan = Schedule(done, kids, {"m": 11, "a": 4, "fold": 9}, last_point)
+    plan = Schedule(done, kids, {"m": 14, "a": 7, "fold": 10}, last_point)
 
     def place(kind, r, f):
         return tree.pos[r, f] if kind == "a" else tree.m_pos[r, f]
@@ -564,7 +580,7 @@
         if unit[0] != "a":
             return ref["acc"].at[k]
         rows = pl.ds(k % 2 * s_.half, s_.half)
-        return ref["acc"].at[WHOLE_BUFFERS, :, rows] if k < 2 else spare(1, rows)
+        return spare(1, rows) if k < 2 else ref["acc"].at[WHOLE_BUFFERS, :, rows]
 
     def z_slot(kind, f, step):
         return ref["z_g" + kind].at[f, step]
@@ -717,7 +733,14 @@
             ref["hidden_sum"][step] = ref["hidden_sum"][step] + row_sum(grad_before.astype(F32))
             return 0
 
-        lax.fori_loop(0, n // big, rows_of, 0)
+        lax.fori_loop(0, n // big // 2, rows_of, 0)
+
+        @pl.when(step >= 1)
+        def _():
+            stage_kept("m", step - 1, 3 - slot)
+
+        loop_point(step, 0, 3, 0, n_units)
+        lax.fori_loop(n // big // 2, n // big, rows_of, 0)
 
         for k in range(1, n_units - 1, 2):
 
@@ -727,11 +750,7 @@
                     take_m(*unit)
 
 
-        @pl.when(step >= 1)
-        def _():
-            stage_kept("m", step - 1, 3 - slot)
-
-        loop_point(step, 0, 2, 0, n_units)
+        loop_point(step, 0, 3, 1, n_units)
         stage = 2 + slot
 
         @pl.when(step >= 2)
@@ -756,7 +775,7 @@
             pl.when(step == k)(load_next)
         lax.fori_loop(s_.z // 4, s_.z // 2, grads, 0)
         stage_out("m", step, stage)
-        loop_point(step, 0, 2, 1, n_units)
+        loop_point(step, 0, 3, 2, n_units)
         return 0
 
     lax.fori_loop(0, n_units, feed, 0)
@@ -817,7 +836,7 @@
         def _():
             stage_kept("a", r + 1, 3 - slot)
 
-        loop_point(step, chunk_points, 4, 0, s_.n_hid)
+        loop_point(step, chunk_points, 5, 0, s_.n_hid)
 
         def pull_attention(i, _):
             rows = pl.ds(pl.multiple_of(i * BLOCK, BLOCK), BLOCK)
@@ -840,8 +859,10 @@
             pull_attention(2 * i, 0)
             return pull_attention(2 * i + 1, 0)
 
-        lax.fori_loop(0, s_.blocks // 2, pull_two, 0)
-        loop_point(step, chunk_points, 4, 1, s_.n_hid)
+        lax.fori_loop(0, s_.blocks // 4, pull_two, 0)
+        loop_point(step, chunk_points, 5, 1, s_.n_hid)
+        lax.fori_loop(s_.blocks // 4, s_.blocks // 2, pull_two, 0)
+        loop_point(step, chunk_points, 5, 2, s_.n_hid)
 
         @pl.when(step >= 2)
         def _():
@@ -857,7 +878,7 @@
 
         lax.fori_loop(0, s_.z // 2, grads, 0)
         stage_out("a", r, stage)
-        loop_point(step, chunk_points, 4, 2, s_.n_hid)
+        loop_point(step, chunk_points, 5, 3, s_.n_hid)
 
         def pull_rows(i, _):
             rows = pl.ds(pl.multiple_of(i * tile, tile), tile)
@@ -872,7 +893,7 @@
         def _():
             lax.fori_loop(0, s_.tiles, pull_rows, 0)
 
-        loop_point(step, chunk_points, 4, 3, s_.n_hid)
+        loop_point(step, chunk_points, 5, 4, s_.n_hid)
         return 0
 
     lax.fori_loop(0, s_.n_hid, back_chunk, 0)
@@ -898,10 +919,10 @@
         source = ref["ct"].at[pl.ds(i * tile, tile), columns(block_of(r), kh)]
         return source, ref["grad_rows"].at[pl.ds(pl.multiple_of(h * n + i * tile, tile), tile)]
 
-    def send_rows(i):
-        for r in range(1, s_.n_hid):
-            send("gt", i * s_.n_hid + r, *row_copy(i, r), peer(r))
-        local(41 + i, *row_copy(i, 0)).start()
+    def send_rows(blocks):
+        for i in range(s_.tiles):
+            for r in blocks:
+                send("gt", i * s_.n_hid + r, *row_copy(i, r), peer(r))
 
     for i in range(s_.tiles):
         back_one(i)
@@ -912,8 +933,9 @@
             ]
     for r in range(1, s_.n_hid):
         send("sum1", r, ref["sums"].at[:, columns(block_of(r), kh)], ref["sum1"].at[r], peer(r))
+    send_rows(tree.near)
     for i in range(s_.tiles):
-        send_rows(i)
+        local(41 + i, *row_copy(i, 0)).start()
 
     finals = [("m", 0), ("m", 1), ("a", 0), ("a", 1)]
 
@@ -965,6 +987,8 @@
             total = total + ref["sum1"][r]
         ref["sum2"][0] = total
         send("sum2", 0, ref["sum2"].at[0], ref["sum2"].at[1], sibling)
+
+    def second_sums():
         arrived("sum2", 0, ref["sum2"].at[1])
         ref["sum3"][0] = ref["sum2"][0] + ref["sum2"][1]
         for step in range(1, s_.z):
@@ -976,9 +1000,13 @@
         if not feed_done and units and units[0][:2] == ("a", 0):
             first_finals()
             feed_done = True
-        act(point)
+        for verb, unit in plan.at.get(point, ()):
+            if verb == "fetch" and unit == ("a", 0, 1):
+                first_sums()
+            (fetch if verb == "fetch" else finish)(unit)
         if ("a", 0, 1) in units:
-            first_sums()
+            send_rows(tree.far)
+            second_sums()
     if not feed_done:
         first_finals()
 
@@ -1006,7 +1034,6 @@
             left("gt", i * s_.n_hid + r, source)
     for r in range(1, s_.n_hid):
         arrived("lo", r, out_rows("layer_out", h))
-        left("params", r, ref["params"])
         left("ct", r, cot_rows(h))
         left("lo", r, cot_rows(h))
         left("sum1", r, ref["sum1"].at[r])
@@ -1090,7 +1117,7 @@
     for name, count in pairs.items():
         out[name + "_s"] = pltpu.SemaphoreType.DMA((count,))
         out[name + "_r"] = pltpu.SemaphoreType.DMA((count,))
-    out["local"] = pltpu.SemaphoreType.DMA((48,))
+    out["local"] = pltpu.SemaphoreType.DMA((64,))
     out["wload"] = pltpu.SemaphoreType.DMA((s_.n_hid,))
     out["keep"] = pltpu.SemaphoreType.DMA((2,))
     return out
@@ -1121,7 +1148,7 @@
 
 def finish(size, grad, grad_a, grad_m):
     positions, features = grad.shape
-    rows = min(1024, positions)
+    rows = min(2048, positions)
     tb, fs = size.tb, size.fs
     whole = [((features, tb), F32), ((tb, 2 * fs), F32), ((2 * fs, tb), F32), ((3, tb, features), F32)]
     return pl.pallas_call(
@@ -1168,13 +1195,7 @@
     tree = Tree(n_hid)
     tb, fs, wide, z = size.tb, size.fs, size.wide, size.z
     vectors = (first_gain, first_shift, second_gain, second_shift, query_bias, value_bias, mixer_bias, down_bias)
-    params = jnp.concatenate(
-        [
-            jnp.stack(vectors),
-            hidden_bias.reshape(ff // d, features),
-            jnp.zeros((SMALL_ROWS - 8 - ff // d, features), F32),
-        ]
-    )
+    rows = [v.reshape(1, features) for v in vectors] + [hidden_bias.reshape(ff // d, features)]
     units = len(tree.units)
     outputs = {
         "layer_out": ((positions, features), BF16),
@@ -1198,7 +1219,7 @@
     results = pl.pallas_call(
         functools.partial(layer_kernel, size, tree),
         out_shape=[jax.ShapeDtypeStruct(*outputs[name]) for name in OUTPUTS],
-        in_specs=[hbm] * len(INPUTS),
+        in_specs=[hbm] * (len(INPUTS) + len(rows)),
         out_specs=[hbm] * len(OUTPUTS),
         scratch_shapes=list(scratch(size, tree).values()),
         compiler_params=pltpu.CompilerParams(
@@ -1215,7 +1236,7 @@
         output_weight,
         up_weight,
         down_weight,
-        params,
+        *rows,
     )
     layer_out, grad_rows, grad_a, grad_m, small = results[:5]
     grad_tokens, grad_middle, grad_coarse, grad_output, grad_up, grad_down, grad_attend = finish(

time: 324 us -> 320 us (0.988)
  no operation moved by 1% of the time
where the time goes in v8:
time: 320 us; the launch traced here: 318 us
  Pallas kernels  312 us (98%)
  local copies, waits for them, and re-layouts  5.18 us (2%)
    pallas_call x1, Pallas kernels, shards(): pl.pallas_call(functools.partial(layer_kernel, size, tree), out_shape=[ja...  307 us

profile of v8, /device:TPU:8, one launch (start us, length us, event | category | flops | bytes accessed | tf_op | source)
XLA Modules:
  0.0 318.2 jit_solution(17598941929477006736)
XLA Ops:
  0.7 1.3 reshape.72.refs_16_
  1.9 306.9 %layer.1 = (bf16[4096,256]{1,0:T(8,128)(2,1)}, bf16[4096,256]{1,0:T(8,128)(2,1)}, f32[128,1024]{1,0:T(8,128)}, f32[2,128,1024]{2,1,0:T(8,128)}, f32[16,256]{1,0:...) custom-call(bf16[4096,256]{1,0:T(8,128)(2,1)} %refs_0_.1, ...), custom_call_target="tpu_custom_call" | custom-call | flops 80000000000 | bytes 200000000 | tf_op jit(solution)/shard_map/layer/pallas_call | solution.py:1219
  308.8 0.0 copy-start
  308.8 5.4 %token_gradients.1 = (f32[4096,256]{1,0:T(8,128)}, f32[1024,256]{1,0:T(8,128)}, f32[256,256]{1,0:T(8,128)}, f32[256,128]{1,0:T(8,128)}, f32[128,1024]{1,0:T(8,12...) custom-call(bf16[4096,256]{1,0:T(8,128)(2,1)} %get-tuple-element.30.grad_ref, f32[128,1024]{1,0:T(8,128)} %get-tuple-element.31.a_ref, ...), custom_call_target="tpu_custom_call" | custom-call | tf_op jit(solution)/shard_map/token_gradients/pallas_call | solution.py:1154
  314.3 0.7 slice.27
  315.0 0.1 constant_dynamic-slice_fusion
  315.0 0.5 slice_bitcast_fusion
  315.6 1.3 dynamic-slice_bitcast_fusion
  316.8 0.0 copy-done
  316.8 1.3 copy.35
Async XLA Ops:
  308.8 8.0 %copy-start = (bf16[4096,256]{1,0:T(8,128)(2,1)S(1)}, bf16[4096,256]{1,0:T(8,128)(2,1)}, u32[]{:S(2)}) copy-start(bf16[4096,256]{1,0:T(8,128)(2,1)} %get-tuple-element.66) | copy-start | bytes 6291460

commit v9 on v8

--- a/solution.py
+++ b/solution.py
@@ -846,7 +846,8 @@
                 attention = ref["probs"][r, p, rows, :]
                 weights = attention.astype(F32)
                 grad_attention = dot_t(grad, two_heads(value))
-                centre = spread(halves(weights * grad_attention, row_add))
+                shares = zip(halves(weights * grad_attention, row_add), halves(weights, row_add), strict=True)
+                centre = spread([part / whole for part, whole in shares])
                 grad_scores = (weights * (grad_attention - centre) * HEAD ** (-0.5)).astype(BF16)
                 grad_query = dot(grad_scores, two_heads(key))
                 grad_key = pick_heads(dot_l(grad_scores, query))

time: 320 us -> 320 us (level)
  no operation moved by 1% of the time
where the time goes in v9:
time: 320 us; the launch traced here: 318 us
  Pallas kernels  312 us (98%)
  local copies, waits for them, and re-layouts  5.18 us (2%)
    pallas_call x1, Pallas kernels, shards(): pl.pallas_call(functools.partial(layer_kernel, size, tree), out_shape=[ja...  307 us

profile of v9, /device:TPU:8, one launch (start us, length us, event | category | flops | bytes accessed | tf_op | source)
XLA Modules:
  0.0 318.2 jit_solution(4910384593765589726)
XLA Ops:
  0.7 1.3 reshape.72.refs_16_
  1.9 306.9 %layer.1 = (bf16[4096,256]{1,0:T(8,128)(2,1)}, bf16[4096,256]{1,0:T(8,128)(2,1)}, f32[128,1024]{1,0:T(8,128)}, f32[2,128,1024]{2,1,0:T(8,128)}, f32[16,256]{1,0:...) custom-call(bf16[4096,256]{1,0:T(8,128)(2,1)} %refs_0_.1, ...), custom_call_target="tpu_custom_call" | custom-call | flops 80000000000 | bytes 200000000 | tf_op jit(solution)/shard_map/layer/pallas_call | solution.py:1220
  308.8 0.0 copy-start
  308.8 5.4 %token_gradients.1 = (f32[4096,256]{1,0:T(8,128)}, f32[1024,256]{1,0:T(8,128)}, f32[256,256]{1,0:T(8,128)}, f32[256,128]{1,0:T(8,128)}, f32[128,1024]{1,0:T(8,12...) custom-call(bf16[4096,256]{1,0:T(8,128)(2,1)} %get-tuple-element.30.grad_ref, f32[128,1024]{1,0:T(8,128)} %get-tuple-element.31.a_ref, ...), custom_call_target="tpu_custom_call" | custom-call | tf_op jit(solution)/shard_map/token_gradients/pallas_call | solution.py:1155
  314.3 0.7 slice.27
  315.0 0.1 constant_dynamic-slice_fusion
  315.0 0.5 slice_bitcast_fusion
  315.6 1.3 dynamic-slice_bitcast_fusion
  316.8 0.0 copy-done
  316.8 1.3 copy.35
Async XLA Ops:
  308.8 8.0 %copy-start = (bf16[4096,256]{1,0:T(8,128)(2,1)S(1)}, bf16[4096,256]{1,0:T(8,128)(2,1)}, u32[]{:S(2)}) copy-start(bf16[4096,256]{1,0:T(8,128)(2,1)} %get-tuple-element.66) | copy-start | bytes 6291460
